TPU v7x, 256 devices: a whole 4x4x8 slice. The times are simulated.
256 devices in a mesh: dp: 32 (over x_lo, z, core), tp: 8 (over x_hi, y).
Axes of the slice: x: 4 (x_hi: 2, x_lo: 2; x = x_hi * 2 + x_lo), y: 4, z: 8, core: 2. Of those that a mesh axis runs over, the one named last changes fastest.
Arguments:
- queries: bfloat16 [128, 3, 128, 576], P('dp', None, 'tp'), may hold values from -200 to 200
- new_latent: bfloat16 [128, 3, 576], P('dp'), may hold values from -6 to 6
- cache: bfloat16 [131072, 576], P('dp'), may hold values from -6 to 6
- cache_lengths: int32 [32, 4], replicated, may hold values from 1 to 2048, as said below
- w_uv: bfloat16 [128, 512, 128], P('tp'), may hold values from -1 to 1
- w_o: bfloat16 [16384, 7168], P('tp', 'dp'), may hold values from -0.09375 to 0.09375
- residual: bfloat16 [384, 7168], P(None, ('dp', 'tp')), may hold values from -6 to 6
- norm_gain: bfloat16 [7168], replicated, may hold values from 0.099609375 to 1.8984375
- w_gate: bfloat16 [7168, 18432], P(None, ('dp', 'tp')), may hold values from -0.3125 to 0.3125
- w_up: bfloat16 [7168, 18432], P(None, ('dp', 'tp')), may hold values from -0.3125 to 0.3125
- w_down: bfloat16 [18432, 7168], P(('dp', 'tp')), may hold values from -0.1875 to 0.1875
Outputs:
- layer_out: bfloat16 [384, 7168], P(None, ('dp', 'tp'))
Inputs may be any that keep to these rules, and one draw needn't show every extreme that they name: `cache_lengths`: row d lists the cache lengths of the 4 requests of dp index d, packed in order from the first of that index's 4096 cache rows; every row sums to at most 4096; one request holds at most 4096 // min(4, 2) tokens, and some request holds exactly that many.
All inputs are finite; a program needn't handle non-finite values.
Results may differ from a plain program's by a relative error of at most 0.02.
Values may be sent and summed in bfloat16 or wider, within the bound.
No kernel may reach another device: no remote copies, remote signals or barrier semaphores. Data moves between devices by JAX's collectives and lax.ppermute only.
A program may use at most 128 MiB of HBM per device.

v0:
```python
import jax
import jax.numpy as jnp
from jax import lax
from jax.sharding import PartitionSpec as P

BLOCK = 512


score_scale = 192.0 ** (-0.5)
big_negative = -1e30


def segment_table(lengths_row, slot_ids):
    starts = jnp.cumsum(lengths_row) - lengths_row
    filled = jnp.sum(lengths_row)
    labels = jnp.sum((slot_ids[:, None] >= starts[None, :]).astype(jnp.int32), axis=1) - 1
    return (jnp.where(slot_ids < filled, labels, -1), filled)


def block_pass(state, flat_queries, owners, key_rows, label_rows, block_count, latent):

    def advance(block_index, state_now):
        running_max, running_sum, weighted = state_now
        key_block = lax.dynamic_slice_in_dim(key_rows, block_index * BLOCK, BLOCK, 0)
        label_block = lax.dynamic_slice_in_dim(label_rows, block_index * BLOCK, BLOCK, 0)
        scores = (
            lax.dot_general(
                flat_queries,
                key_block,
                (((1,), (1,)), ((), ())),
                preferred_element_type=jnp.float32,
            )
            * score_scale
        )
        allowed = label_block[None, :] == owners[:, None]
        new_max = jnp.maximum(
            running_max, jnp.max(jnp.where(allowed, scores, big_negative), axis=1)
        )
        weights = jnp.where(allowed, jnp.exp(scores - new_max[:, None]), 0.0)
        factor = jnp.exp(running_max - new_max)
        running_sum = running_sum * factor + jnp.sum(weights, axis=1)
        weighted = weighted * factor[:, None] + jnp.dot(
            weights.astype(jnp.bfloat16), key_block[:, :latent], preferred_element_type=jnp.float32
        )
        return (new_max, running_sum, weighted)

    return lax.fori_loop(0, block_count, advance, state)


def body(
    queries, new_latent, cache, cache_lengths, w_uv, w_o, residual, norm_gain, w_gate, w_up, w_down
):
    requests, step_count, local_heads, key_width = queries.shape
    latent = w_uv.shape[1]
    cache_span = cache.shape[0]
    dp_index = lax.axis_index("dp")
    slot_ids = jnp.arange(cache_span, dtype=jnp.int32)
    own_lengths = lax.dynamic_index_in_dim(cache_lengths, dp_index, 0, keepdims=False)
    own_labels, own_filled = segment_table(own_lengths, slot_ids)
    query_rows = requests * step_count * local_heads
    owners = jnp.broadcast_to(
        jnp.arange(requests, dtype=jnp.int32)[:, None, None], (requests, step_count, local_heads)
    ).reshape(query_rows)
    flat_queries = queries.reshape(query_rows, key_width)
    fresh_scores = (
        jnp.einsum("rthk,rsk->rths", queries, new_latent, preferred_element_type=jnp.float32)
        * score_scale
    )
    step_ids = jnp.arange(step_count, dtype=jnp.int32)
    causal = (step_ids[None, :] <= step_ids[:, None])[None, :, None, :]
    fresh_max = jnp.max(jnp.where(causal, fresh_scores, big_negative), axis=-1)
    fresh_weights = jnp.where(causal, jnp.exp(fresh_scores - fresh_max[..., None]), 0.0)
    fresh_sum = jnp.sum(fresh_weights, axis=-1)
    fresh_weighted = jnp.einsum(
        "rths,rsl->rthl",
        fresh_weights.astype(jnp.bfloat16),
        new_latent[..., :latent],
        preferred_element_type=jnp.float32,
    )
    state = (
        fresh_max.reshape(query_rows),
        fresh_sum.reshape(query_rows),
        fresh_weighted.reshape(query_rows, latent),
    )
    blocks_live = (own_filled + BLOCK - 1) // BLOCK
    state = block_pass(state, flat_queries, owners, cache, own_labels, blocks_live, latent)
    running_max, running_sum, weighted = state
    mixed_latent = (weighted / running_sum[:, None]).astype(jnp.bfloat16)
    mixed_latent = mixed_latent.reshape(requests * step_count, local_heads, latent)
    head_values = jnp.einsum("nhl,hlv->nhv", mixed_latent, w_uv, preferred_element_type=jnp.float32)
    head_values = head_values.astype(jnp.bfloat16).reshape(
        requests * step_count, local_heads * w_uv.shape[2]
    )
    partial_out = jnp.dot(
        lax.all_gather(head_values, "dp", axis=0, tiled=True),
        w_o,
        preferred_element_type=jnp.float32,
    )
    attended = lax.psum_scatter(
        partial_out.astype(jnp.bfloat16), "tp", scatter_dimension=1, tiled=True
    ).astype(jnp.float32)
    updated = (residual.astype(jnp.float32) + attended).astype(jnp.bfloat16)
    gathered = lax.all_gather(updated, ("dp", "tp"), axis=1, tiled=True)
    widened = gathered.astype(jnp.float32)
    inverse_rms = lax.rsqrt(jnp.mean(widened * widened, axis=-1, keepdims=True) + 1e-06)
    normed = (widened * inverse_rms * norm_gain.astype(jnp.float32)).astype(jnp.bfloat16)
    gate_out = jnp.dot(normed, w_gate, preferred_element_type=jnp.float32)
    up_out = jnp.dot(normed, w_up, preferred_element_type=jnp.float32)
    hidden = (jax.nn.silu(gate_out) * up_out).astype(jnp.bfloat16)
    ffn_term = jnp.dot(hidden, w_down, preferred_element_type=jnp.float32)
    ffn_part = lax.psum_scatter(ffn_term, ("dp", "tp"), scatter_dimension=1, tiled=True)
    return (updated.astype(jnp.float32) + ffn_part).astype(jnp.bfloat16)


def solution(mesh):
    return jax.shard_map(
        body,
        mesh=mesh,
        in_specs=(
            P("dp", None, "tp", None),
            P("dp", None, None),
            P("dp", None),
            P(),
            P("tp", None, None),
            P("tp", "dp"),
            P(None, ("dp", "tp")),
            P(),
            P(None, ("dp", "tp")),
            P(None, ("dp", "tp")),
            P(("dp", "tp"), None),
        ),
        out_specs=P(None, ("dp", "tp")),
        check_vma=False,
    )
```

profile of v0, /device:TPU:32, one launch (start us, length us, event | category | flops | bytes accessed | tf_op | source)
XLA Modules:
  0.0 1781.1 jit_solution(9929711165519908971)
XLA Ops:
  12.8 14.1 while.15
  13.0 1.6 fusion.59
  14.9 1.4 convolution_add_fusion.2
  16.5 1.6 fusion.59
  18.4 1.4 convolution_add_fusion.2
  20.1 1.6 fusion.59
  21.9 1.4 convolution_add_fusion.2
  23.6 1.6 fusion.59
  28.3 75.2 %all-gather.5.cloned.1.call-done = bf16[32,12,2048]{2,1,0:T(8,128)(2,1)} async-done(((bf16[1,12,2048]{2,1,0:T(8,128)(2,1)}), bf16[32,12,2048]{2,1,0:T(8,128)(2,1)}) %all-gather.5.cloned.1.call-update) | async-done | bytes 1572880 | tf_op jit(solution)/shard_map/all_gather | solution.py:95
  103.5 3.6 reshape.58
  107.1 2.4 convolution_convert_fusion
  109.4 26.0 %fusion.2 = bf16[384,32]{0,1:T(8,128)(2,1)S(1)} fusion(bf16[384,224]{0,1:T(8,128)(2,1)S(1)} %convolution_convert_fusion), kind=kCustom, calls=%all-reduce-scatter | all-reduce-scatter fusion | flops 98305 | bytes 197632
  139.2 720.4 %all-gather.7.cloned.1.call-done = bf16[256,28,384]{2,1,0:T(8,128)(2,1)} async-done(((bf16[1,28,384]{2,1,0:T(8,128)(2,1)}), bf16[256,28,384]{2,1,0:T(8,128)(2,1)}) %all-gather.7.cloned.1.call-update) | async-done | bytes 5505040 | tf_op jit(solution)/shard_map/all_gather | solution.py:103
  859.6 9.9 reshape.62
  869.5 5.3 multiply_reduce_fusion
  874.8 2.0 copy-done.1
  876.8 3.0 multiply_convert_fusion
  879.8 2.3 copy-done.2
  883.4 9.9 fusion.20
  893.3 668.4 %fusion.3 = f32[384,32]{0,1:T(8,128)S(1)} fusion(f32[384,7168]{0,1:T(8,128)} %fusion.20), kind=kCustom, calls=%all-reduce-scatter.1 | all-reduce-scatter fusion | flops 3145729 | bytes 11059200
  1561.7 3.3 collective-permute-start.1
  1565.1 14.8 collective-permute-start.32
  1579.9 24.2 %collective-permute-start.10 = (f32[384,32]{0,1:T(8,128)S(1)}, f32[384,32]{0,1:T(8,128)S(1)}, u32[]{:S(2)}, u32[]{:S(2)}) collective-permute-start(f32[384,32]{0,1:T(8,128)S(1)} %fusion.3), channel_id=1, source_target_pairs={{0,10},{1,11},{2,12},{3,13},{4,14},{5,15},{6,16},{7,17},{8,18},{9,... | collective-permute-start | bytes 147464
  1604.1 12.8 collective-permute-start.11
  1616.9 1.9 collective-permute-start.12
  1618.9 7.7 collective-permute-start.13
  1626.6 9.7 collective-permute-start.14
  1636.3 1.9 collective-permute-start.15
  1638.2 1.9 collective-permute-start.16
  1642.8 18.5 %collective-permute-start.19 = (f32[384,32]{0,1:T(8,128)S(1)}, f32[384,32]{0,1:T(8,128)S(1)}, u32[]{:S(2)}, u32[]{:S(2)}) collective-permute-start(f32[384,32]{0,1:T(8,128)S(1)} %fusion.3), channel_id=1, source_target_pairs={{0,19},{1,20},{2,21},{3,22},{4,23},{5,24},{6,25},{7,26},{8,27},{9,... | collective-permute-start | bytes 147464
  1661.3 1.9 collective-permute-start.2
  1663.2 3.8 collective-permute-start.20
  1667.0 4.2 collective-permute-start.21
  1671.3 7.0 collective-permute-start.22
  1683.7 3.2 collective-permute-start.27
  1688.2 2.2 collective-permute-start.29
  1690.4 3.3 collective-permute-start.3
  1693.7 4.6 collective-permute-start.30
  1698.3 1.6 collective-permute-start.31
  1700.0 4.6 collective-permute-start.4
  1704.6 1.9 collective-permute-start.5
  1706.6 4.9 collective-permute-start.6
  1711.5 2.5 collective-permute-start.7
  1714.0 1.9 collective-permute-start.8
  1716.6 1.9 collective-permute-start.9
  1719.5 7.6 collective-permute-done.9
  1727.2 45.6 %concatenate.1 = f32[384,1052]{0,1:T(8,128)} concatenate(f32[384,28]{0,1:T(8,128)S(1)} %collective-permute-done.32, f32[384,32]{0,1:T(8,128)S(1)} %collective-permute-done.31, f32[384,32]{0,1:T(8,128)S(1)} %collective-permute-done.30, f32[384,32]{0,1:T(8,128)S(1)} %collective-permute-done.29, f32[384,32]{0,1:T(8,128)S(1)} %collective-permute-done.28, ...), dimensions={1} | concatenate | bytes 3231744
  1772.8 1.5 fusion.28
  (113 shorter events, 25.2 us)
Async XLA Ops:
  6.5 20.5 %copy-start = (bf16[16,512,128]{2,1,0:T(8,128)(2,1)S(1)}, bf16[16,512,128]{2,1,0:T(8,128)(2,1)}, u32[]{:S(2)}) copy-start(bf16[16,512,128]{2,1,0:T(8,128)(2,1)} %param.17) | copy-start | bytes 6291460
  6.5 96.9 %all-gather.5.cloned.1.call-start = ((), (), s32[]{:S(2)}) async-start(), calls=%async_computation | async-start | bytes 2162688 | tf_op jit(solution)/shard_map/all_gather | solution.py:95
  26.9 109.9 %copy-start.8 = (u32[256]{0:T(256)S(1)}, u32[256]{0:T(256)}, u32[]{:S(2)}) copy-start(u32[256]{0:T(256)} %constant.77) | copy-start | bytes 3076
  26.9 111.6 %copy-start.5 = (bf16[384,28]{0,1:T(8,128)(2,1)S(1)}, bf16[384,28]{0,1:T(8,128)(2,1)}, u32[]{:S(2)}) copy-start(bf16[384,28]{0,1:T(8,128)(2,1)} %param.19) | copy-start | bytes 64516
  27.0 112.3 %copy-start.7 = (bf16[7168]{0:T(1024)(128)(2,1)S(1)}, bf16[7168]{0:T(1024)(128)(2,1)}, u32[]{:S(2)}) copy-start(bf16[7168]{0:T(1024)(128)(2,1)} %param.20) | copy-start | bytes 43012
  28.3 831.3 %all-gather.7.cloned.1.call-start = ((), (), s32[]{:S(2)}) async-start(), calls=%async_computation.1 | async-start | bytes 6316032 | tf_op jit(solution)/shard_map/all_gather | solution.py:103
  135.5 2.8 collective-permute-start
  869.5 7.3 copy-start.1
  876.8 5.4 copy-start.4
  879.8 2.4 copy-start.2
  882.2 1.2 copy-start.3
  1561.7 64.9 %collective-permute-start.1 = (f32[384,32]{0,1:T(8,128)S(1)}, f32[384,32]{0,1:T(8,128)S(1)}, u32[]{:S(2)}, u32[]{:S(2)}) collective-permute-start(f32[384,32]{0,1:T(8,128)S(1)} %fusion.3), channel_id=1, source_target_pairs={{0,1},{1,2},{2,3},{3,4},{4,5},{5,6},{6,7},{7,8},{8,9},{9,10},{10,1... | collective-permute-start | bytes 147464
  1565.1 53.8 %collective-permute-start.32 = (f32[384,28]{0,1:T(8,128)S(1)}, f32[384,28]{0,1:T(8,128)S(1)}, u32[]{:S(2)}, u32[]{:S(2)}) collective-permute-start(f32[384,28]{0,1:T(8,128)S(1)} %slice.9), channel_id=1, source_target_pairs={{0,32},{1,33},{2,34},{3,35},{4,36},{5,37},{6,38},{7,39},{8,40},{9,... | collective-permute-start | bytes 129032
  1579.9 56.4 %collective-permute-start.10 = (f32[384,32]{0,1:T(8,128)S(1)}, f32[384,32]{0,1:T(8,128)S(1)}, u32[]{:S(2)}, u32[]{:S(2)}) collective-permute-start(f32[384,32]{0,1:T(8,128)S(1)} %fusion.3), channel_id=1, source_target_pairs={{0,10},{1,11},{2,12},{3,13},{4,14},{5,15},{6,16},{7,17},{8,18},{9,... | collective-permute-start | bytes 147464
  1604.1 34.1 %collective-permute-start.11 = (f32[384,32]{0,1:T(8,128)S(1)}, f32[384,32]{0,1:T(8,128)S(1)}, u32[]{:S(2)}, u32[]{:S(2)}) collective-permute-start(f32[384,32]{0,1:T(8,128)S(1)} %fusion.3), channel_id=1, source_target_pairs={{0,11},{1,12},{2,13},{3,14},{4,15},{5,16},{6,17},{7,18},{8,19},{9,... | collective-permute-start | bytes 147464
  1616.9 23.2 %collective-permute-start.12 = (f32[384,32]{0,1:T(8,128)S(1)}, f32[384,32]{0,1:T(8,128)S(1)}, u32[]{:S(2)}, u32[]{:S(2)}) collective-permute-start(f32[384,32]{0,1:T(8,128)S(1)} %fusion.3), channel_id=1, source_target_pairs={{0,12},{1,13},{2,14},{3,15},{4,16},{5,17},{6,18},{7,19},{8,20},{9,... | collective-permute-start | bytes 147464
  1618.9 22.6 %collective-permute-start.13 = (f32[384,32]{0,1:T(8,128)S(1)}, f32[384,32]{0,1:T(8,128)S(1)}, u32[]{:S(2)}, u32[]{:S(2)}) collective-permute-start(f32[384,32]{0,1:T(8,128)S(1)} %fusion.3), channel_id=1, source_target_pairs={{0,13},{1,14},{2,15},{3,16},{4,17},{5,18},{6,19},{7,20},{8,21},{9,... | collective-permute-start | bytes 147464
  1626.6 16.2 collective-permute-start.14
  1636.3 25.0 %collective-permute-start.15 = (f32[384,32]{0,1:T(8,128)S(1)}, f32[384,32]{0,1:T(8,128)S(1)}, u32[]{:S(2)}, u32[]{:S(2)}) collective-permute-start(f32[384,32]{0,1:T(8,128)S(1)} %fusion.3), channel_id=1, source_target_pairs={{0,15},{1,16},{2,17},{3,18},{4,19},{5,20},{6,21},{7,22},{8,23},{9,... | collective-permute-start | bytes 147464
  1638.2 25.0 %collective-permute-start.16 = (f32[384,32]{0,1:T(8,128)S(1)}, f32[384,32]{0,1:T(8,128)S(1)}, u32[]{:S(2)}, u32[]{:S(2)}) collective-permute-start(f32[384,32]{0,1:T(8,128)S(1)} %fusion.3), channel_id=1, source_target_pairs={{0,16},{1,17},{2,18},{3,19},{4,20},{5,21},{6,22},{7,23},{8,24},{9,... | collective-permute-start | bytes 147464
  1640.2 26.8 %collective-permute-start.17 = (f32[384,32]{0,1:T(8,128)S(1)}, f32[384,32]{0,1:T(8,128)S(1)}, u32[]{:S(2)}, u32[]{:S(2)}) collective-permute-start(f32[384,32]{0,1:T(8,128)S(1)} %fusion.3), channel_id=1, source_target_pairs={{0,17},{1,18},{2,19},{3,20},{4,21},{5,22},{6,23},{7,24},{8,25},{9,... | collective-permute-start | bytes 147464
  1641.5 29.8 %collective-permute-start.18 = (f32[384,32]{0,1:T(8,128)S(1)}, f32[384,32]{0,1:T(8,128)S(1)}, u32[]{:S(2)}, u32[]{:S(2)}) collective-permute-start(f32[384,32]{0,1:T(8,128)S(1)} %fusion.3), channel_id=1, source_target_pairs={{0,18},{1,19},{2,20},{3,21},{4,22},{5,23},{6,24},{7,25},{8,26},{9,... | collective-permute-start | bytes 147464
  1642.8 35.5 %collective-permute-start.19 = (f32[384,32]{0,1:T(8,128)S(1)}, f32[384,32]{0,1:T(8,128)S(1)}, u32[]{:S(2)}, u32[]{:S(2)}) collective-permute-start(f32[384,32]{0,1:T(8,128)S(1)} %fusion.3), channel_id=1, source_target_pairs={{0,19},{1,20},{2,21},{3,22},{4,23},{5,24},{6,25},{7,26},{8,27},{9,... | collective-permute-start | bytes 147464
  1661.3 18.3 %collective-permute-start.2 = (f32[384,32]{0,1:T(8,128)S(1)}, f32[384,32]{0,1:T(8,128)S(1)}, u32[]{:S(2)}, u32[]{:S(2)}) collective-permute-start(f32[384,32]{0,1:T(8,128)S(1)} %fusion.3), channel_id=1, source_target_pairs={{0,2},{1,3},{2,4},{3,5},{4,6},{5,7},{6,8},{7,9},{8,10},{9,11},{10,... | collective-permute-start | bytes 147464
  1663.2 17.7 collective-permute-start.20
  1667.0 15.2 collective-permute-start.21
  1671.3 12.4 collective-permute-start.22
  1678.3 8.6 collective-permute-start.23
  1679.6 8.6 collective-permute-start.24
  1680.9 9.5 collective-permute-start.25
  1682.2 11.5 collective-permute-start.26
  1683.7 14.7 collective-permute-start.27
  1686.9 13.1 collective-permute-start.28
  1688.2 16.4 collective-permute-start.29
  1690.4 16.1 collective-permute-start.3
  1693.7 17.7 collective-permute-start.30
  1698.3 15.7 collective-permute-start.31
  1700.0 16.0 collective-permute-start.4
  1704.6 13.9 collective-permute-start.5
  1706.6 11.9 collective-permute-start.6
  1711.5 7.1 collective-permute-start.7
  1714.0 5.5 collective-permute-start.8
  1716.0 0.6 copy-start.6
  1716.6 10.6 collective-permute-start.9
Sparse Core Ops, SparseCore 0:
  28.4 75.0 all-gather.4
  139.3 720.2 all-gather.6
where the time goes:
time: 1790 us; the launch traced here: 1780 us
  waiting for transfers between devices  805 us (45%)
  blocking collectives  694 us (39%)
  starting transfers between devices  157 us (9%)
  local copies, waits for them, and re-layouts  68.3 us (4%)
  matrix products  27.5 us (2%)
    all_gather x1, waiting for transfers between devices, body(): gathered = lax.all_gather(updated, ('dp', 'tp'), axis=1, tiled=True)  720 us
    unnamed x2, blocking collectives  694 us
    unnamed x33, starting transfers between devices  157 us
    all_gather x1, waiting for transfers between devices, body(): lax.all_gather(head_values, 'dp', axis=0, tiled=True)  75.2 us
    unnamed x25, local copies, waits for them, and re-layouts  56 us
  transfers between devices with their start and end apart: 35, of which 5 were waited for; matrix products, arithmetic and copies ran while one was open for 0% of the time, Pallas kernels for 0%

commit v1 on v0

v1 whole, which is shorter than its diff:
```python
import functools

import jax
import jax.numpy as jnp
import numpy as np
from jax import lax
from jax.experimental import pallas as pl
from jax.experimental.pallas import tpu as pltpu
from jax.sharding import Mesh, PartitionSpec as P

DP = ("xl", "z", "c")
RING = ("xl", "z")
TP = ("xh", "y")
SIZES = {"xl": 2, "z": 8, "c": 2, "xh": 2, "y": 4}
N_RING, N_TP = 16, 8

STEPS, HEADS, REQ = 3, 16, 4
NEW = REQ * STEPS
ROWS = NEW * HEADS
TOKENS = 384
LAT, KDIM, VDIM = 512, 576, 128
CTX, CHUNK = 4096, 512
N_CHUNK = CTX // CHUNK
D, FEAT, PIECE, PAD = 7168, 224, 28, 32
FF = 72
EPS = 1e-06
LOG2E = 1.4426950408889634
SCALE = 192.0 ** (-0.5)
NEG = -1e30

NT = (((1,), (1,)), ((), ()))
TN = (((0,), (0,)), ((), ()))


def dot(a, b, dims=(((1,), (0,)), ((), ()))):
    return lax.dot_general(a, b, dims, preferred_element_type=jnp.float32)


def attend_kernel(
    bounds, q_ref, fresh_ref, cache_hbm, w_uv_hbm, out_ref, keys, scores, w_uv, key_sems, w_sem
):
    copies = [
        pltpu.make_async_copy(
            cache_hbm.at[:, pl.ds(j * CHUNK, CHUNK)], keys.at[j], key_sems.at[j]
        )
        for j in range(N_CHUNK)
    ]
    w_copy = pltpu.make_async_copy(w_uv_hbm, w_uv, w_sem)
    for copy in copies:
        copy.start()
    w_copy.start()

    q = q_ref[...]
    row = lax.broadcasted_iota(jnp.int32, (ROWS, 1), 0)
    request = row // (STEPS * HEADS)
    step = row // HEADS - request * STEPS
    low = jnp.zeros((ROWS, 1), jnp.int32)
    high = jnp.zeros((ROWS, 1), jnp.int32)
    for r in range(REQ):
        low = jnp.where(request == r, bounds[r], low)
        high = jnp.where(request == r, bounds[REQ + r], high)

    fresh = fresh_ref[...]
    key = lax.broadcasted_iota(jnp.int32, (ROWS, NEW), 1)
    key_step = key // REQ
    seen = (key - key_step * REQ == request) & (key_step <= step)
    fresh_scores = jnp.where(seen, dot(q, fresh, NT) * (SCALE * LOG2E), NEG)
    top = jnp.max(fresh_scores, axis=1, keepdims=True)

    for j in range(N_CHUNK):
        copies[j].wait()
        slot = j * CHUNK + lax.broadcasted_iota(jnp.int32, (ROWS, CHUNK), 1)
        part = dot(q, keys[j]) * (SCALE * LOG2E)
        part = jnp.where((slot >= low) & (slot < high), part, NEG)
        scores[j] = part
        top = jnp.maximum(top, jnp.max(part, axis=1, keepdims=True))

    weights = jnp.exp2(fresh_scores - top)
    total = jnp.sum(weights, axis=1, keepdims=True)
    mixed = dot(weights.astype(jnp.bfloat16), fresh[:, :LAT])
    for j in range(N_CHUNK):
        weights = jnp.exp2(scores[j] - top)
        total = total + jnp.sum(weights, axis=1, keepdims=True)
        mixed = mixed + dot(weights.astype(jnp.bfloat16), keys[j, :LAT, :], NT)
    mixed = (mixed / total).astype(jnp.bfloat16)

    w_copy.wait()
    head = row - (row // HEADS) * HEADS
    for h in range(HEADS):
        values = jnp.where(head == h, dot(mixed, w_uv[h]), 0.0)
        values = jnp.sum(values.reshape(NEW, HEADS, VDIM), axis=1).astype(jnp.bfloat16)
        half, at = h // (HEADS // 2), h % (HEADS // 2)
        out_ref[half, :, at * VDIM : (at + 1) * VDIM] = values


def attend(bounds, q, fresh, cache_t, w_uv):
    vmem = pl.BlockSpec(memory_space=pltpu.VMEM)
    anyspace = pl.BlockSpec(memory_space=pl.ANY)
    return pl.pallas_call(
        attend_kernel,
        out_shape=jax.ShapeDtypeStruct((2, NEW, HEADS // 2 * VDIM), jnp.bfloat16),
        in_specs=[
            pl.BlockSpec(memory_space=pltpu.SMEM),
            vmem,
            vmem,
            anyspace,
            anyspace,
        ],
        out_specs=vmem,
        scratch_shapes=[
            pltpu.VMEM((N_CHUNK, KDIM, CHUNK), jnp.bfloat16),
            pltpu.VMEM((N_CHUNK, ROWS, CHUNK), jnp.float32),
            pltpu.VMEM((HEADS, LAT, VDIM), jnp.bfloat16),
            pltpu.SemaphoreType.DMA((N_CHUNK,)),
            pltpu.SemaphoreType.DMA,
        ],
        compiler_params=pltpu.CompilerParams(vmem_limit_bytes=40 * 2**20),
        cost_estimate=pl.CostEstimate(
            flops=2 * ROWS * CTX * (KDIM + LAT), bytes_accessed=7 * 2**20, transcendentals=ROWS * CTX
        ),
        name="attend",
    )(bounds, q, fresh, cache_t, w_uv)


def regroup_kernel(source_ref, gate_ref, up_ref, down_ref, mix_ref, out_ref):
    width = 4 * FEAT
    lanes = N_TP * 4 * PAD
    pick = lax.broadcasted_iota(jnp.int32, (width, lanes), 0) == source_ref[...]
    pick = jnp.where(pick, 1.0, 0.0).astype(jnp.bfloat16)
    for m in range(D // width):
        for which, ref in enumerate((gate_ref, up_ref, down_ref)):
            moved = dot(ref[:, m * width : (m + 1) * width], pick).astype(jnp.bfloat16)
            for t in range(N_TP):
                piece = moved[:, t * 128 : (t + 1) * 128]
                if which < 2:
                    mix_ref[t, which, :, m * 128 : (m + 1) * 128] = piece
                else:
                    out_ref[t, :, m * 128 : (m + 1) * 128] = piece


def regroup(source, gate_t, up_t, down):
    vmem = pl.BlockSpec(memory_space=pltpu.VMEM)
    return pl.pallas_call(
        regroup_kernel,
        out_shape=(
            jax.ShapeDtypeStruct((N_TP, 2, FF, 1024), jnp.bfloat16),
            jax.ShapeDtypeStruct((N_TP, FF, 1024), jnp.bfloat16),
        ),
        in_specs=[vmem] * 4,
        out_specs=(vmem, vmem),
        compiler_params=pltpu.CompilerParams(vmem_limit_bytes=40 * 2**20),
        cost_estimate=pl.CostEstimate(
            flops=2 * 3 * FF * D * 1024, bytes_accessed=7 * 2**20, transcendentals=0
        ),
        name="regroup",
    )(source, gate_t, up_t, down)


def swap(x, axes):
    return lax.all_to_all(x, axes, 0, 0, tiled=True)


def spread(x, axes, count):
    return swap(jnp.broadcast_to(x[None], (count, *x.shape)), axes)


def other_core(x):
    return lax.ppermute(x, "c", [(0, 1), (1, 0)])


def pad_pieces(x):
    lead = x.shape[0] // PIECE
    x = x.reshape(lead, PIECE, *x.shape[1:])
    x = jnp.pad(x, ((0, 0), (0, PAD - PIECE)) + ((0, 0),) * (x.ndim - 2))
    return x.reshape(lead * PAD, *x.shape[2:])


def split_sum(x):
    high = x.astype(jnp.bfloat16)
    return high, (x - high.astype(jnp.float32)).astype(jnp.bfloat16)


def body(
    queries, new_latent, cache, cache_lengths, w_uv, w_o, residual, norm_gain, w_gate, w_up, w_down
):
    core = lax.axis_index("c")
    dp_index = lax.axis_index(DP)
    tp_index = lax.axis_index(TP)

    lane = np.arange(N_TP * 4 * PAD)
    lane_t, lane_core, lane_u, lane_j = lane // 128, lane // 64 % 2, lane // 32 % 2, lane % PAD
    base = jnp.asarray(lane_u * 2 * FEAT + lane_t * PIECE + lane_j, jnp.int32)
    source = base + (jnp.asarray(lane_core, jnp.int32) ^ core) * FEAT
    source = jnp.where(jnp.asarray(lane_j < PIECE), source, -1)[None, :]
    mix_w, down_w = regroup(source, w_gate.T, w_up.T, w_down)
    mix_w = swap(mix_w, TP).reshape(N_TP * 2 * FF, 1024)
    down_w = swap(down_w, TP).reshape(N_TP * FF, 1024)

    own_lengths = lax.dynamic_index_in_dim(cache_lengths, dp_index, 0, keepdims=False)
    ends = jnp.cumsum(own_lengths)
    bounds = jnp.concatenate([ends - own_lengths, ends]).astype(jnp.int32)
    fresh = jnp.transpose(new_latent, (1, 0, 2)).reshape(NEW, KDIM)
    heads = attend(bounds, queries.reshape(ROWS, KDIM), fresh, cache.T, w_uv)

    heads = swap(heads, "c").reshape(2 * NEW, HEADS // 2 * VDIM)
    heads = spread(heads, RING, N_RING).reshape(TOKENS, HEADS // 2 * VDIM)
    more_heads = other_core(heads)
    w_ot = pad_pieces(w_o.T)
    half = HEADS // 2 * VDIM
    w_own = lax.dynamic_slice_in_dim(w_ot, core * half, half, 1)
    w_more = lax.dynamic_slice_in_dim(w_ot, (1 - core) * half, half, 1)
    partial = dot(w_own, heads, NT) + dot(w_more, more_heads, NT)
    partial = partial.astype(jnp.bfloat16).reshape(N_TP, PAD, TOKENS)
    attended = jnp.sum(swap(partial, TP).astype(jnp.float32), axis=0)
    updated = (pad_pieces(residual.T).astype(jnp.float32) + attended).astype(jnp.bfloat16)

    wide = updated.astype(jnp.float32)
    gain = lax.dynamic_slice_in_dim(norm_gain, dp_index * FEAT + tp_index * PIECE, PIECE, 0)
    scaled = (wide[:PIECE] * gain.astype(jnp.float32)[:, None]).astype(jnp.bfloat16)
    high, low = split_sum(jnp.sum(wide * wide, axis=0, keepdims=True))
    block = jnp.concatenate([scaled, high, low, jnp.zeros((2, TOKENS), jnp.bfloat16)], axis=0)
    own = spread(block, RING, N_RING)
    more = other_core(own)

    def squares(x):
        return jnp.sum(x[:, PIECE : PIECE + 2].astype(jnp.float32), axis=(0, 1))

    high, low = split_sum((squares(own) + squares(more))[None])
    features = jnp.stack([own.reshape(8, 64, TOKENS), more.reshape(8, 64, TOKENS)], axis=1)
    mix = dot(mix_w, features.reshape(1024, TOKENS)).astype(jnp.bfloat16)
    tail = jnp.concatenate([high, low, jnp.zeros((6, TOKENS), jnp.bfloat16)], axis=0)
    mix = jnp.concatenate(
        [mix.reshape(N_TP, 2 * FF, TOKENS), jnp.broadcast_to(tail, (N_TP, 8, TOKENS))], axis=1
    )
    mix = jnp.sum(swap(mix, TP).astype(jnp.float32), axis=0)
    mean = (mix[2 * FF] + mix[2 * FF + 1]) * (1.0 / D)
    inverse_rms = lax.rsqrt(mean + EPS)[None]
    gate_out = mix[:FF] * inverse_rms
    up_out = mix[FF : 2 * FF] * inverse_rms
    hidden = (jax.nn.silu(gate_out) * up_out).astype(jnp.bfloat16)
    hidden = spread(hidden, TP, N_TP).reshape(N_TP * FF, TOKENS)

    term = dot(down_w, hidden, TN).reshape(8, 2, 64, TOKENS)
    term = term[:, 0] + other_core(term[:, 1].astype(jnp.bfloat16)).astype(jnp.float32)
    term = swap(term.astype(jnp.bfloat16).reshape(N_RING, PAD, TOKENS), RING)
    term = jnp.sum(term.astype(jnp.float32), axis=0)
    return (wide[:PIECE] + term[:PIECE]).astype(jnp.bfloat16).T


def solution(mesh):
    parts = Mesh(mesh.devices.reshape(tuple(SIZES.values())), tuple(SIZES))
    everywhere = DP + TP
    return jax.shard_map(
        body,
        mesh=parts,
        in_specs=(
            P(DP, None, TP, None),
            P(DP, None, None),
            P(DP, None),
            P(),
            P(TP, None, None),
            P(TP, DP),
            P(None, everywhere),
            P(),
            P(None, everywhere),
            P(None, everywhere),
            P(everywhere, None),
        ),
        out_specs=P(None, everywhere),
        check_vma=False,
    )
```

time: 1790 us -> 200 us (0.11)
  waiting for transfers between devices: 805 us -> 62.5 us
  blocking collectives: 694 us -> 76 us
  starting transfers between devices: 157 us -> 22.4 us
  local copies, waits for them, and re-layouts: 68.3 us -> 9.45 us
  matrix products: 27.5 us -> 7.6 us
    all_gather x2 -> x0, waiting for transfers between devices: 796 us -> none  [the longest x1 720 us: body(): gathered = lax.all_gather(updated, ('dp', 'tp'), axis=1, tiled=True)]
    unnamed x2 -> x0, blocking collectives: 694 us -> none
    unnamed x33 -> x0, starting transfers between devices: 157 us -> none
    all_to_all x0 -> x4, blocking collectives: none -> 76 us  [swap(): return lax.all_to_all(x, axes, 0, 0, tiled=True)]
    all_to_all x0 -> x5, waiting for transfers between devices: none -> 58.6 us  [swap(): return lax.all_to_all(x, axes, 0, 0, tiled=True)]
    unnamed x25 -> x24, local copies, waits for them, and re-layouts: 56 us -> 5.6 us
    all_to_all x0 -> x5, starting transfers between devices: none -> 22.2 us  [swap(): return lax.all_to_all(x, axes, 0, 0, tiled=True)]
    dot_general x14 -> x4, matrix products: 27.5 us -> 7.6 us  [dot(): return lax.dot_general(a, b, dims, preferred_element_type=jnp.float32)]
  transfers between devices with their start and end apart: 35 -> 8, of which waited for: 5 -> 8; matrix products, arithmetic and copies ran while one was open for 0% -> 2% of each run, Pallas kernels for 0% -> 5%
where the time goes in v1:
time: 200 us; the launch traced here: 199 us
  blocking collectives  76 us (38%)
  waiting for transfers between devices  62.5 us (31%)
  starting transfers between devices  22.4 us (11%)
  Pallas kernels  17.5 us (9%)
  local copies, waits for them, and re-layouts  9.45 us (5%)
  matrix products  7.6 us (4%)
  other arithmetic  3.47 us (2%)
    all_to_all x4, blocking collectives, swap(): return lax.all_to_all(x, axes, 0, 0, tiled=True)  76 us
    all_to_all x5, waiting for transfers between devices, swap(): return lax.all_to_all(x, axes, 0, 0, tiled=True)  58.6 us
    all_to_all x5, starting transfers between devices, swap(): return lax.all_to_all(x, axes, 0, 0, tiled=True)  22.2 us
    pallas_call x1, Pallas kernels, regroup(): pl.pallas_call(regroup_kernel, out_shape=(jax.ShapeDtypeStruct((N_TP, 2,...  9.74 us
    pallas_call x1, Pallas kernels, attend(): pl.pallas_call(attend_kernel, out_shape=jax.ShapeDtypeStruct((2, NEW, HEA...  7.76 us
    dot_general x4, matrix products, dot(): return lax.dot_general(a, b, dims, preferred_element_type=jnp.float32)  7.6 us
    unnamed x24, local copies, waits for them, and re-layouts  5.6 us
  transfers between devices with their start and end apart: 8, of which 8 were waited for; matrix products, arithmetic and copies ran while one was open for 2% of the time, Pallas kernels for 5%

profile of v1, /device:TPU:32, one launch (start us, length us, event | category | flops | bytes accessed | tf_op | source)
XLA Modules:
  0.0 199.2 jit_solution(11832382250207189658)
XLA Ops:
  0.0 0.7 copy-done
  0.7 0.2 dynamic-slice_reduce_fusion
  0.9 0.2 reduce-window.9
  1.1 0.7 reshape.142.fresh_ref
  1.9 2.3 %copy-done.1 = bf16[4096,576]{0,1:T(8,128)(2,1)S(1)} copy-done((bf16[4096,576]{0,1:T(8,128)(2,1)S(1)}, bf16[4096,576]{0,1:T(8,128)(2,1)}, u32[]{:S(2)}) %copy-start.1) | copy-done | bytes 4718616
  4.2 1.6 copy-done.2
  5.8 0.9 copy-done.3
  6.7 7.8 %attend.1 = bf16[2,12,1024]{2,1,0:T(8,128)(2,1)S(1)} custom-call(s32[8]{0:T(128)S(1)} %pad_add_fusion.bounds, bf16[192,576]{1,0:T(8,128)(2,1)S(1)} %bitcast.54, bf16[12,576]{1,0:T(8,128)(2,1)S(1)} %reshape.142.fresh_ref, bf16[576,4096]{1,0:T(8,128)(2,1)S(1)} %bitcast.53, bf16[16,512,128]{2,1,0:T(8,128)(2,1)S(1)} %copy-done.2), custom_call_target="tpu_custom_call" | custom-call | flops 1711276032 | bytes 7340032 | tf_op jit(solution)/shard_map/attend/pallas_call | solution.py:99
  14.5 3.9 %all_to_all.45 = bf16[2,12,1024]{2,1,0:T(8,128)(2,1)S(1)} all-to-all(bf16[2,12,1024]{2,1,0:T(8,128)(2,1)S(1)} %attend.1), channel_id=1, replica_groups=mesh['xl'=2,'z'=8,'c'=2,'xh'=2,'y'=4] {'c'}, dimensions={0} | all-to-all | bytes 98304 | tf_op jit(solution)/shard_map/all_to_all | solution.py:160
  18.5 0.1 broadcast_in_dim.40
  18.6 31.3 %all_to_all.46 = bf16[16,24,1024]{2,1,0:T(8,128)(2,1)} all-to-all(bf16[16,24,1024]{2,1,0:T(8,128)(2,1)S(1)} %broadcast_in_dim.40), channel_id=1, replica_groups=mesh['xl'=2,'z'=8,'c'=2,'xh'=2,'y'=4] {'xl','z'}, dimensions={0} | all-to-all | bytes 1572864 | tf_op jit(solution)/shard_map/all_to_all | solution.py:160
  49.8 0.2 reshape.137
  50.0 0.1 pad.9
  50.2 1.6 fusion.4
  51.9 0.6 collective-permute-done
  52.5 2.6 %fusion = bf16[256,384]{1,0:T(8,128)(2,1)} fusion(f32[256,384]{1,0:T(8,128)S(1)} %fusion.4, bf16[384,1024]{1,0:T(8,128)(2,1)} %collective-permute-done, bf16[256,2048]{1,0:T(8,128)(2,1)S(1)} %bitcast.61, s32[]{:T(128)S(6)} %select_n.19), kind=kOutput, calls=%fused_computation.3 | convolution fusion | flops 201523200 | bytes 1900548 | tf_op jit(solution)/shard_map/dot_general | solution.py:36
  55.0 6.6 %all-to-all-start.2 = ((bf16[8,32,384]{2,1,0:T(8,128)(2,1)}), bf16[8,32,384]{2,1,0:T(8,128)(2,1)S(1)}, u32[]{:S(2)}, u32[]{:S(2)}) async-start(bf16[8,32,384]{2,1,0:T(8,128)(2,1)} %bitcast.10), calls=%async_computation.2 | async-start | bytes 393216 | tf_op jit(solution)/shard_map/all_to_all | solution.py:160
  61.7 0.1 pad.20.clone
  61.8 0.8 dynamic-slice_convert_fusion
  62.5 7.6 %all-to-all-done.2 = bf16[8,32,384]{2,1,0:T(8,128)(2,1)S(1)} async-done(((bf16[8,32,384]{2,1,0:T(8,128)(2,1)}), bf16[8,32,384]{2,1,0:T(8,128)(2,1)S(1)}, u32[]{:S(2)}, u32[]{:S(2)}) %all-to-all-start.2) | async-done | bytes 196640 | tf_op jit(solution)/shard_map/all_to_all | solution.py:160
  70.2 0.1 multiply_convert_fusion
  70.3 0.1 maximum_maximum_fusion
  70.4 0.8 broadcast_in_dim.44
  71.2 4.1 %all-to-all-start.5 = ((bf16[16,32,384]{2,1,0:T(8,128)(2,1)}), bf16[16,32,384]{2,1,0:T(8,128)(2,1)S(1)}, u32[]{:S(2)}, u32[]{:S(2)}) async-start(bf16[16,32,384]{2,1,0:T(8,128)(2,1)} %broadcast_in_dim.44), calls=%async_computation.5 | async-start | bytes 786432 | tf_op jit(solution)/shard_map/all_to_all | solution.py:160
  75.4 9.7 %regroup.1 = (bf16[8,2,72,1024]{3,2,1,0:T(8,128)(2,1)}, bf16[8,72,1024]{2,1,0:T(8,128)(2,1)}) custom-call(s32[1,1024]{1,0:T(1,128)S(1)} %bitcast.55, bf16[72,7168]{1,0:T(8,128)(2,1)S(1)} %bitcast.56, bf16[72,7168]{1,0:T(8,128)(2,1)S(1)} %bitcast.57, bf16[72,7168]{1,0:T(8,128)(2,1)S(1)} %copy-done.6), custom_call_target="tpu_custom_call" | custom-call | flops 3170893824 | bytes 7340032 | tf_op jit(solution)/shard_map/regroup/pallas_call | solution.py:143
  85.1 1.7 all-to-all-done.5
  86.8 3.6 %all-to-all-start.4 = ((bf16[8,2,72,1024]{3,2,1,0:T(8,128)(2,1)}), bf16[8,2,72,1024]{3,2,1,0:T(8,128)(2,1)S(1)}, u32[]{:S(2)}, u32[]{:S(2)}) async-start(bf16[8,2,72,1024]{3,2,1,0:T(8,128)(2,1)} %get-tuple-element.8), calls=%async_computation.4 | async-start | bytes 4718592 | tf_op jit(solution)/shard_map/all_to_all | solution.py:160
  90.4 0.1 collective-permute-start.1
  90.5 0.1 pad.14.clone
  90.6 1.6 collective-permute-done.1
  92.3 1.0 pad_maximum_fusion.1
  93.3 23.9 %all-to-all-done.4 = bf16[8,2,72,1024]{3,2,1,0:T(8,128)(2,1)S(1)} async-done(((bf16[8,2,72,1024]{3,2,1,0:T(8,128)(2,1)}), bf16[8,2,72,1024]{3,2,1,0:T(8,128)(2,1)S(1)}, u32[]{:S(2)}, u32[]{:S(2)}) %all-to-all-start.4) | async-done | bytes 2359328 | tf_op jit(solution)/shard_map/all_to_all | solution.py:160
  117.1 2.5 %convolution_convert_fusion = bf16[1152,384]{1,0:T(8,128)(2,1)S(1)} fusion(bf16[1152,1024]{1,0:T(8,128)(2,1)S(1)} %bitcast.62, bf16[1024,384]{1,0:T(8,128)(2,1)} %bitcast.68), kind=kOutput, calls=%fused_computation | convolution fusion | flops 906412032 | bytes 4030464 | tf_op jit(solution)/shard_map/dot_general | solution.py:36
  119.7 0.1 pad_maximum_fusion
  119.8 20.8 %all_to_all.47 = bf16[8,152,384]{2,1,0:T(8,128)(2,1)S(1)} all-to-all(bf16[8,152,384]{2,1,0:T(8,128)(2,1)S(1)} %pad_maximum_fusion), channel_id=1, replica_groups=mesh['xl'=2,'z'=8,'c'=2,'xh'=2,'y'=4] {'xh','y'}, dimensions={0} | all-to-all | bytes 1867776 | tf_op jit(solution)/shard_map/all_to_all | solution.py:160
  140.6 3.6 %all-to-all-start.3 = ((bf16[8,72,1024]{2,1,0:T(8,128)(2,1)}), bf16[8,72,1024]{2,1,0:T(8,128)(2,1)S(1)}, u32[]{:S(2)}, u32[]{:S(2)}) async-start(bf16[8,72,1024]{2,1,0:T(8,128)(2,1)} %get-tuple-element.7), calls=%async_computation.3 | async-start | bytes 2359296 | tf_op jit(solution)/shard_map/all_to_all | solution.py:160
  144.2 0.1 convert_reduce_fusion
  144.4 15.7 %all-to-all-done.3 = bf16[8,72,1024]{2,1,0:T(8,128)(2,1)S(1)} async-done(((bf16[8,72,1024]{2,1,0:T(8,128)(2,1)}), bf16[8,72,1024]{2,1,0:T(8,128)(2,1)S(1)}, u32[]{:S(2)}, u32[]{:S(2)}) %all-to-all-start.3) | async-done | bytes 1179680 | tf_op jit(solution)/shard_map/all_to_all | solution.py:160
  160.1 0.8 broadcast_in_dim.47
  160.9 4.2 %all-to-all-start.7 = ((bf16[8,72,384]{2,1,0:T(8,128)(2,1)}), bf16[8,72,384]{2,1,0:T(8,128)(2,1)S(1)}, u32[]{:S(2)}, u32[]{:S(2)}) async-start(bf16[8,72,384]{2,1,0:T(8,128)(2,1)} %broadcast_in_dim.47), calls=%async_computation.7 | async-start | bytes 884736 | tf_op jit(solution)/shard_map/all_to_all | solution.py:160
  165.1 0.7 copy.17
  165.8 9.8 %all-to-all-done.7 = bf16[8,72,384]{2,1,0:T(8,128)(2,1)S(1)} async-done(((bf16[8,72,384]{2,1,0:T(8,128)(2,1)}), bf16[8,72,384]{2,1,0:T(8,128)(2,1)S(1)}, u32[]{:S(2)}, u32[]{:S(2)}) %all-to-all-start.7) | async-done | bytes 442400 | tf_op jit(solution)/shard_map/all_to_all | solution.py:160
  175.6 0.9 fusion.17
  176.6 0.1 collective-permute-start.2
  176.7 1.7 collective-permute-done.2
  178.4 0.1 fusion.2
  178.5 20.0 %all_to_all.48 = bf16[16,32,384]{2,1,0:T(8,128)(2,1)S(1)} all-to-all(bf16[16,32,384]{2,1,0:T(8,128)(2,1)S(1)} %bitcast.65), channel_id=1, replica_groups=mesh['xl'=2,'z'=8,'c'=2,'xh'=2,'y'=4] {'xl','z'}, dimensions={0} | all-to-all | bytes 786432 | tf_op jit(solution)/shard_map/all_to_all | solution.py:160
  198.5 0.6 fusion.12
  (42 shorter events, 0.6 us)
Async XLA Ops:
  0.0 0.7 copy-start
  1.9 2.3 %copy-start.1 = (bf16[4096,576]{0,1:T(8,128)(2,1)S(1)}, bf16[4096,576]{0,1:T(8,128)(2,1)}, u32[]{:S(2)}) copy-start(bf16[4096,576]{0,1:T(8,128)(2,1)} %param.16) | copy-start | bytes 14155780
  4.2 1.6 copy-start.2
  5.8 0.9 copy-start.3
  14.5 35.3 %copy-start.7 = (bf16[2048,224]{0,1:T(8,128)(2,1)S(1)}, bf16[2048,224]{0,1:T(8,128)(2,1)}, u32[]{:S(2)}) copy-start(bf16[2048,224]{0,1:T(8,128)(2,1)} %param.19) | copy-start | bytes 2752516
  49.8 2.6 %collective-permute-start = (bf16[384,1024]{1,0:T(8,128)(2,1)}, bf16[384,1024]{1,0:T(8,128)(2,1)}, u32[]{:S(2)}, u32[]{:S(2)}) collective-permute-start(bf16[384,1024]{1,0:T(8,128)(2,1)} %bitcast.9), channel_id=1, source_target_pairs={{0,8},{8,0},{1,9},{9,1},{2,10},{10,2},{3,11},{11,3},{4,12},{12,4},... | collective-permute-start | bytes 2359304 | tf_op jit(solution)/shard_map/ppermute | solution.py:168
  50.2 20.0 %copy-start.8 = (bf16[384,28]{0,1:T(8,128)(2,1)S(1)}, bf16[384,28]{0,1:T(8,128)(2,1)}, u32[]{:S(2)}) copy-start(bf16[384,28]{0,1:T(8,128)(2,1)} %param.20) | copy-start | bytes 64516
  51.8 23.5 %copy-start.9 = (s32[1024]{0:T(1024)S(1)}, s32[1024]{0:T(1024)}, u32[]{:S(2)}) copy-start(s32[1024]{0:T(1024)} %constant.71.clone) | copy-start | bytes 12292
  51.8 23.5 %copy-start.10 = (s32[1024]{0:T(1024)S(1)}, s32[1024]{0:T(1024)}, u32[]{:S(2)}) copy-start(s32[1024]{0:T(1024)} %constant.70.clone) | copy-start | bytes 12292
  51.8 23.5 %copy-start.11 = (pred[1024]{0:T(1024)(128)(4,1)S(1)}, pred[1024]{0:T(1024)(128)(4,1)}, u32[]{:S(2)}) copy-start(pred[1024]{0:T(1024)(128)(4,1)} %constant.72.clone) | copy-start | bytes 3076
  51.8 23.5 %copy-start.4 = (bf16[7168,72]{0,1:T(8,128)(2,1)S(1)}, bf16[7168,72]{0,1:T(8,128)(2,1)}, u32[]{:S(2)}) copy-start(bf16[7168,72]{0,1:T(8,128)(2,1)} %param.22) | copy-start | bytes 3096580
  51.8 23.5 %copy-start.5 = (bf16[7168,72]{0,1:T(8,128)(2,1)S(1)}, bf16[7168,72]{0,1:T(8,128)(2,1)}, u32[]{:S(2)}) copy-start(bf16[7168,72]{0,1:T(8,128)(2,1)} %param.23) | copy-start | bytes 3096580
  51.8 23.5 %copy-start.6 = (bf16[72,7168]{1,0:T(8,128)(2,1)S(1)}, bf16[72,7168]{1,0:T(8,128)(2,1)}, u32[]{:S(2)}) copy-start(bf16[72,7168]{1,0:T(8,128)(2,1)} %down_ref.1) | copy-start | bytes 3096580
  55.0 15.1 %all-to-all-start.2 = ((bf16[8,32,384]{2,1,0:T(8,128)(2,1)}), bf16[8,32,384]{2,1,0:T(8,128)(2,1)S(1)}, u32[]{:S(2)}, u32[]{:S(2)}) async-start(bf16[8,32,384]{2,1,0:T(8,128)(2,1)} %bitcast.10), calls=%async_computation.2 | async-start | bytes 393216 | tf_op jit(solution)/shard_map/all_to_all | solution.py:160
  71.2 15.6 %all-to-all-start.5 = ((bf16[16,32,384]{2,1,0:T(8,128)(2,1)}), bf16[16,32,384]{2,1,0:T(8,128)(2,1)S(1)}, u32[]{:S(2)}, u32[]{:S(2)}) async-start(bf16[16,32,384]{2,1,0:T(8,128)(2,1)} %broadcast_in_dim.44), calls=%async_computation.5 | async-start | bytes 786432 | tf_op jit(solution)/shard_map/all_to_all | solution.py:160
  86.8 30.4 %all-to-all-start.4 = ((bf16[8,2,72,1024]{3,2,1,0:T(8,128)(2,1)}), bf16[8,2,72,1024]{3,2,1,0:T(8,128)(2,1)S(1)}, u32[]{:S(2)}, u32[]{:S(2)}) async-start(bf16[8,2,72,1024]{3,2,1,0:T(8,128)(2,1)} %get-tuple-element.8), calls=%async_computation.4 | async-start | bytes 4718592 | tf_op jit(solution)/shard_map/all_to_all | solution.py:160
  90.4 1.8 collective-permute-start.1
  140.6 19.5 %all-to-all-start.3 = ((bf16[8,72,1024]{2,1,0:T(8,128)(2,1)}), bf16[8,72,1024]{2,1,0:T(8,128)(2,1)S(1)}, u32[]{:S(2)}, u32[]{:S(2)}) async-start(bf16[8,72,1024]{2,1,0:T(8,128)(2,1)} %get-tuple-element.7), calls=%async_computation.3 | async-start | bytes 2359296 | tf_op jit(solution)/shard_map/all_to_all | solution.py:160
  160.9 14.7 %all-to-all-start.7 = ((bf16[8,72,384]{2,1,0:T(8,128)(2,1)}), bf16[8,72,384]{2,1,0:T(8,128)(2,1)S(1)}, u32[]{:S(2)}, u32[]{:S(2)}) async-start(bf16[8,72,384]{2,1,0:T(8,128)(2,1)} %broadcast_in_dim.47), calls=%async_computation.7 | async-start | bytes 884736 | tf_op jit(solution)/shard_map/all_to_all | solution.py:160
  176.6 1.8 collective-permute-start.2

commit v2 on v1

v2 whole, which is shorter than its diff:
```python
import functools

import jax
import jax.numpy as jnp
from jax import lax
from jax.experimental import pallas as pl
from jax.experimental.pallas import tpu as pltpu
from jax.sharding import Mesh, PartitionSpec as P

DP = ("xl", "z", "c")
RING = ("xl", "z")
TP = ("xh", "y")
SIZES = {"xl": 2, "z": 8, "c": 2, "xh": 2, "y": 4}
N_RING, N_TP, N_Y = 16, 8, 4

STEPS, HEADS, REQ = 3, 16, 4
NEW = REQ * STEPS
ROWS = NEW * HEADS
TOKENS = 384
LAT, KDIM, VDIM = 512, 576, 128
HALF = HEADS // 2 * VDIM
CTX, CHUNK = 4096, 512
N_CHUNK = CTX // CHUNK
D, FEAT, PIECE, PAD = 7168, 224, 28, 32
PAIR = 2 * PIECE
SIDE = N_RING * PAIR
OUT = N_RING * 2 * PAD
FF, ROOM = 72, 80
EPS = 1e-06
LOG2E = 1.4426950408889634
SCALE = 192.0 ** (-0.5)
NEG = -1e30

NT = (((1,), (1,)), ((), ()))
TN = (((0,), (0,)), ((), ()))

VMEM = pl.BlockSpec(memory_space=pltpu.VMEM)
SMEM = pl.BlockSpec(memory_space=pltpu.SMEM)
ANY = pl.BlockSpec(memory_space=pl.ANY)


def params(mib=40):
    return pltpu.CompilerParams(vmem_limit_bytes=mib * 2**20)


def shape(*dims, dtype=jnp.bfloat16):
    return jax.ShapeDtypeStruct(dims, dtype)


def dot(a, b, dims=(((1,), (0,)), ((), ()))):
    return lax.dot_general(a, b, dims, preferred_element_type=jnp.float32)


def attend_kernel(
    lengths, q_ref, fresh_ref, cache_hbm, w_uv_hbm, mine_ref, theirs_ref, keys, scores, w_uv,
    new_keys, key_sems, w_sem,
):
    copies = [
        pltpu.make_async_copy(
            cache_hbm.at[:, pl.ds(j * CHUNK, CHUNK)], keys.at[j], key_sems.at[j]
        )
        for j in range(N_CHUNK)
    ]
    w_copy = pltpu.make_async_copy(w_uv_hbm, w_uv, w_sem)
    for copy in copies:
        copy.start()
    w_copy.start()

    dp_index = lax.axis_index(DP)
    q = q_ref[...]
    row = lax.broadcasted_iota(jnp.int32, (ROWS, 1), 0)
    request = row // (STEPS * HEADS)
    step = row // HEADS - request * STEPS
    low = jnp.zeros((ROWS, 1), jnp.int32)
    high = jnp.zeros((ROWS, 1), jnp.int32)
    start = 0
    for r in range(REQ):
        end = start + lengths[r, dp_index]
        low = jnp.where(request == r, start, low)
        high = jnp.where(request == r, end, high)
        start = end

    new_keys[...] = jnp.zeros_like(new_keys)
    for i in range(STEPS):
        new_keys[i * REQ : (i + 1) * REQ, :] = fresh_ref[i].astype(jnp.float32)
    fresh = new_keys[...].astype(jnp.bfloat16)
    key = lax.broadcasted_iota(jnp.int32, (ROWS, 16), 1)
    key_step = key // REQ
    seen = (key - key_step * REQ == request) & (key_step <= step)
    fresh_scores = jnp.where(seen, dot(q, fresh, NT) * (SCALE * LOG2E), NEG)
    top = jnp.max(fresh_scores, axis=1, keepdims=True)

    for j in range(N_CHUNK):
        copies[j].wait()
        slot = j * CHUNK + lax.broadcasted_iota(jnp.int32, (ROWS, CHUNK), 1)
        part = dot(q, keys[j]) * (SCALE * LOG2E)
        part = jnp.where((slot >= low) & (slot < high), part, NEG)
        scores[j] = part
        top = jnp.maximum(top, jnp.max(part, axis=1, keepdims=True))

    weights = jnp.exp2(fresh_scores - top)
    total = jnp.sum(weights, axis=1, keepdims=True)
    mixed = dot(weights.astype(jnp.bfloat16), fresh[:, :LAT])
    for j in range(N_CHUNK):
        weights = jnp.exp2(scores[j] - top)
        total = total + jnp.sum(weights, axis=1, keepdims=True)
        mixed = mixed + dot(weights.astype(jnp.bfloat16), keys[j, :LAT, :], NT)
    mixed = (mixed / total).astype(jnp.bfloat16)

    w_copy.wait()
    head = row - (row // HEADS) * HEADS
    halves = []
    for half in range(2):
        values = []
        for h in range(half * HEADS // 2, (half + 1) * HEADS // 2):
            value = jnp.where(head == h, dot(mixed, w_uv[h]), 0.0)
            values.append(jnp.sum(value.reshape(NEW, HEADS, VDIM), axis=1))
        halves.append(jnp.concatenate(values, axis=1))
    second = lax.axis_index("c") == 1
    mine_ref[...] = jnp.where(second, halves[1], halves[0]).astype(jnp.bfloat16)
    theirs_ref[...] = jnp.where(second, halves[0], halves[1]).astype(jnp.bfloat16)


def attend(lengths, q, fresh, cache_t, w_uv):
    return pl.pallas_call(
        attend_kernel,
        out_shape=(shape(NEW, HALF), shape(NEW, HALF)),
        in_specs=[SMEM, VMEM, VMEM, ANY, ANY],
        out_specs=(VMEM, VMEM),
        scratch_shapes=[
            pltpu.VMEM((N_CHUNK, KDIM, CHUNK), jnp.bfloat16),
            pltpu.VMEM((N_CHUNK, ROWS, CHUNK), jnp.float32),
            pltpu.VMEM((HEADS, LAT, VDIM), jnp.bfloat16),
            pltpu.VMEM((16, KDIM), jnp.float32),
            pltpu.SemaphoreType.DMA((N_CHUNK,)),
            pltpu.SemaphoreType.DMA,
        ],
        compiler_params=params(58),
        cost_estimate=pl.CostEstimate(
            flops=2 * ROWS * CTX * (KDIM + LAT), bytes_accessed=7 * 2**20, transcendentals=ROWS * CTX
        ),
        name="attend",
    )(lengths, q, fresh, cache_t, w_uv)


def fan_kernel(mine_ref, theirs_ref, out_ref):
    second = lax.axis_index("c") == 1
    mine, theirs = mine_ref[...].astype(jnp.float32), theirs_ref[...].astype(jnp.float32)
    both = jnp.concatenate(
        [jnp.where(second, theirs, mine), jnp.where(second, mine, theirs)], axis=0
    ).astype(jnp.bfloat16)
    for i in range(N_RING):
        out_ref[i] = both


def fan(mine, theirs):
    return pl.pallas_call(
        fan_kernel,
        out_shape=shape(N_RING, 2 * NEW, HALF),
        in_specs=[VMEM, VMEM],
        out_specs=VMEM,
        compiler_params=params(),
        name="fan",
    )(mine, theirs)


def pick_columns(piece, width):
    lane = lax.broadcasted_iota(jnp.int32, (1, N_Y * 8 * piece), 1)
    k, rest = lane // (8 * piece), lane % (8 * piece)
    side, rest = rest // (4 * piece), rest % (4 * piece)
    u, rest = rest // (2 * piece), rest % (2 * piece)
    xh, j = rest // piece, rest % piece
    source = (2 * u + (side ^ lax.axis_index("c"))) * FEAT
    source = source + (xh * N_Y + (k ^ lax.axis_index("y"))) * PIECE + j
    source = jnp.where(j < PIECE, source, -1)
    rows = lax.broadcasted_iota(jnp.int32, (width, N_Y * 8 * piece), 0)
    return jnp.where(rows == source, 1.0, 0.0).astype(jnp.bfloat16)


def regroup_kernel(gate_ref, up_ref, down_ref, gain_ref, _, *refs):
    mix_refs, down_refs, rows = refs[:N_Y], refs[N_Y:-1], refs[-1]
    gain = gain_ref[...].astype(jnp.float32)
    for i, ref in enumerate((gate_ref, up_ref)):
        rows[i * ROOM + ROOM - 16 : (i + 1) * ROOM, :] = jnp.zeros((16, D), jnp.bfloat16)
        rows[i * ROOM : i * ROOM + FF, :] = (ref[...].astype(jnp.float32) * gain).astype(jnp.bfloat16)
    rows[3 * ROOM - 16 : 3 * ROOM, :] = jnp.zeros((16, D), jnp.bfloat16)
    rows[2 * ROOM : 2 * ROOM + FF, :] = down_ref[...]
    width = 4 * FEAT
    for first, last, refs, piece in ((0, 2 * ROOM, mix_refs, PIECE), (2 * ROOM, 3 * ROOM, down_refs, PAD)):
        pick = pick_columns(piece, width)
        size = 4 * piece
        for m in range(D // width):
            moved = dot(rows[first:last, m * width : (m + 1) * width], pick).astype(jnp.bfloat16)
            for k in range(N_Y):
                for side in range(2):
                    at, to = (2 * k + side) * size, (side * 8 + m) * size
                    refs[k][:, to : to + size] = moved[:, at : at + size]


def regroup(gate_t, up_t, down, gain, after):
    return pl.pallas_call(
        regroup_kernel,
        out_shape=[shape(2 * ROOM, 2 * SIDE)] * N_Y + [shape(ROOM, 2 * OUT)] * N_Y,
        in_specs=[VMEM] * 4 + [ANY],
        out_specs=[VMEM] * (2 * N_Y),
        scratch_shapes=[pltpu.VMEM((3 * ROOM, D), jnp.bfloat16)],
        compiler_params=params(),
        cost_estimate=pl.CostEstimate(
            flops=2 * 3 * ROOM * D * 1024, bytes_accessed=7 * 2**20, transcendentals=0
        ),
        name="regroup",
    )(gate_t, up_t, down, gain, after)


def project_kernel(first_ref, heads_ref, w_ref, out_ref):
    lanes = pl.ds(pl.multiple_of((1 - lax.axis_index("c")) * HALF, HALF), HALF)
    total = first_ref[...] + dot(w_ref[:, lanes], heads_ref[...], NT)
    total = total.astype(jnp.bfloat16)
    out_ref[0] = total
    out_ref[1] = total


def project(first, heads, w_ot):
    return pl.pallas_call(
        project_kernel,
        out_shape=shape(2, FEAT, TOKENS),
        in_specs=[VMEM, VMEM, VMEM],
        out_specs=VMEM,
        compiler_params=params(),
        name="project",
    )(first, heads, w_ot)


def update_kernel(parts_ref, residual_ref, updated_ref, out_ref):
    attended = jnp.sum(parts_ref[...].astype(jnp.float32), axis=0)
    updated = (residual_ref[...].astype(jnp.float32) + attended).astype(jnp.bfloat16)
    updated_ref[...] = updated
    for i in range(N_RING):
        out_ref[i] = updated


def update(parts, residual):
    return pl.pallas_call(
        update_kernel,
        out_shape=(shape(PAIR, TOKENS), shape(N_RING, PAIR, TOKENS)),
        in_specs=[VMEM] * 2,
        out_specs=(VMEM, VMEM),
        compiler_params=params(),
        name="update",
    )(parts, residual)


def squares_of(ref):
    wide = ref[...].astype(jnp.float32)
    return jnp.sum(wide * wide, axis=(0, 1))[None]


def mix_own_kernel(own_ref, *refs):
    blocks, (out_ref, squares_ref, held, sems) = refs[:N_Y], refs[N_Y:]
    copies = [
        pltpu.make_async_copy(blocks[k].at[:, pl.ds(0, SIDE)], held.at[k], sems.at[k])
        for k in range(N_Y)
    ]
    for copy in copies:
        copy.start()
    squares_ref[...] = squares_of(own_ref)
    own = own_ref[...].reshape(SIDE, TOKENS)
    for k in range(N_Y):
        copies[k].wait()
        out_ref[k] = dot(held[k], own)


def mix_more_kernel(part_ref, squares_ref, more_ref, *refs):
    blocks, (out_ref, held, sems) = refs[:N_Y], refs[N_Y:]
    copies = [
        pltpu.make_async_copy(blocks[k].at[:, pl.ds(SIDE, SIDE)], held.at[k], sems.at[k])
        for k in range(N_Y)
    ]
    for copy in copies:
        copy.start()
    squares = squares_ref[...] + squares_of(more_ref)
    more = more_ref[...].reshape(SIDE, TOKENS)
    high = squares.astype(jnp.bfloat16).astype(jnp.float32)
    row = lax.broadcasted_iota(jnp.int32, (2 * ROOM, TOKENS), 0)
    y = lax.axis_index("y")
    for k in range(N_Y):
        copies[k].wait()
        part = part_ref[k] + dot(held[k], more)
        part = jnp.where(row == FF, high, jnp.where(row == FF + 1, squares - high, part))
        out_ref[y ^ k] = part.astype(jnp.bfloat16)


def mix(own, more, blocks):
    scratch = [
        pltpu.VMEM((N_Y, 2 * ROOM, SIDE), jnp.bfloat16),
        pltpu.SemaphoreType.DMA((N_Y,)),
    ]
    cost = pl.CostEstimate(
        flops=2 * N_Y * 2 * ROOM * SIDE * TOKENS, bytes_accessed=4 * 2**20, transcendentals=0
    )
    part, squares = pl.pallas_call(
        mix_own_kernel,
        out_shape=(
            shape(N_Y, 2 * ROOM, TOKENS, dtype=jnp.float32),
            shape(1, TOKENS, dtype=jnp.float32),
        ),
        in_specs=[VMEM] + [ANY] * N_Y,
        out_specs=(VMEM, VMEM),
        scratch_shapes=scratch,
        compiler_params=params(),
        cost_estimate=cost,
        name="mix_own",
    )(own, *blocks)
    return pl.pallas_call(
        mix_more_kernel,
        out_shape=shape(N_Y, 2 * ROOM, TOKENS),
        in_specs=[VMEM] * 3 + [ANY] * N_Y,
        out_specs=VMEM,
        scratch_shapes=scratch,
        compiler_params=params(),
        cost_estimate=cost,
        name="mix_more",
    )(part, squares, more, *blocks)


def gate_kernel(parts_ref, out_ref):
    total = jnp.sum(parts_ref[...].astype(jnp.float32), axis=0)
    mean = (total[FF : FF + 1] + total[FF + 1 : FF + 2]) * (1.0 / D)
    inverse_rms = lax.rsqrt(mean + EPS)
    gate_out, up_out = total[:ROOM] * inverse_rms, total[ROOM:] * inverse_rms
    row = lax.broadcasted_iota(jnp.int32, (ROOM, TOKENS), 0)
    hidden = jnp.where(row < FF, gate_out / (1.0 + jnp.exp(-gate_out)) * up_out, 0.0)
    hidden = hidden.astype(jnp.bfloat16)
    for t in range(N_Y):
        out_ref[t] = hidden


def gate(parts):
    return pl.pallas_call(
        gate_kernel,
        out_shape=shape(N_Y, ROOM, TOKENS),
        in_specs=[VMEM],
        out_specs=VMEM,
        compiler_params=params(),
        name="gate",
    )(parts)


def down_kernel(side, hidden_ref, *refs):
    blocks, (out_ref, held, hidden, sems) = refs[:N_Y], refs[N_Y:]
    copies = [
        pltpu.make_async_copy(
            blocks[k].at[:, pl.ds(side * OUT, OUT)], held.at[pl.ds(k * ROOM, ROOM), :], sems.at[k]
        )
        for k in range(N_Y)
    ]
    for copy in copies:
        copy.start()
    y = lax.axis_index("y")
    for k in range(N_Y):
        hidden[k * ROOM : (k + 1) * ROOM, :] = hidden_ref[y ^ k]
    for copy in copies:
        copy.wait()
    out_ref[...] = dot(held[...], hidden[...], TN).astype(out_ref.dtype)


def down(side, hidden, blocks):
    return pl.pallas_call(
        functools.partial(down_kernel, side),
        out_shape=shape(OUT, TOKENS, dtype=jnp.bfloat16 if side else jnp.float32),
        in_specs=[VMEM] + [ANY] * N_Y,
        out_specs=VMEM,
        scratch_shapes=[
            pltpu.VMEM((N_Y * ROOM, OUT), jnp.bfloat16),
            pltpu.VMEM((N_Y * ROOM, TOKENS), jnp.bfloat16),
            pltpu.SemaphoreType.DMA((N_Y,)),
        ],
        compiler_params=params(),
        cost_estimate=pl.CostEstimate(
            flops=2 * N_Y * ROOM * OUT * TOKENS, bytes_accessed=3 * 2**20, transcendentals=0
        ),
        name="down",
    )(hidden, *blocks)


def swap(x, axes):
    return lax.all_to_all(x, axes, 0, 0, tiled=True)


def other_core(x):
    return lax.ppermute(x, "c", [(0, 1), (1, 0)])


def other_half(x):
    return lax.ppermute(x, "xh", [(0, 1), (1, 0)])


def body(
    queries, new_latent, cache, cache_lengths, w_uv, w_o, residual, norm_gain, w_gate, w_up, w_down
):
    core, xh = lax.axis_index("c"), lax.axis_index("xh")

    fresh = jnp.transpose(new_latent, (1, 0, 2))
    mine, theirs = attend(
        cache_lengths.T, queries.reshape(ROWS, KDIM), fresh, cache.T, w_uv
    )

    blocks = regroup(w_gate.T, w_up.T, w_down, norm_gain[None], mine)
    mix_blocks, down_blocks = list(blocks[:N_Y]), list(blocks[N_Y:])

    def exchange(blocks, which):
        for k in which:
            blocks[k] = lax.ppermute(blocks[k], "y", [(i, i ^ k) for i in range(N_Y)])

    def fence(*x):
        out = lax.optimization_barrier((*x, *mix_blocks, *down_blocks))
        mix_blocks[:], down_blocks[:] = out[-2 * N_Y : -N_Y], out[-N_Y:]
        return out[: -2 * N_Y]

    partner = other_half(residual.T)
    residual = jnp.concatenate(
        [jnp.where(xh == 0, residual.T, partner), jnp.where(xh == 0, partner, residual.T)], axis=0
    )
    w_ot = w_o.T.reshape(2, N_Y, PIECE, HEADS * VDIM).transpose(1, 0, 2, 3)
    w_ot = w_ot.reshape(FEAT, HEADS * VDIM)
    w_own = lax.dynamic_slice_in_dim(w_ot, core * HALF, HALF, 1)

    heads = swap(fan(mine, other_core(theirs)), RING).reshape(TOKENS, HALF)
    exchange(mix_blocks, (1, 3))
    heads, residual, w_ot, w_own = fence(heads, residual, w_ot, w_own)
    more_heads = other_core(heads)
    first = dot(w_own, heads, NT)
    exchange(down_blocks, (2,))
    (partial,) = fence(project(first, more_heads, w_ot))

    updated, block = update(swap(partial.reshape(N_TP, PAIR, TOKENS), TP), residual)
    exchange(mix_blocks, (2,))
    exchange(down_blocks, (1, 3))
    (own,) = fence(swap(block, RING))
    hidden = gate(swap(mix(own, other_core(own), mix_blocks), "y"))
    hidden = swap(hidden, "y")
    more = other_core(down(1, hidden, down_blocks))
    term = down(0, hidden, down_blocks) + more.astype(jnp.float32)
    term = swap(term.astype(jnp.bfloat16).reshape(2 * N_RING, PAD, TOKENS), RING + ("xh",))
    term = jnp.sum(term.astype(jnp.float32), axis=0)[:PIECE]
    updated = jnp.where(xh == 0, updated[:PIECE], updated[PIECE:])
    return (updated.astype(jnp.float32) + term).astype(jnp.bfloat16).T


def solution(mesh):
    parts = Mesh(mesh.devices.reshape(tuple(SIZES.values())), tuple(SIZES))
    everywhere = DP + TP
    return jax.shard_map(
        body,
        mesh=parts,
        in_specs=(
            P(DP, None, TP, None),
            P(DP, None, None),
            P(DP, None),
            P(),
            P(TP, None, None),
            P(TP, DP),
            P(None, everywhere),
            P(),
            P(None, everywhere),
            P(None, everywhere),
            P(everywhere, None),
        ),
        out_specs=P(None, everywhere),
        check_vma=False,
    )
```

time: 200 us -> 169 us (0.84)
  waiting for transfers between devices: 62.5 us -> 31.2 us
  starting transfers between devices: 22.4 us -> 29.7 us
  blocking collectives: 76 us -> 68.9 us
  matrix products: 7.6 us -> 1.72 us
  Pallas kernels: 17.5 us -> 22.4 us
  local copies, waits for them, and re-layouts: 9.45 us -> 13 us
  other arithmetic: 3.47 us -> 0.97 us
    all_to_all x5 -> x2, waiting for transfers between devices: 58.6 us -> 0.01 us  [swap(): return lax.all_to_all(x, axes, 0, 0, tiled=True)]
    ppermute x0 -> x7, waiting for transfers between devices: none -> 28 us  [the longest x6 28 us: exchange(): blocks[k] = lax.ppermute(blocks[k], 'y', [(i, i ^ k) for i in range(N_Y)])]
    ppermute x0 -> x7, starting transfers between devices: none -> 12.4 us  [the longest x6 9.7 us: exchange(): blocks[k] = lax.ppermute(blocks[k], 'y', [(i, i ^ k) for i in range(N_Y)])]
    all_to_all x4, blocking collectives: 76 us -> 68.9 us  [swap(): return lax.all_to_all(x, axes, 0, 0, tiled=True)]
    dot_general x4 -> x1, matrix products: 7.6 us -> 1.72 us  [dot(): return lax.dot_general(a, b, dims, preferred_element_type=jnp.float32)]
    all_to_all x5 -> x2, starting transfers between devices: 22.2 us -> 17 us  [swap(): return lax.all_to_all(x, axes, 0, 0, tiled=True)]
    pallas_call x2 -> x10, Pallas kernels: 17.5 us -> 22.4 us  [the longest x1 8.91 us: attend(): pl.pallas_call(attend_kernel, out_shape=(shape(NEW, HALF), shape(NEW, HAL...]
    reshape x2, local copies, waits for them, and re-layouts: 0.92 us -> 3.59 us  [the longest x1 2.22 us: body(): w_ot = w_o.T.reshape(2, N_Y, PIECE, HEADS * VDIM).transpose(1, 0, 2, 3)]
  transfers between devices with their start and end apart: 8 -> 13, of which waited for: 8 -> 8; matrix products, arithmetic and copies ran while one was open for 2% -> 5% of each run, Pallas kernels for 5% -> 6%
where the time goes in v2:
time: 169 us; the launch traced here: 168 us
  blocking collectives  68.9 us (41%)
  waiting for transfers between devices  31.2 us (18%)
  starting transfers between devices  29.7 us (18%)
  Pallas kernels  22.4 us (13%)
  local copies, waits for them, and re-layouts  13 us (8%)
  matrix products  1.72 us (1%)
    all_to_all x4, blocking collectives, swap(): return lax.all_to_all(x, axes, 0, 0, tiled=True)  68.9 us
    ppermute x6, waiting for transfers between devices, exchange(): blocks[k] = lax.ppermute(blocks[k], 'y', [(i, i ^ k) for i in range(N_Y)])  28 us
    all_to_all x2, starting transfers between devices, swap(): return lax.all_to_all(x, axes, 0, 0, tiled=True)  17 us
    ppermute x6, starting transfers between devices, exchange(): blocks[k] = lax.ppermute(blocks[k], 'y', [(i, i ^ k) for i in range(N_Y)])  9.7 us
    pallas_call x1, Pallas kernels, attend(): pl.pallas_call(attend_kernel, out_shape=(shape(NEW, HALF), shape(NEW, HAL...  8.91 us
    pallas_call x1, Pallas kernels, regroup(): pl.pallas_call(regroup_kernel, out_shape=[shape(2 * ROOM, 2 * SIDE)] * N_...  6.75 us
    unnamed x36, local copies, waits for them, and re-layouts  6.29 us
  transfers between devices with their start and end apart: 13, of which 8 were waited for; matrix products, arithmetic and copies ran while one was open for 5% of the time, Pallas kernels for 6%

profile of v2, /device:TPU:32, one launch (start us, length us, event | category | flops | bytes accessed | tf_op | source)
XLA Modules:
  0.0 168.1 jit_solution(11993602954198744987)
XLA Ops:
  0.0 8.9 %attend.1 = (bf16[12,1024]{1,0:T(8,128)(2,1)}, bf16[12,1024]{1,0:T(8,128)(2,1)}) custom-call(s32[4,32]{1,0:T(4,128)} %bitcast.28, bf16[192,576]{1,0:T(8,128)(2,1)} %bitcast.25, bf16[3,4,576]{2,1,0:T(4,128)(2,1)} %bitcast.27, bf16[576,4096]{1,0:T(8,128)(2,1)} %bitcast.21, bf16[16,512,128]{2,1,0:T(8,128)(2,1)} %w_uv_hbm.1), custom_call_target="tpu_custom_call" | custom-call | flops 1711276032 | bytes 7340032 | tf_op jit(solution)/shard_map/attend/pallas_call | solution.py:125
  8.9 0.1 collective-permute-start
  9.0 1.4 collective-permute-done.theirs_ref
  10.4 0.8 copy-done.7
  11.2 1.0 fan.1
  12.2 9.5 %all-to-all-start = ((bf16[16,24,1024]{2,1,0:T(8,128)(2,1)}), bf16[16,24,1024]{2,1,0:T(8,128)(2,1)}, u32[]{:S(2)}, u32[]{:S(2)}) async-start(bf16[16,24,1024]{2,1,0:T(8,128)(2,1)} %fan.1), calls=%async_computation | async-start | bytes 1572864 | tf_op jit(solution)/shard_map/all_to_all | solution.py:387
  21.8 1.2 copy-done.10
  23.0 1.2 copy-done.11
  24.2 6.7 %regroup.1 = (bf16[160,1792]{1,0:T(8,128)(2,1)S(1)}, bf16[160,1792]{1,0:T(8,128)(2,1)}, bf16[160,1792]{1,0:T(8,128)(2,1)S(1)}, bf16[160,1792]{1,0:T(8,128)(2,1)}...) custom-call(bf16[72,7168]{1,0:T(8,128)(2,1)S(1)} %bitcast.19, ...), custom_call_target="tpu_custom_call" | custom-call | flops 3523215360 | bytes 7340032 | tf_op jit(solution)/shard_map/regroup/pallas_call | solution.py:201
  30.9 0.7 copy-done.15
  31.7 1.6 collective-permute-start.2
  33.3 2.3 %collective-permute-start.3 = (bf16[160,1792]{1,0:T(8,128)(2,1)}, bf16[160,1792]{1,0:T(8,128)(2,1)S(1)}, u32[]{:S(2)}, u32[]{:S(2)}) collective-permute-start(bf16[160,1792]{1,0:T(8,128)(2,1)} %get-tuple-element.54), channel_id=1, source_target_pairs={{0,3},{1,2},{2,1},{3,0},{4,7},{5,6},{6,5},{7,4},{8,11},{9,10},{10,... | collective-permute-start | bytes 1720328 | tf_op jit(solution)/shard_map/ppermute | solution.py:413
  35.6 2.7 %collective-permute-start.1 = (bf16[28,384]{1,0:T(8,128)(2,1)S(1)}, bf16[28,384]{1,0:T(8,128)(2,1)S(1)}, u32[]{:S(2)}, u32[]{:S(2)}) collective-permute-start(bf16[28,384]{1,0:T(8,128)(2,1)S(1)} %bitcast.26), channel_id=1, source_target_pairs={{0,4},{4,0},{1,5},{5,1},{2,6},{6,2},{3,7},{7,3},{8,12},{12,8},{9,1... | collective-permute-start | bytes 64520 | tf_op jit(solution)/shard_map/ppermute | solution.py:395
  38.3 2.2 %reshape.20 = bf16[2,4,28,2048]{3,2,1,0:T(8,128)(2,1)} reshape(bf16[224,2048]{1,0:T(8,128)(2,1)} %bitcast.24) | data formatting | bytes 1835008 | tf_op jit(solution)/shard_map/reshape | solution.py:424
  40.6 2.3 %copy.13 = bf16[4,2,28,2048]{3,2,1,0:T(8,128)(2,1)} copy(bf16[4,2,28,2048]{3,2,0,1:T(8,128)(2,1)} %bitcast.22) | data formatting | bytes 1835008 | tf_op jit(solution)/shard_map/transpose | solution.py:424
  42.9 1.4 reshape.21.w_ref
  44.2 0.8 constant_dynamic-slice_fusion
  45.1 1.3 collective-permute-done.2.refs_1_
  46.4 2.5 %collective-permute-done.3.refs_3_ = bf16[160,1792]{1,0:T(8,128)(2,1)S(1)} collective-permute-done((bf16[160,1792]{1,0:T(8,128)(2,1)}, bf16[160,1792]{1,0:T(8,128)(2,1)S(1)}, u32[]{:S(2)}, u32[]{:S(2)}) %collective-permute-start.3) | collective-permute-done | bytes 573472 | tf_op jit(solution)/shard_map/ppermute | solution.py:413
  48.9 1.7 %collective-permute-start.5 = (bf16[80,2048]{1,0:T(8,128)(2,1)}, bf16[80,2048]{1,0:T(8,128)(2,1)S(1)}, u32[]{:S(2)}, u32[]{:S(2)}) collective-permute-start(bf16[80,2048]{1,0:T(8,128)(2,1)} %copy-done.15), channel_id=1, source_target_pairs={{0,2},{1,3},{2,0},{3,1},{4,6},{5,7},{6,4},{7,5},{8,10},{9,11},{10,... | collective-permute-start | bytes 983048 | tf_op jit(solution)/shard_map/ppermute | solution.py:413
  50.6 1.7 %fusion.2.first_ref = f32[224,384]{1,0:T(8,128)S(1)} fusion(bf16[224,1024]{1,0:T(8,128)(2,1)} %constant_dynamic-slice_fusion, bf16[384,1024]{1,0:T(8,128)(2,1)} %bitcast.4), kind=kOutput, calls=%fused_computation.9 | convolution fusion | flops 176160768 | bytes 1589248 | tf_op jit(solution)/shard_map/dot_general | solution.py:51
  52.3 0.5 project.1
  52.8 7.9 %collective-permute-done.5.refs_2_ = bf16[80,2048]{1,0:T(8,128)(2,1)S(1)} collective-permute-done((bf16[80,2048]{1,0:T(8,128)(2,1)}, bf16[80,2048]{1,0:T(8,128)(2,1)S(1)}, u32[]{:S(2)}, u32[]{:S(2)}) %collective-permute-start.5) | collective-permute-done | bytes 327712 | tf_op jit(solution)/shard_map/ppermute | solution.py:413
  60.7 15.5 %all_to_all.30.parts_ref = bf16[8,56,384]{2,1,0:T(8,128)(2,1)S(1)} all-to-all(bf16[8,56,384]{2,1,0:T(8,128)(2,1)S(1)} %bitcast.18), channel_id=1, replica_groups=mesh['xl'=2,'z'=8,'c'=2,'xh'=2,'y'=4] {'xh','y'}, dimensions={0} | all-to-all | bytes 688128 | tf_op jit(solution)/shard_map/all_to_all | solution.py:387
  76.2 0.1 update.1
  76.3 0.8 copy-done.6
  77.1 7.5 %all-to-all-start.2 = ((bf16[16,56,384]{2,1,0:T(8,128)(2,1)}), bf16[16,56,384]{2,1,0:T(8,128)(2,1)S(1)}, u32[]{:S(2)}, u32[]{:S(2)}) async-start(bf16[16,56,384]{2,1,0:T(8,128)(2,1)} %copy-done.6), calls=%async_computation.2 | async-start | bytes 1376256 | tf_op jit(solution)/shard_map/all_to_all | solution.py:387
  84.7 1.1 collective-permute-start.6
  85.7 1.0 collective-permute-start.7
  86.7 2.1 %collective-permute-start.8 = (bf16[80,2048]{1,0:T(8,128)(2,1)}, bf16[80,2048]{1,0:T(8,128)(2,1)S(1)}, u32[]{:S(2)}, u32[]{:S(2)}) collective-permute-start(bf16[80,2048]{1,0:T(8,128)(2,1)} %copy-done.13), channel_id=1, source_target_pairs={{0,3},{1,2},{2,1},{3,0},{4,7},{5,6},{6,5},{7,4},{8,11},{9,10},{10,... | collective-permute-start | bytes 983048 | tf_op jit(solution)/shard_map/ppermute | solution.py:413
  88.8 15.5 %collective-permute-done.7.refs_1_ = bf16[80,2048]{1,0:T(8,128)(2,1)S(1)} collective-permute-done((bf16[80,2048]{1,0:T(8,128)(2,1)}, bf16[80,2048]{1,0:T(8,128)(2,1)S(1)}, u32[]{:S(2)}, u32[]{:S(2)}) %collective-permute-start.7) | collective-permute-done | bytes 327712 | tf_op jit(solution)/shard_map/ppermute | solution.py:413
  104.3 0.7 copy-done.2
  105.0 0.7 collective-permute-done.8.refs_3_
  105.8 0.7 copy-done.4
  106.5 1.7 mix_own.1
  108.2 0.5 collective-permute-done.9.more_ref
  108.6 1.7 mix_more.1
  110.4 12.6 %all_to_all.31.parts_ref = bf16[4,160,384]{2,1,0:T(8,128)(2,1)S(1)} all-to-all(bf16[4,160,384]{2,1,0:T(8,128)(2,1)S(1)} %mix_more.1), channel_id=1, replica_groups=mesh['xl'=2,'z'=8,'c'=2,'xh'=2,'y'=4] {'y'}, dimensions={0} | all-to-all | bytes 983040 | tf_op jit(solution)/shard_map/all_to_all | solution.py:387
  123.0 0.1 gate.1
  123.1 9.0 %all_to_all.32.hidden_ref = bf16[4,80,384]{2,1,0:T(8,128)(2,1)S(1)} all-to-all(bf16[4,80,384]{2,1,0:T(8,128)(2,1)S(1)} %gate.1), channel_id=1, replica_groups=mesh['xl'=2,'z'=8,'c'=2,'xh'=2,'y'=4] {'y'}, dimensions={0} | all-to-all | bytes 491520 | tf_op jit(solution)/shard_map/all_to_all | solution.py:387
  132.1 0.9 down.3
  132.9 0.1 collective-permute-start.10
  133.0 0.9 down.2
  133.9 1.4 collective-permute-done.10
  135.3 0.2 add_convert_fusion
  135.5 31.8 %all_to_all.33 = bf16[32,32,384]{2,1,0:T(8,128)(2,1)S(1)} all-to-all(bf16[32,32,384]{2,1,0:T(8,128)(2,1)S(1)} %bitcast.23), channel_id=1, replica_groups=mesh['xl'=2,'z'=8,'c'=2,'xh'=2,'y'=4] {'xl','z','xh'}, dimensions={0} | all-to-all | bytes 1572864 | tf_op jit(solution)/shard_map/all_to_all | solution.py:387
  167.4 0.1 convert_reduce_fusion
  167.5 0.6 fusion.1
  (39 shorter events, 0.1 us)
Async XLA Ops:
  0.0 21.7 %copy-start.17 = (bf16[7168]{0:T(1024)(128)(2,1)S(1)}, bf16[7168]{0:T(1024)(128)(2,1)}, u32[]{:S(2)}) copy-start(bf16[7168]{0:T(1024)(128)(2,1)} %param.18) | copy-start | bytes 43012
  0.0 21.7 %copy-start.9 = (bf16[7168,72]{0,1:T(8,128)(2,1)S(1)}, bf16[7168,72]{0,1:T(8,128)(2,1)}, u32[]{:S(2)}) copy-start(bf16[7168,72]{0,1:T(8,128)(2,1)} %param.19) | copy-start | bytes 3096580
  8.9 1.5 collective-permute-start
  10.4 0.8 copy-start.7
  11.2 10.5 %copy-start.8 = (bf16[12,1024]{1,0:T(8,128)(2,1)S(1)}, bf16[12,1024]{1,0:T(8,128)(2,1)}, u32[]{:S(2)}) copy-start(bf16[12,1024]{1,0:T(8,128)(2,1)} %get-tuple-element.49.mine_ref._) | copy-start | bytes 73732
  12.2 36.7 %all-to-all-start = ((bf16[16,24,1024]{2,1,0:T(8,128)(2,1)}), bf16[16,24,1024]{2,1,0:T(8,128)(2,1)}, u32[]{:S(2)}, u32[]{:S(2)}) async-start(bf16[16,24,1024]{2,1,0:T(8,128)(2,1)} %fan.1), calls=%async_computation | async-start | bytes 1572864 | tf_op jit(solution)/shard_map/all_to_all | solution.py:387
  21.7 1.2 copy-start.10
  23.0 1.2 copy-start.11
  24.2 11.4 %copy-start.16 = (bf16[384,28]{0,1:T(8,128)(2,1)S(1)}, bf16[384,28]{0,1:T(8,128)(2,1)}, u32[]{:S(2)}) copy-start(bf16[384,28]{0,1:T(8,128)(2,1)} %param.17) | copy-start | bytes 64516
  30.9 0.7 copy-start.15
  31.7 1.6 copy-start.12
  31.7 1.6 copy-start.13
  31.7 3.9 %copy-start.14 = (bf16[80,2048]{1,0:T(8,128)(2,1)}, bf16[80,2048]{1,0:T(8,128)(2,1)S(1)}, u32[]{:S(2)}) copy-start(bf16[80,2048]{1,0:T(8,128)(2,1)S(1)} %get-tuple-element.79) | copy-start | bytes 983044
  31.7 14.7 %collective-permute-start.2 = (bf16[160,1792]{1,0:T(8,128)(2,1)}, bf16[160,1792]{1,0:T(8,128)(2,1)S(1)}, u32[]{:S(2)}, u32[]{:S(2)}) collective-permute-start(bf16[160,1792]{1,0:T(8,128)(2,1)} %get-tuple-element.52), channel_id=1, source_target_pairs={{0,1},{1,0},{2,3},{3,2},{4,5},{5,4},{6,7},{7,6},{8,9},{9,8},{10,11... | collective-permute-start | bytes 1720328 | tf_op jit(solution)/shard_map/ppermute | solution.py:413
  33.3 15.6 %collective-permute-start.3 = (bf16[160,1792]{1,0:T(8,128)(2,1)}, bf16[160,1792]{1,0:T(8,128)(2,1)S(1)}, u32[]{:S(2)}, u32[]{:S(2)}) collective-permute-start(bf16[160,1792]{1,0:T(8,128)(2,1)} %get-tuple-element.54), channel_id=1, source_target_pairs={{0,3},{1,2},{2,1},{3,0},{4,7},{5,6},{6,5},{7,4},{8,11},{9,10},{10,... | collective-permute-start | bytes 1720328 | tf_op jit(solution)/shard_map/ppermute | solution.py:413
  35.6 9.5 %collective-permute-start.1 = (bf16[28,384]{1,0:T(8,128)(2,1)S(1)}, bf16[28,384]{1,0:T(8,128)(2,1)S(1)}, u32[]{:S(2)}, u32[]{:S(2)}) collective-permute-start(bf16[28,384]{1,0:T(8,128)(2,1)S(1)} %bitcast.26), channel_id=1, source_target_pairs={{0,4},{4,0},{1,5},{5,1},{2,6},{6,2},{3,7},{7,3},{8,12},{12,8},{9,1... | collective-permute-start | bytes 64520 | tf_op jit(solution)/shard_map/ppermute | solution.py:395
  48.9 3.4 %collective-permute-start.4 = (bf16[384,1024]{1,0:T(8,128)(2,1)}, bf16[384,1024]{1,0:T(8,128)(2,1)S(1)}, u32[]{:S(2)}, u32[]{:S(2)}) collective-permute-start(bf16[384,1024]{1,0:T(8,128)(2,1)} %bitcast.4), channel_id=1, source_target_pairs={{0,8},{8,0},{1,9},{9,1},{2,10},{10,2},{3,11},{11,3},{4,12},{12,4},... | collective-permute-start | bytes 2359304 | tf_op jit(solution)/shard_map/ppermute | solution.py:391
  48.9 11.8 %collective-permute-start.5 = (bf16[80,2048]{1,0:T(8,128)(2,1)}, bf16[80,2048]{1,0:T(8,128)(2,1)S(1)}, u32[]{:S(2)}, u32[]{:S(2)}) collective-permute-start(bf16[80,2048]{1,0:T(8,128)(2,1)} %copy-done.15), channel_id=1, source_target_pairs={{0,2},{1,3},{2,0},{3,1},{4,6},{5,7},{6,4},{7,5},{8,10},{9,11},{10,... | collective-permute-start | bytes 983048 | tf_op jit(solution)/shard_map/ppermute | solution.py:413
  60.7 16.4 %copy-start = (bf16[80,2048]{1,0:T(8,128)(2,1)}, bf16[80,2048]{1,0:T(8,128)(2,1)S(1)}, u32[]{:S(2)}) copy-start(bf16[80,2048]{1,0:T(8,128)(2,1)S(1)} %collective-permute-done.5.refs_2_) | copy-start | bytes 983044
  76.3 0.9 copy-start.6
  77.1 29.4 %all-to-all-start.2 = ((bf16[16,56,384]{2,1,0:T(8,128)(2,1)}), bf16[16,56,384]{2,1,0:T(8,128)(2,1)S(1)}, u32[]{:S(2)}, u32[]{:S(2)}) async-start(bf16[16,56,384]{2,1,0:T(8,128)(2,1)} %copy-done.6), calls=%async_computation.2 | async-start | bytes 1376256 | tf_op jit(solution)/shard_map/all_to_all | solution.py:387
  84.7 21.8 %collective-permute-start.6 = (bf16[160,1792]{1,0:T(8,128)(2,1)}, bf16[160,1792]{1,0:T(8,128)(2,1)S(1)}, u32[]{:S(2)}, u32[]{:S(2)}) collective-permute-start(bf16[160,1792]{1,0:T(8,128)(2,1)} %copy-done.12), channel_id=1, source_target_pairs={{0,2},{1,3},{2,0},{3,1},{4,6},{5,7},{6,4},{7,5},{8,10},{9,11},{10,... | collective-permute-start | bytes 1720328 | tf_op jit(solution)/shard_map/ppermute | solution.py:413
  85.7 18.5 %collective-permute-start.7 = (bf16[80,2048]{1,0:T(8,128)(2,1)}, bf16[80,2048]{1,0:T(8,128)(2,1)S(1)}, u32[]{:S(2)}, u32[]{:S(2)}) collective-permute-start(bf16[80,2048]{1,0:T(8,128)(2,1)} %copy-done.14), channel_id=1, source_target_pairs={{0,1},{1,0},{2,3},{3,2},{4,5},{5,4},{6,7},{7,6},{8,9},{9,8},{10,11... | collective-permute-start | bytes 983048 | tf_op jit(solution)/shard_map/ppermute | solution.py:413
  86.7 19.0 %collective-permute-start.8 = (bf16[80,2048]{1,0:T(8,128)(2,1)}, bf16[80,2048]{1,0:T(8,128)(2,1)S(1)}, u32[]{:S(2)}, u32[]{:S(2)}) collective-permute-start(bf16[80,2048]{1,0:T(8,128)(2,1)} %copy-done.13), channel_id=1, source_target_pairs={{0,3},{1,2},{2,1},{3,0},{4,7},{5,6},{6,5},{7,4},{8,11},{9,10},{10,... | collective-permute-start | bytes 983048 | tf_op jit(solution)/shard_map/ppermute | solution.py:413
  104.3 0.7 copy-start.2
  105.8 0.7 copy-start.4
  106.5 2.1 %collective-permute-start.9 = (bf16[16,56,384]{2,1,0:T(8,128)(2,1)S(1)}, bf16[16,56,384]{2,1,0:T(8,128)(2,1)S(1)}, u32[]{:S(2)}, u32[]{:S(2)}) collective-permute-start(bf16[16,56,384]{2,1,0:T(8,128)(2,1)S(1)} %all-to-all-done.2.own_ref), channel_id=1, source_target_pairs={{0,8},{8,0},{1,9},{9,1},{2,10},{10,2},{3,11},{11,3},{4,12},{12,4},... | collective-permute-start | bytes 2064392 | tf_op jit(solution)/shard_map/ppermute | solution.py:391
  110.3 21.7 %copy-start.1 = (bf16[80,2048]{1,0:T(8,128)(2,1)S(1)}, bf16[80,2048]{1,0:T(8,128)(2,1)}, u32[]{:S(2)}) copy-start(bf16[80,2048]{1,0:T(8,128)(2,1)} %copy-done) | copy-start | bytes 983044
  110.3 21.7 %copy-start.3 = (bf16[80,2048]{1,0:T(8,128)(2,1)S(1)}, bf16[80,2048]{1,0:T(8,128)(2,1)}, u32[]{:S(2)}) copy-start(bf16[80,2048]{1,0:T(8,128)(2,1)} %copy-done.2) | copy-start | bytes 983044
  110.4 21.7 %copy-start.5 = (bf16[80,2048]{1,0:T(8,128)(2,1)S(1)}, bf16[80,2048]{1,0:T(8,128)(2,1)}, u32[]{:S(2)}) copy-start(bf16[80,2048]{1,0:T(8,128)(2,1)} %copy-done.4) | copy-start | bytes 983044
  132.9 2.4 %collective-permute-start.10 = (bf16[1024,384]{1,0:T(8,128)(2,1)S(1)}, bf16[1024,384]{1,0:T(8,128)(2,1)S(1)}, u32[]{:S(2)}, u32[]{:S(2)}) collective-permute-start(bf16[1024,384]{1,0:T(8,128)(2,1)S(1)} %down.3), channel_id=1, source_target_pairs={{0,8},{8,0},{1,9},{9,1},{2,10},{10,2},{3,11},{11,3},{4,12},{12,4},... | collective-permute-start | bytes 2359304 | tf_op jit(solution)/shard_map/ppermute | solution.py:391

commit v3 on v2

--- a/solution.py
+++ b/solution.py
@@ -19,7 +19,7 @@
 TOKENS = 384
 LAT, KDIM, VDIM = 512, 576, 128
 HALF = HEADS // 2 * VDIM
-CTX, CHUNK = 4096, 512
+CTX, CHUNK = 4096, 1024
 N_CHUNK = CTX // CHUNK
 D, FEAT, PIECE, PAD = 7168, 224, 28, 32
 PAIR = 2 * PIECE
@@ -37,9 +37,10 @@
 VMEM = pl.BlockSpec(memory_space=pltpu.VMEM)
 SMEM = pl.BlockSpec(memory_space=pltpu.SMEM)
 ANY = pl.BlockSpec(memory_space=pl.ANY)
-
-
-def params(mib=40):
+HBM = pl.BlockSpec(memory_space=pltpu.HBM)
+
+
+def params(mib=24):
     return pltpu.CompilerParams(vmem_limit_bytes=mib * 2**20)
 
 
@@ -64,7 +65,6 @@
     w_copy = pltpu.make_async_copy(w_uv_hbm, w_uv, w_sem)
     for copy in copies:
         copy.start()
-    w_copy.start()
 
     dp_index = lax.axis_index(DP)
     q = q_ref[...]
@@ -90,21 +90,29 @@
     fresh_scores = jnp.where(seen, dot(q, fresh, NT) * (SCALE * LOG2E), NEG)
     top = jnp.max(fresh_scores, axis=1, keepdims=True)
 
+    tops = jnp.full((ROWS, 128), NEG, jnp.float32)
     for j in range(N_CHUNK):
         copies[j].wait()
+        if j == 1:
+            w_copy.start()
         slot = j * CHUNK + lax.broadcasted_iota(jnp.int32, (ROWS, CHUNK), 1)
         part = dot(q, keys[j]) * (SCALE * LOG2E)
         part = jnp.where((slot >= low) & (slot < high), part, NEG)
         scores[j] = part
-        top = jnp.maximum(top, jnp.max(part, axis=1, keepdims=True))
-
+        for i in range(0, CHUNK, 128):
+            tops = jnp.maximum(tops, part[:, i : i + 128])
+    top = jnp.maximum(top, jnp.max(tops, axis=1, keepdims=True))
+
+    totals = jnp.zeros((ROWS, 128), jnp.float32)
     weights = jnp.exp2(fresh_scores - top)
     total = jnp.sum(weights, axis=1, keepdims=True)
     mixed = dot(weights.astype(jnp.bfloat16), fresh[:, :LAT])
     for j in range(N_CHUNK):
         weights = jnp.exp2(scores[j] - top)
-        total = total + jnp.sum(weights, axis=1, keepdims=True)
+        for i in range(0, CHUNK, 128):
+            totals = totals + weights[:, i : i + 128]
         mixed = mixed + dot(weights.astype(jnp.bfloat16), keys[j, :LAT, :], NT)
+    total = total + jnp.sum(totals, axis=1, keepdims=True)
     mixed = (mixed / total).astype(jnp.bfloat16)
 
     w_copy.wait()
@@ -112,9 +120,11 @@
     halves = []
     for half in range(2):
         values = []
-        for h in range(half * HEADS // 2, (half + 1) * HEADS // 2):
-            value = jnp.where(head == h, dot(mixed, w_uv[h]), 0.0)
-            values.append(jnp.sum(value.reshape(NEW, HEADS, VDIM), axis=1))
+        for h in range(half * HEADS // 2, (half + 1) * HEADS // 2, 2):
+            pair = dot(mixed, jnp.concatenate([w_uv[h], w_uv[h + 1]], axis=1))
+            for i in range(2):
+                value = jnp.where(head == h + i, pair[:, i * VDIM : (i + 1) * VDIM], 0.0)
+                values.append(jnp.sum(value.reshape(NEW, HEADS, VDIM), axis=1))
         halves.append(jnp.concatenate(values, axis=1))
     second = lax.axis_index("c") == 1
     mine_ref[...] = jnp.where(second, halves[1], halves[0]).astype(jnp.bfloat16)
@@ -164,71 +174,116 @@
     )(mine, theirs)
 
 
-def pick_columns(piece, width):
-    lane = lax.broadcasted_iota(jnp.int32, (1, N_Y * 8 * piece), 1)
-    k, rest = lane // (8 * piece), lane % (8 * piece)
-    side, rest = rest // (4 * piece), rest % (4 * piece)
-    u, rest = rest // (2 * piece), rest % (2 * piece)
-    xh, j = rest // piece, rest % piece
+def pick_columns(ks, width):
+    lanes = len(ks) * 8 * PAD
+    lane = lax.broadcasted_iota(jnp.int32, (1, lanes), 1)
+    n, side, u = lane // (8 * PAD), lane // (4 * PAD) % 2, lane // (2 * PAD) % 2
+    k = jnp.zeros_like(n)
+    for i in range(len(ks)):
+        k = jnp.where(n == i, ks[i], k)
+    xh, j = lane // PAD % 2, lane % PAD
     source = (2 * u + (side ^ lax.axis_index("c"))) * FEAT
     source = source + (xh * N_Y + (k ^ lax.axis_index("y"))) * PIECE + j
     source = jnp.where(j < PIECE, source, -1)
-    rows = lax.broadcasted_iota(jnp.int32, (width, N_Y * 8 * piece), 0)
+    rows = lax.broadcasted_iota(jnp.int32, (width, lanes), 0)
     return jnp.where(rows == source, 1.0, 0.0).astype(jnp.bfloat16)
 
 
-def regroup_kernel(gate_ref, up_ref, down_ref, gain_ref, _, *refs):
-    mix_refs, down_refs, rows = refs[:N_Y], refs[N_Y:-1], refs[-1]
-    gain = gain_ref[...].astype(jnp.float32)
-    for i, ref in enumerate((gate_ref, up_ref)):
+def regroup_kernel(ks, count, gained, *refs):
+    sources, gain_ref, refs = refs[:count], refs[count], refs[count + 2 :]
+    outs, (rows, loaded, moved_ref, in_sems, out_sems) = refs[:-5], refs[-5:]
+    width = 4 * FEAT
+    loads = [
+        pltpu.make_async_copy(source, loaded.at[i], in_sems.at[i])
+        for i, source in enumerate(sources)
+    ]
+    for load in loads:
+        load.start()
+    pick = pick_columns(ks, width)
+    for i in range(count):
+        loads[i].wait()
         rows[i * ROOM + ROOM - 16 : (i + 1) * ROOM, :] = jnp.zeros((16, D), jnp.bfloat16)
-        rows[i * ROOM : i * ROOM + FF, :] = (ref[...].astype(jnp.float32) * gain).astype(jnp.bfloat16)
-    rows[3 * ROOM - 16 : 3 * ROOM, :] = jnp.zeros((16, D), jnp.bfloat16)
-    rows[2 * ROOM : 2 * ROOM + FF, :] = down_ref[...]
-    width = 4 * FEAT
-    for first, last, refs, piece in ((0, 2 * ROOM, mix_refs, PIECE), (2 * ROOM, 3 * ROOM, down_refs, PAD)):
-        pick = pick_columns(piece, width)
-        size = 4 * piece
+        if gained:
+            for j in range(D // 128):
+                lanes = slice(j * 128, (j + 1) * 128)
+                wide = loaded[i, :, lanes].astype(jnp.float32)
+                wide = wide * gain_ref[j : j + 1, :].astype(jnp.float32)
+                rows[i * ROOM : i * ROOM + FF, lanes] = wide.astype(jnp.bfloat16)
+        else:
+            rows[i * ROOM : i * ROOM + FF, :] = loaded[i]
+    stores = []
+    for n in range(len(ks)):
         for m in range(D // width):
-            moved = dot(rows[first:last, m * width : (m + 1) * width], pick).astype(jnp.bfloat16)
-            for k in range(N_Y):
-                for side in range(2):
-                    at, to = (2 * k + side) * size, (side * 8 + m) * size
-                    refs[k][:, to : to + size] = moved[:, at : at + size]
-
-
-def regroup(gate_t, up_t, down, gain, after):
-    return pl.pallas_call(
-        regroup_kernel,
-        out_shape=[shape(2 * ROOM, 2 * SIDE)] * N_Y + [shape(ROOM, 2 * OUT)] * N_Y,
-        in_specs=[VMEM] * 4 + [ANY],
-        out_specs=[VMEM] * (2 * N_Y),
-        scratch_shapes=[pltpu.VMEM((3 * ROOM, D), jnp.bfloat16)],
-        compiler_params=params(),
+            moved = dot(rows[:, m * width : (m + 1) * width], pick[:, n * 256 : (n + 1) * 256])
+            moved = moved.astype(jnp.bfloat16)
+            for side in range(2):
+                to = (side * 8 + m) * 128
+                moved_ref[n, :, to : to + 128] = moved[:, side * 128 : (side + 1) * 128]
+        stores.append(pltpu.make_async_copy(moved_ref.at[n], outs[n], out_sems.at[n]))
+        stores[-1].start()
+    for store in stores:
+        store.wait()
+
+
+def regroup(ks, sources, gain, gained, after):
+    count = len(sources)
+    return pl.pallas_call(
+        functools.partial(regroup_kernel, ks, count, gained),
+        out_shape=[shape(count * ROOM, 2 * OUT)] * len(ks),
+        in_specs=[HBM] * count + [VMEM, ANY],
+        out_specs=[HBM] * len(ks),
+        scratch_shapes=[
+            pltpu.VMEM((count * ROOM, D), jnp.bfloat16),
+            pltpu.VMEM((count, FF, D), jnp.bfloat16),
+            pltpu.VMEM((len(ks), count * ROOM, 2 * OUT), jnp.bfloat16),
+            pltpu.SemaphoreType.DMA((count,)),
+            pltpu.SemaphoreType.DMA((len(ks),)),
+        ],
+        compiler_params=params(58),
         cost_estimate=pl.CostEstimate(
-            flops=2 * 3 * ROOM * D * 1024, bytes_accessed=7 * 2**20, transcendentals=0
+            flops=2 * count * ROOM * D * 256 * len(ks), bytes_accessed=5 * 2**20, transcendentals=0
         ),
         name="regroup",
-    )(gate_t, up_t, down, gain, after)
-
-
-def project_kernel(first_ref, heads_ref, w_ref, out_ref):
+    )(*sources, gain, after)
+
+
+def project_own_kernel(heads_ref, w_ref, out_ref):
+    lanes = pl.ds(pl.multiple_of(lax.axis_index("c") * HALF, HALF), HALF)
+    out_ref[...] = dot(w_ref[:, lanes], heads_ref[...], NT)
+
+
+def project_more_kernel(first_ref, heads_ref, w_ref, out_ref):
     lanes = pl.ds(pl.multiple_of((1 - lax.axis_index("c")) * HALF, HALF), HALF)
     total = first_ref[...] + dot(w_ref[:, lanes], heads_ref[...], NT)
-    total = total.astype(jnp.bfloat16)
-    out_ref[0] = total
-    out_ref[1] = total
-
-
-def project(first, heads, w_ot):
-    return pl.pallas_call(
-        project_kernel,
-        out_shape=shape(2, FEAT, TOKENS),
-        in_specs=[VMEM, VMEM, VMEM],
+    pieces = [total[t * PIECE : (t + 1) * PIECE] for t in range(N_TP)]
+    for y in range(N_Y):
+        pair = jnp.concatenate([pieces[y], pieces[N_Y + y]], axis=0).astype(jnp.bfloat16)
+        out_ref[y] = pair
+        out_ref[N_Y + y] = pair
+
+
+def project(heads, more_heads, w_ot):
+    cost = pl.CostEstimate(
+        flops=2 * FEAT * HALF * TOKENS, bytes_accessed=2 * 2**20, transcendentals=0
+    )
+    first = pl.pallas_call(
+        project_own_kernel,
+        out_shape=shape(FEAT, TOKENS, dtype=jnp.float32),
+        in_specs=[VMEM] * 2,
         out_specs=VMEM,
         compiler_params=params(),
-        name="project",
-    )(first, heads, w_ot)
+        cost_estimate=cost,
+        name="project_own",
+    )(heads, w_ot)
+    return pl.pallas_call(
+        project_more_kernel,
+        out_shape=shape(N_TP, PAIR, TOKENS),
+        in_specs=[VMEM] * 3,
+        out_specs=VMEM,
+        compiler_params=params(),
+        cost_estimate=cost,
+        name="project_more",
+    )(first, more_heads, w_ot)
 
 
 def update_kernel(parts_ref, residual_ref, updated_ref, out_ref):
@@ -250,21 +305,23 @@
     )(parts, residual)
 
 
-def squares_of(ref):
-    wide = ref[...].astype(jnp.float32)
-    return jnp.sum(wide * wide, axis=(0, 1))[None]
+def spaced(ref):
+    wide = ref[...].astype(jnp.float32).reshape(SIDE, TOKENS)
+    squares = jnp.sum(wide * wide, axis=0, keepdims=True)
+    wide = jnp.concatenate([wide, jnp.zeros((8, TOKENS), jnp.float32)], axis=0)
+    pieces = [wide[i * PIECE : i * PIECE + PAD] for i in range(SIDE // PIECE)]
+    return jnp.concatenate(pieces, axis=0).astype(jnp.bfloat16), squares
 
 
 def mix_own_kernel(own_ref, *refs):
     blocks, (out_ref, squares_ref, held, sems) = refs[:N_Y], refs[N_Y:]
     copies = [
-        pltpu.make_async_copy(blocks[k].at[:, pl.ds(0, SIDE)], held.at[k], sems.at[k])
+        pltpu.make_async_copy(blocks[k].at[:, pl.ds(0, OUT)], held.at[k], sems.at[k])
         for k in range(N_Y)
     ]
     for copy in copies:
         copy.start()
-    squares_ref[...] = squares_of(own_ref)
-    own = own_ref[...].reshape(SIDE, TOKENS)
+    own, squares_ref[...] = spaced(own_ref)
     for k in range(N_Y):
         copies[k].wait()
         out_ref[k] = dot(held[k], own)
@@ -273,13 +330,13 @@
 def mix_more_kernel(part_ref, squares_ref, more_ref, *refs):
     blocks, (out_ref, held, sems) = refs[:N_Y], refs[N_Y:]
     copies = [
-        pltpu.make_async_copy(blocks[k].at[:, pl.ds(SIDE, SIDE)], held.at[k], sems.at[k])
+        pltpu.make_async_copy(blocks[k].at[:, pl.ds(OUT, OUT)], held.at[k], sems.at[k])
         for k in range(N_Y)
     ]
     for copy in copies:
         copy.start()
-    squares = squares_ref[...] + squares_of(more_ref)
-    more = more_ref[...].reshape(SIDE, TOKENS)
+    more, squares = spaced(more_ref)
+    squares = squares_ref[...] + squares
     high = squares.astype(jnp.bfloat16).astype(jnp.float32)
     row = lax.broadcasted_iota(jnp.int32, (2 * ROOM, TOKENS), 0)
     y = lax.axis_index("y")
@@ -292,11 +349,11 @@
 
 def mix(own, more, blocks):
     scratch = [
-        pltpu.VMEM((N_Y, 2 * ROOM, SIDE), jnp.bfloat16),
+        pltpu.VMEM((N_Y, 2 * ROOM, OUT), jnp.bfloat16),
         pltpu.SemaphoreType.DMA((N_Y,)),
     ]
     cost = pl.CostEstimate(
-        flops=2 * N_Y * 2 * ROOM * SIDE * TOKENS, bytes_accessed=4 * 2**20, transcendentals=0
+        flops=2 * N_Y * 2 * ROOM * OUT * TOKENS, bytes_accessed=4 * 2**20, transcendentals=0
     )
     part, squares = pl.pallas_call(
         mix_own_kernel,
@@ -398,45 +455,41 @@
 def body(
     queries, new_latent, cache, cache_lengths, w_uv, w_o, residual, norm_gain, w_gate, w_up, w_down
 ):
-    core, xh = lax.axis_index("c"), lax.axis_index("xh")
-
-    fresh = jnp.transpose(new_latent, (1, 0, 2))
+    xh = lax.axis_index("xh")
+
     mine, theirs = attend(
-        cache_lengths.T, queries.reshape(ROWS, KDIM), fresh, cache.T, w_uv
-    )
-
-    blocks = regroup(w_gate.T, w_up.T, w_down, norm_gain[None], mine)
-    mix_blocks, down_blocks = list(blocks[:N_Y]), list(blocks[N_Y:])
-
-    def exchange(blocks, which):
-        for k in which:
-            blocks[k] = lax.ppermute(blocks[k], "y", [(i, i ^ k) for i in range(N_Y)])
-
-    def fence(*x):
-        out = lax.optimization_barrier((*x, *mix_blocks, *down_blocks))
-        mix_blocks[:], down_blocks[:] = out[-2 * N_Y : -N_Y], out[-N_Y:]
-        return out[: -2 * N_Y]
+        cache_lengths.T, queries.reshape(ROWS, KDIM), jnp.transpose(new_latent, (1, 0, 2)), cache.T,
+        w_uv,
+    )
+
+    def exchange(block, k):
+        return lax.ppermute(block, "y", [(i, i ^ k) for i in range(N_Y)])
+
+    gain = norm_gain.reshape(D // 128, 128)
+    sources = (w_gate.T, w_up.T)
+    mix_1, mix_3 = regroup((1, 3), sources, gain, True, mine)
+    mix_2, mix_0 = regroup((2, 0), sources, gain, True, mix_1)
+
+    heads = swap(fan(mine, other_core(theirs)), RING).reshape(TOKENS, HALF)
+    heads, mix_1, mix_3, mix_0 = lax.optimization_barrier(
+        (heads, exchange(mix_1, 1), exchange(mix_3, 3), mix_0)
+    )
+    partial = project(heads, other_core(heads), w_o.T)
 
     partner = other_half(residual.T)
     residual = jnp.concatenate(
         [jnp.where(xh == 0, residual.T, partner), jnp.where(xh == 0, partner, residual.T)], axis=0
     )
-    w_ot = w_o.T.reshape(2, N_Y, PIECE, HEADS * VDIM).transpose(1, 0, 2, 3)
-    w_ot = w_ot.reshape(FEAT, HEADS * VDIM)
-    w_own = lax.dynamic_slice_in_dim(w_ot, core * HALF, HALF, 1)
-
-    heads = swap(fan(mine, other_core(theirs)), RING).reshape(TOKENS, HALF)
-    exchange(mix_blocks, (1, 3))
-    heads, residual, w_ot, w_own = fence(heads, residual, w_ot, w_own)
-    more_heads = other_core(heads)
-    first = dot(w_own, heads, NT)
-    exchange(down_blocks, (2,))
-    (partial,) = fence(project(first, more_heads, w_ot))
-
-    updated, block = update(swap(partial.reshape(N_TP, PAIR, TOKENS), TP), residual)
-    exchange(mix_blocks, (2,))
-    exchange(down_blocks, (1, 3))
-    (own,) = fence(swap(block, RING))
+    down_blocks = regroup((1, 3, 2, 0), (w_down,), gain, False, partial)
+    updated, block = update(swap(partial, TP), residual)
+    block, mix_2, *down_blocks = lax.optimization_barrier(
+        (block, exchange(mix_2, 2), *down_blocks)
+    )
+    down_1, down_3, down_2, down_0 = down_blocks
+    own, down_1, down_2, down_3 = lax.optimization_barrier(
+        (swap(block, RING), exchange(down_1, 1), exchange(down_2, 2), exchange(down_3, 3))
+    )
+    mix_blocks, down_blocks = (mix_0, mix_1, mix_2, mix_3), (down_0, down_1, down_2, down_3)
     hidden = gate(swap(mix(own, other_core(own), mix_blocks), "y"))
     hidden = swap(hidden, "y")
     more = other_core(down(1, hidden, down_blocks))

time: 169 us -> 159 us (0.941)
  blocking collectives: 68.9 us -> 54.1 us
  local copies, waits for them, and re-layouts: 13 us -> 2.34 us
  Pallas kernels: 22.4 us -> 31.5 us
  waiting for transfers between devices: 31.2 us -> 35.6 us
  starting transfers between devices: 29.7 us -> 33.5 us
  matrix products: 1.72 us -> 0 us
    all_to_all x4 -> x3, blocking collectives: 68.9 us -> 54.1 us  [swap(): return lax.all_to_all(x, axes, 0, 0, tiled=True)]
    pallas_call x2 -> x5, Pallas kernels: 7.2 us -> 17.7 us  [the longest x3 14.9 us: regroup(): pl.pallas_call(functools.partial(regroup_kernel, ks, count, gained), out_...]
    all_to_all x2 -> x3, waiting for transfers between devices: 0.01 us -> 6.46 us  [swap(): return lax.all_to_all(x, axes, 0, 0, tiled=True)]
    all_to_all x2 -> x3, starting transfers between devices: 17 us -> 22 us  [swap(): return lax.all_to_all(x, axes, 0, 0, tiled=True)]
    unnamed x36 -> x16, local copies, waits for them, and re-layouts: 6.29 us -> 2.34 us
    reshape x2 -> x0, local copies, waits for them, and re-layouts: 3.59 us -> none  [the longest x1 2.22 us: body(): w_ot = w_o.T.reshape(2, N_Y, PIECE, HEADS * VDIM).transpose(1, 0, 2, 3)]
    transpose x1 -> x0, local copies, waits for them, and re-layouts: 2.3 us -> none  [body(): w_ot = w_o.T.reshape(2, N_Y, PIECE, HEADS * VDIM).transpose(1, 0, 2, 3)]
    ppermute x6, waiting for transfers between devices: 28 us -> 25.9 us  [exchange(): return lax.ppermute(block, 'y', [(i, i ^ k) for i in range(N_Y)])]
  transfers between devices with their start and end apart: 13 -> 14, of which waited for: 8 -> 9; matrix products, arithmetic and copies ran while one was open for 5% -> 0% of each run, Pallas kernels for 6% -> 13%
where the time goes in v3:
time: 159 us; the launch traced here: 158 us
  blocking collectives  54.1 us (34%)
  waiting for transfers between devices  35.6 us (22%)
  starting transfers between devices  33.5 us (21%)
  Pallas kernels  31.5 us (20%)
  local copies, waits for them, and re-layouts  2.34 us (1%)
    all_to_all x3, blocking collectives, swap(): return lax.all_to_all(x, axes, 0, 0, tiled=True)  54.1 us
    ppermute x6, waiting for transfers between devices, exchange(): return lax.ppermute(block, 'y', [(i, i ^ k) for i in range(N_Y)])  25.9 us
    all_to_all x3, starting transfers between devices, swap(): return lax.all_to_all(x, axes, 0, 0, tiled=True)  22 us
    pallas_call x3, Pallas kernels, regroup(): pl.pallas_call(functools.partial(regroup_kernel, ks, count, gained), out_...  14.9 us
    ppermute x6, starting transfers between devices, exchange(): return lax.ppermute(block, 'y', [(i, i ^ k) for i in range(N_Y)])  8.58 us
    pallas_call x1, Pallas kernels, attend(): pl.pallas_call(attend_kernel, out_shape=(shape(NEW, HALF), shape(NEW, HAL...  7.5 us
    all_to_all x3, waiting for transfers between devices, swap(): return lax.all_to_all(x, axes, 0, 0, tiled=True)  6.46 us
    ppermute x4, waiting for transfers between devices, other_core(): return lax.ppermute(x, 'c', [(0, 1), (1, 0)])  3.2 us
  transfers between devices with their start and end apart: 14, of which 9 were waited for; matrix products, arithmetic and copies ran while one was open for 0% of the time, Pallas kernels for 13%

profile of v3, /device:TPU:32, one launch (start us, length us, event | category | flops | bytes accessed | tf_op | source)
XLA Modules:
  0.0 158.2 jit_solution(495441339646193906)
XLA Ops:
  0.0 7.5 %attend.1 = (bf16[12,1024]{1,0:T(8,128)(2,1)}, bf16[12,1024]{1,0:T(8,128)(2,1)}) custom-call(s32[4,32]{1,0:T(4,128)} %bitcast.24, bf16[192,576]{1,0:T(8,128)(2,1)} %bitcast.21, bf16[3,4,576]{2,1,0:T(4,128)(2,1)} %bitcast.23, bf16[576,4096]{1,0:T(8,128)(2,1)} %bitcast.19, bf16[16,512,128]{2,1,0:T(8,128)(2,1)} %w_uv_hbm.1), custom_call_target="tpu_custom_call" | custom-call | flops 1711276032 | bytes 7340032 | tf_op jit(solution)/shard_map/attend/pallas_call | solution.py:135
  7.5 0.1 collective-permute-start
  7.6 1.4 collective-permute-done.theirs_ref
  9.0 0.8 copy-done.6
  9.8 1.0 fan.1
  10.7 9.5 %all-to-all-start = ((bf16[16,24,1024]{2,1,0:T(8,128)(2,1)}), bf16[16,24,1024]{2,1,0:T(8,128)(2,1)S(1)}, u32[]{:S(2)}, u32[]{:S(2)}) async-start(bf16[16,24,1024]{2,1,0:T(8,128)(2,1)} %fan.1), calls=%async_computation | async-start | bytes 1572864 | tf_op jit(solution)/shard_map/all_to_all | solution.py:444
  20.3 4.7 %regroup.3 = (bf16[160,2048]{1,0:T(8,128)(2,1)}, bf16[160,2048]{1,0:T(8,128)(2,1)}) custom-call(bf16[72,7168]{1,0:T(8,128)(2,1)} %bitcast.25, bf16[72,7168]{1,0:T(8,128)(2,1)} %bitcast.27, bf16[56,128]{1,0:T(8,128)(2,1)} %bitcast.29, bf16[12,1024]{1,0:T(8,128)(2,1)} %get-tuple-element.33.mine_ref.refs_3_), custom_call_target="tpu_custom_call" | custom-call | flops 1174405120 | bytes 5242880 | tf_op jit(solution)/shard_map/regroup/pallas_call | solution.py:230
  24.9 3.1 %collective-permute-start.2 = (bf16[160,2048]{1,0:T(8,128)(2,1)}, bf16[160,2048]{1,0:T(8,128)(2,1)S(1)}, u32[]{:S(2)}, u32[]{:S(2)}) collective-permute-start(bf16[160,2048]{1,0:T(8,128)(2,1)} %get-tuple-element.36), channel_id=1, source_target_pairs={{0,3},{1,2},{2,1},{3,0},{4,7},{5,6},{6,5},{7,4},{8,11},{9,10},{10,... | collective-permute-start | bytes 1966088 | tf_op jit(solution)/shard_map/ppermute | solution.py:466
  28.0 0.1 collective-permute-start.1
  28.2 4.8 %regroup.4 = (bf16[160,2048]{1,0:T(8,128)(2,1)}, bf16[160,2048]{1,0:T(8,128)(2,1)}) custom-call(bf16[72,7168]{1,0:T(8,128)(2,1)} %bitcast.26, bf16[72,7168]{1,0:T(8,128)(2,1)} %bitcast.28, bf16[56,128]{1,0:T(8,128)(2,1)} %bitcast.30, bf16[160,2048]{1,0:T(8,128)(2,1)} %get-tuple-element.35.refs_3_), custom_call_target="tpu_custom_call" | custom-call | flops 1174405120 | bytes 5242880 | tf_op jit(solution)/shard_map/regroup/pallas_call | solution.py:230
  32.9 9.8 %collective-permute-done.2.refs_3_ = bf16[160,2048]{1,0:T(8,128)(2,1)S(1)} collective-permute-done((bf16[160,2048]{1,0:T(8,128)(2,1)}, bf16[160,2048]{1,0:T(8,128)(2,1)S(1)}, u32[]{:S(2)}, u32[]{:S(2)}) %collective-permute-start.2) | collective-permute-done | bytes 655392 | tf_op jit(solution)/shard_map/ppermute | solution.py:466
  42.8 1.5 collective-permute-done.1.refs_1_
  44.2 0.0 all-to-all-done
  44.2 0.0 collective-permute-start.3
  44.2 0.7 collective-permute-start.5
  44.9 2.7 %collective-permute-start.4 = (bf16[28,384]{1,0:T(8,128)(2,1)S(1)}, bf16[28,384]{1,0:T(8,128)(2,1)S(1)}, u32[]{:S(2)}, u32[]{:S(2)}) collective-permute-start(bf16[28,384]{1,0:T(8,128)(2,1)S(1)} %bitcast.22), channel_id=1, source_target_pairs={{0,4},{4,0},{1,5},{5,1},{2,6},{6,2},{3,7},{7,3},{8,12},{12,8},{9,1... | collective-permute-start | bytes 64520 | tf_op jit(solution)/shard_map/ppermute | solution.py:452
  47.6 0.4 project_own.1.first_ref
  48.1 2.3 %project_more.1.refs_2_ = bf16[8,56,384]{2,1,0:T(8,128)(2,1)} custom-call(f32[224,384]{1,0:T(8,128)S(1)} %project_own.1.first_ref, bf16[384,1024]{1,0:T(8,128)(2,1)} %collective-permute-done.3.heads_ref, bf16[224,2048]{1,0:T(8,128)(2,1)S(1)} %bitcast.16), custom_call_target="tpu_custom_call" | custom-call | flops 176160768 | bytes 2097152 | tf_op jit(solution)/shard_map/project_more/pallas_call | solution.py:278
  50.4 4.4 %all-to-all-start.1 = ((bf16[8,56,384]{2,1,0:T(8,128)(2,1)}), bf16[8,56,384]{2,1,0:T(8,128)(2,1)S(1)}, u32[]{:S(2)}, u32[]{:S(2)}) async-start(bf16[8,56,384]{2,1,0:T(8,128)(2,1)} %project_more.1.refs_2_), calls=%async_computation.1 | async-start | bytes 688128 | tf_op jit(solution)/shard_map/all_to_all | solution.py:444
  54.8 5.5 %regroup.5 = (bf16[80,2048]{1,0:T(8,128)(2,1)}, bf16[80,2048]{1,0:T(8,128)(2,1)}, bf16[80,2048]{1,0:T(8,128)(2,1)}, bf16[80,2048]{1,0:T(8,128)(2,1)}) custom-call(bf16[72,7168]{1,0:T(8,128)(2,1)} %refs_0_.1, bf16[56,128]{1,0:T(8,128)(2,1)} %bitcast.31, bf16[8,56,384]{2,1,0:T(8,128)(2,1)} %project_more.1.refs_2_), custom_call_target="tpu_custom_call" | custom-call | flops 1174405120 | bytes 5242880 | tf_op jit(solution)/shard_map/regroup/pallas_call | solution.py:230
  60.3 6.5 %all-to-all-done.1.parts_ref = bf16[8,56,384]{2,1,0:T(8,128)(2,1)S(1)} async-done(((bf16[8,56,384]{2,1,0:T(8,128)(2,1)}), bf16[8,56,384]{2,1,0:T(8,128)(2,1)S(1)}, u32[]{:S(2)}, u32[]{:S(2)}) %all-to-all-start.1) | async-done | bytes 344096 | tf_op jit(solution)/shard_map/all_to_all | solution.py:444
  66.8 0.1 update.1
  66.9 0.8 copy-done.5
  67.7 0.0 collective-permute-done.5.refs_2_
  67.7 8.1 %all-to-all-start.2 = ((bf16[16,56,384]{2,1,0:T(8,128)(2,1)}), bf16[16,56,384]{2,1,0:T(8,128)(2,1)S(1)}, u32[]{:S(2)}, u32[]{:S(2)}) async-start(bf16[16,56,384]{2,1,0:T(8,128)(2,1)} %copy-done.5), calls=%async_computation.2 | async-start | bytes 1376256 | tf_op jit(solution)/shard_map/all_to_all | solution.py:444
  75.8 0.3 collective-permute-start.6
  76.2 2.7 %collective-permute-start.7 = (bf16[80,2048]{1,0:T(8,128)(2,1)}, bf16[80,2048]{1,0:T(8,128)(2,1)S(1)}, u32[]{:S(2)}, u32[]{:S(2)}) collective-permute-start(bf16[80,2048]{1,0:T(8,128)(2,1)} %get-tuple-element.48), channel_id=1, source_target_pairs={{0,2},{1,3},{2,0},{3,1},{4,6},{5,7},{6,4},{7,5},{8,10},{9,11},{10,... | collective-permute-start | bytes 983048 | tf_op jit(solution)/shard_map/ppermute | solution.py:466
  78.8 1.7 %collective-permute-start.8 = (bf16[80,2048]{1,0:T(8,128)(2,1)}, bf16[80,2048]{1,0:T(8,128)(2,1)S(1)}, u32[]{:S(2)}, u32[]{:S(2)}) collective-permute-start(bf16[80,2048]{1,0:T(8,128)(2,1)} %get-tuple-element.49), channel_id=1, source_target_pairs={{0,3},{1,2},{2,1},{3,0},{4,7},{5,6},{6,5},{7,4},{8,11},{9,10},{10,... | collective-permute-start | bytes 983048 | tf_op jit(solution)/shard_map/ppermute | solution.py:466
  80.5 6.2 %collective-permute-done.6.refs_1_ = bf16[80,2048]{1,0:T(8,128)(2,1)S(1)} collective-permute-done((bf16[80,2048]{1,0:T(8,128)(2,1)}, bf16[80,2048]{1,0:T(8,128)(2,1)S(1)}, u32[]{:S(2)}, u32[]{:S(2)}) %collective-permute-start.6) | collective-permute-done | bytes 327712 | tf_op jit(solution)/shard_map/ppermute | solution.py:466
  86.7 5.9 %collective-permute-done.7.refs_2_ = bf16[80,2048]{1,0:T(8,128)(2,1)S(1)} collective-permute-done((bf16[80,2048]{1,0:T(8,128)(2,1)}, bf16[80,2048]{1,0:T(8,128)(2,1)S(1)}, u32[]{:S(2)}, u32[]{:S(2)}) %collective-permute-start.7) | collective-permute-done | bytes 327712 | tf_op jit(solution)/shard_map/ppermute | solution.py:466
  92.6 2.6 %collective-permute-done.8.refs_3_ = bf16[80,2048]{1,0:T(8,128)(2,1)S(1)} collective-permute-done((bf16[80,2048]{1,0:T(8,128)(2,1)}, bf16[80,2048]{1,0:T(8,128)(2,1)S(1)}, u32[]{:S(2)}, u32[]{:S(2)}) %collective-permute-start.8) | collective-permute-done | bytes 327712 | tf_op jit(solution)/shard_map/ppermute | solution.py:466
  95.2 0.7 copy-done.3
  95.9 0.0 all-to-all-done.2.own_ref
  95.9 0.0 collective-permute-start.9
  95.9 1.7 %mix_own.1 = (f32[4,160,384]{2,1,0:T(8,128)S(1)}, f32[1,384]{1,0:T(1,128)S(1)}) custom-call(bf16[16,56,384]{2,1,0:T(8,128)(2,1)S(1)} %all-to-all-done.2.own_ref, bf16[160,2048]{1,0:T(8,128)(2,1)S(1)} %copy-done.1, bf16[160,2048]{1,0:T(8,128)(2,1)S(1)} %collective-permute-done.1.refs_1_, bf16[160,2048]{1,0:T(8,128)(2,1)} %collective-permute-done.5.refs_2_, ...), custom_call_target="tpu_custom_call" | custom-call | flops 503316480 | bytes 4194304 | tf_op jit(solution)/shard_map/mix_own/pallas_call | solution.py:358
  97.6 0.4 collective-permute-done.9.more_ref
  98.0 1.7 %mix_more.1 = bf16[4,160,384]{2,1,0:T(8,128)(2,1)S(1)} custom-call(f32[4,160,384]{2,1,0:T(8,128)S(1)} %get-tuple-element.55.part_ref, f32[1,384]{1,0:T(1,128)S(1)} %get-tuple-element.56.squares_ref, bf16[16,56,384]{2,1,0:T(8,128)(2,1)S(1)} %collective-permute-done.9.more_ref, bf16[160,2048]{1,0:T(8,128)(2,1)S(1)} %copy-done.1, ...), custom_call_target="tpu_custom_call" | custom-call | flops 503316480 | bytes 4194304 | tf_op jit(solution)/shard_map/mix_more/pallas_call | solution.py:371
  99.8 12.9 %all_to_all.30.parts_ref = bf16[4,160,384]{2,1,0:T(8,128)(2,1)S(1)} all-to-all(bf16[4,160,384]{2,1,0:T(8,128)(2,1)S(1)} %mix_more.1), channel_id=1, replica_groups=mesh['xl'=2,'z'=8,'c'=2,'xh'=2,'y'=4] {'y'}, dimensions={0} | all-to-all | bytes 983040 | tf_op jit(solution)/shard_map/all_to_all | solution.py:444
  112.8 0.1 gate.1
  112.9 9.0 %all_to_all.31.hidden_ref = bf16[4,80,384]{2,1,0:T(8,128)(2,1)S(1)} all-to-all(bf16[4,80,384]{2,1,0:T(8,128)(2,1)S(1)} %gate.1), channel_id=1, replica_groups=mesh['xl'=2,'z'=8,'c'=2,'xh'=2,'y'=4] {'y'}, dimensions={0} | all-to-all | bytes 491520 | tf_op jit(solution)/shard_map/all_to_all | solution.py:444
  121.8 0.9 down.3
  122.7 0.1 collective-permute-start.10
  122.8 0.9 down.2
  123.7 1.4 collective-permute-done.10
  125.1 0.2 add_convert_fusion
  125.2 32.2 %all_to_all.32 = bf16[32,32,384]{2,1,0:T(8,128)(2,1)S(1)} all-to-all(bf16[32,32,384]{2,1,0:T(8,128)(2,1)S(1)} %bitcast.20), channel_id=1, replica_groups=mesh['xl'=2,'z'=8,'c'=2,'xh'=2,'y'=4] {'xl','z','xh'}, dimensions={0} | all-to-all | bytes 1572864 | tf_op jit(solution)/shard_map/all_to_all | solution.py:444
  157.5 0.1 convert_reduce_fusion
  157.6 0.6 fusion.1
  (17 shorter events, 0.1 us)
Async XLA Ops:
  7.5 1.5 collective-permute-start
  9.0 0.8 copy-start.6
  10.7 33.5 %all-to-all-start = ((bf16[16,24,1024]{2,1,0:T(8,128)(2,1)}), bf16[16,24,1024]{2,1,0:T(8,128)(2,1)S(1)}, u32[]{:S(2)}, u32[]{:S(2)}) async-start(bf16[16,24,1024]{2,1,0:T(8,128)(2,1)} %fan.1), calls=%async_computation | async-start | bytes 1572864 | tf_op jit(solution)/shard_map/all_to_all | solution.py:444
  24.9 17.8 %collective-permute-start.2 = (bf16[160,2048]{1,0:T(8,128)(2,1)}, bf16[160,2048]{1,0:T(8,128)(2,1)S(1)}, u32[]{:S(2)}, u32[]{:S(2)}) collective-permute-start(bf16[160,2048]{1,0:T(8,128)(2,1)} %get-tuple-element.36), channel_id=1, source_target_pairs={{0,3},{1,2},{2,1},{3,0},{4,7},{5,6},{6,5},{7,4},{8,11},{9,10},{10,... | collective-permute-start | bytes 1966088 | tf_op jit(solution)/shard_map/ppermute | solution.py:466
  28.0 16.8 %copy-start.7 = (bf16[384,28]{0,1:T(8,128)(2,1)S(1)}, bf16[384,28]{0,1:T(8,128)(2,1)}, u32[]{:S(2)}) copy-start(bf16[384,28]{0,1:T(8,128)(2,1)} %param.17) | copy-start | bytes 64516
  28.0 19.6 %copy-start = (bf16[2048,224]{0,1:T(8,128)(2,1)S(1)}, bf16[2048,224]{0,1:T(8,128)(2,1)}, u32[]{:S(2)}) copy-start(bf16[2048,224]{0,1:T(8,128)(2,1)} %param.16) | copy-start | bytes 2752516
  28.0 16.2 %collective-permute-start.1 = (bf16[160,2048]{1,0:T(8,128)(2,1)}, bf16[160,2048]{1,0:T(8,128)(2,1)S(1)}, u32[]{:S(2)}, u32[]{:S(2)}) collective-permute-start(bf16[160,2048]{1,0:T(8,128)(2,1)} %get-tuple-element.35.refs_3_), channel_id=1, source_target_pairs={{0,1},{1,0},{2,3},{3,2},{4,5},{5,4},{6,7},{7,6},{8,9},{9,8},{10,11... | collective-permute-start | bytes 1966088 | tf_op jit(solution)/shard_map/ppermute | solution.py:466
  44.2 3.8 %collective-permute-start.3 = (bf16[384,1024]{1,0:T(8,128)(2,1)S(1)}, bf16[384,1024]{1,0:T(8,128)(2,1)}, u32[]{:S(2)}, u32[]{:S(2)}) collective-permute-start(bf16[384,1024]{1,0:T(8,128)(2,1)S(1)} %bitcast.17), channel_id=1, source_target_pairs={{0,8},{8,0},{1,9},{9,1},{2,10},{10,2},{3,11},{11,3},{4,12},{12,4},... | collective-permute-start | bytes 2359304 | tf_op jit(solution)/shard_map/ppermute | solution.py:448
  44.2 23.5 %collective-permute-start.5 = (bf16[160,2048]{1,0:T(8,128)(2,1)}, bf16[160,2048]{1,0:T(8,128)(2,1)}, u32[]{:S(2)}, u32[]{:S(2)}) collective-permute-start(bf16[160,2048]{1,0:T(8,128)(2,1)} %get-tuple-element.41), channel_id=1, source_target_pairs={{0,2},{1,3},{2,0},{3,1},{4,6},{5,7},{6,4},{7,5},{8,10},{9,11},{10,... | collective-permute-start | bytes 1966088 | tf_op jit(solution)/shard_map/ppermute | solution.py:466
  44.9 9.9 %collective-permute-start.4 = (bf16[28,384]{1,0:T(8,128)(2,1)S(1)}, bf16[28,384]{1,0:T(8,128)(2,1)S(1)}, u32[]{:S(2)}, u32[]{:S(2)}) collective-permute-start(bf16[28,384]{1,0:T(8,128)(2,1)S(1)} %bitcast.22), channel_id=1, source_target_pairs={{0,4},{4,0},{1,5},{5,1},{2,6},{6,2},{3,7},{7,3},{8,12},{12,8},{9,1... | collective-permute-start | bytes 64520 | tf_op jit(solution)/shard_map/ppermute | solution.py:452
  50.4 16.4 %all-to-all-start.1 = ((bf16[8,56,384]{2,1,0:T(8,128)(2,1)}), bf16[8,56,384]{2,1,0:T(8,128)(2,1)S(1)}, u32[]{:S(2)}, u32[]{:S(2)}) async-start(bf16[8,56,384]{2,1,0:T(8,128)(2,1)} %project_more.1.refs_2_), calls=%async_computation.1 | async-start | bytes 688128 | tf_op jit(solution)/shard_map/all_to_all | solution.py:444
  60.3 35.6 %copy-start.1 = (bf16[160,2048]{1,0:T(8,128)(2,1)S(1)}, bf16[160,2048]{1,0:T(8,128)(2,1)}, u32[]{:S(2)}) copy-start(bf16[160,2048]{1,0:T(8,128)(2,1)} %get-tuple-element.51.refs_0_) | copy-start | bytes 1966084
  66.9 0.9 copy-start.5
  67.7 28.2 %all-to-all-start.2 = ((bf16[16,56,384]{2,1,0:T(8,128)(2,1)}), bf16[16,56,384]{2,1,0:T(8,128)(2,1)S(1)}, u32[]{:S(2)}, u32[]{:S(2)}) async-start(bf16[16,56,384]{2,1,0:T(8,128)(2,1)} %copy-done.5), calls=%async_computation.2 | async-start | bytes 1376256 | tf_op jit(solution)/shard_map/all_to_all | solution.py:444
  75.8 10.9 %collective-permute-start.6 = (bf16[80,2048]{1,0:T(8,128)(2,1)}, bf16[80,2048]{1,0:T(8,128)(2,1)S(1)}, u32[]{:S(2)}, u32[]{:S(2)}) collective-permute-start(bf16[80,2048]{1,0:T(8,128)(2,1)} %get-tuple-element.47), channel_id=1, source_target_pairs={{0,1},{1,0},{2,3},{3,2},{4,5},{5,4},{6,7},{7,6},{8,9},{9,8},{10,11... | collective-permute-start | bytes 983048 | tf_op jit(solution)/shard_map/ppermute | solution.py:466
  76.2 16.4 %collective-permute-start.7 = (bf16[80,2048]{1,0:T(8,128)(2,1)}, bf16[80,2048]{1,0:T(8,128)(2,1)S(1)}, u32[]{:S(2)}, u32[]{:S(2)}) collective-permute-start(bf16[80,2048]{1,0:T(8,128)(2,1)} %get-tuple-element.48), channel_id=1, source_target_pairs={{0,2},{1,3},{2,0},{3,1},{4,6},{5,7},{6,4},{7,5},{8,10},{9,11},{10,... | collective-permute-start | bytes 983048 | tf_op jit(solution)/shard_map/ppermute | solution.py:466
  78.8 16.3 %collective-permute-start.8 = (bf16[80,2048]{1,0:T(8,128)(2,1)}, bf16[80,2048]{1,0:T(8,128)(2,1)S(1)}, u32[]{:S(2)}, u32[]{:S(2)}) collective-permute-start(bf16[80,2048]{1,0:T(8,128)(2,1)} %get-tuple-element.49), channel_id=1, source_target_pairs={{0,3},{1,2},{2,1},{3,0},{4,7},{5,6},{6,5},{7,4},{8,11},{9,10},{10,... | collective-permute-start | bytes 983048 | tf_op jit(solution)/shard_map/ppermute | solution.py:466
  95.2 0.7 copy-start.3
  95.9 2.1 %collective-permute-start.9 = (bf16[16,56,384]{2,1,0:T(8,128)(2,1)S(1)}, bf16[16,56,384]{2,1,0:T(8,128)(2,1)S(1)}, u32[]{:S(2)}, u32[]{:S(2)}) collective-permute-start(bf16[16,56,384]{2,1,0:T(8,128)(2,1)S(1)} %all-to-all-done.2.own_ref), channel_id=1, source_target_pairs={{0,8},{8,0},{1,9},{9,1},{2,10},{10,2},{3,11},{11,3},{4,12},{12,4},... | collective-permute-start | bytes 2064392 | tf_op jit(solution)/shard_map/ppermute | solution.py:448
  99.8 22.0 %copy-start.2 = (bf16[80,2048]{1,0:T(8,128)(2,1)S(1)}, bf16[80,2048]{1,0:T(8,128)(2,1)}, u32[]{:S(2)}) copy-start(bf16[80,2048]{1,0:T(8,128)(2,1)} %get-tuple-element.57.refs_0_) | copy-start | bytes 983044
  99.8 22.0 %copy-start.4 = (bf16[80,2048]{1,0:T(8,128)(2,1)S(1)}, bf16[80,2048]{1,0:T(8,128)(2,1)}, u32[]{:S(2)}) copy-start(bf16[80,2048]{1,0:T(8,128)(2,1)} %copy-done.3) | copy-start | bytes 983044
  122.7 2.4 %collective-permute-start.10 = (bf16[1024,384]{1,0:T(8,128)(2,1)S(1)}, bf16[1024,384]{1,0:T(8,128)(2,1)S(1)}, u32[]{:S(2)}, u32[]{:S(2)}) collective-permute-start(bf16[1024,384]{1,0:T(8,128)(2,1)S(1)} %down.3), channel_id=1, source_target_pairs={{0,8},{8,0},{1,9},{9,1},{2,10},{10,2},{3,11},{11,3},{4,12},{12,4},... | collective-permute-start | bytes 2359304 | tf_op jit(solution)/shard_map/ppermute | solution.py:448

commit v4 on v3

--- a/solution.py
+++ b/solution.py
@@ -40,7 +40,7 @@
 HBM = pl.BlockSpec(memory_space=pltpu.HBM)
 
 
-def params(mib=24):
+def params(mib=12):
     return pltpu.CompilerParams(vmem_limit_bytes=mib * 2**20)
 
 
@@ -53,7 +53,7 @@
 
 
 def attend_kernel(
-    lengths, q_ref, fresh_ref, cache_hbm, w_uv_hbm, mine_ref, theirs_ref, keys, scores, w_uv,
+    lengths, q_ref, fresh_ref, cache_hbm, w_uv_hbm, out_ref, keys, scores, w_uv,
     new_keys, key_sems, w_sem,
 ):
     copies = [
@@ -126,17 +126,17 @@
                 value = jnp.where(head == h + i, pair[:, i * VDIM : (i + 1) * VDIM], 0.0)
                 values.append(jnp.sum(value.reshape(NEW, HEADS, VDIM), axis=1))
         halves.append(jnp.concatenate(values, axis=1))
-    second = lax.axis_index("c") == 1
-    mine_ref[...] = jnp.where(second, halves[1], halves[0]).astype(jnp.bfloat16)
-    theirs_ref[...] = jnp.where(second, halves[0], halves[1]).astype(jnp.bfloat16)
+    both = jnp.concatenate(halves, axis=0).astype(jnp.bfloat16)
+    for i in range(N_RING):
+        out_ref[i] = both
 
 
 def attend(lengths, q, fresh, cache_t, w_uv):
     return pl.pallas_call(
         attend_kernel,
-        out_shape=(shape(NEW, HALF), shape(NEW, HALF)),
+        out_shape=shape(N_RING, 2 * NEW, HALF),
         in_specs=[SMEM, VMEM, VMEM, ANY, ANY],
-        out_specs=(VMEM, VMEM),
+        out_specs=VMEM,
         scratch_shapes=[
             pltpu.VMEM((N_CHUNK, KDIM, CHUNK), jnp.bfloat16),
             pltpu.VMEM((N_CHUNK, ROWS, CHUNK), jnp.float32),
@@ -153,25 +153,18 @@
     )(lengths, q, fresh, cache_t, w_uv)
 
 
-def fan_kernel(mine_ref, theirs_ref, out_ref):
-    second = lax.axis_index("c") == 1
-    mine, theirs = mine_ref[...].astype(jnp.float32), theirs_ref[...].astype(jnp.float32)
-    both = jnp.concatenate(
-        [jnp.where(second, theirs, mine), jnp.where(second, mine, theirs)], axis=0
-    ).astype(jnp.bfloat16)
-    for i in range(N_RING):
-        out_ref[i] = both
-
-
-def fan(mine, theirs):
-    return pl.pallas_call(
-        fan_kernel,
-        out_shape=shape(N_RING, 2 * NEW, HALF),
-        in_specs=[VMEM, VMEM],
-        out_specs=VMEM,
-        compiler_params=params(),
-        name="fan",
-    )(mine, theirs)
+def one_hot(rows, columns, source):
+    column = lax.broadcasted_iota(jnp.int32, (1, columns), 1)
+    row = lax.broadcasted_iota(jnp.int32, (rows, columns), 0)
+    return jnp.where(row == source(column), 1.0, 0.0).astype(jnp.bfloat16)
+
+
+def token_order():
+    def source(at):
+        core, rest = at // (N_RING * NEW), at % (N_RING * NEW)
+        return (rest // NEW * 2 + core) * NEW + rest % NEW
+
+    return one_hot(TOKENS, TOKENS, source)
 
 
 def pick_columns(ks, width):
@@ -189,7 +182,7 @@
     return jnp.where(rows == source, 1.0, 0.0).astype(jnp.bfloat16)
 
 
-def regroup_kernel(ks, count, gained, *refs):
+def regroup_kernel(ks, count, *refs):
     sources, gain_ref, refs = refs[:count], refs[count], refs[count + 2 :]
     outs, (rows, loaded, moved_ref, in_sems, out_sems) = refs[:-5], refs[-5:]
     width = 4 * FEAT
@@ -200,17 +193,17 @@
     for load in loads:
         load.start()
     pick = pick_columns(ks, width)
-    for i in range(count):
-        loads[i].wait()
-        rows[i * ROOM + ROOM - 16 : (i + 1) * ROOM, :] = jnp.zeros((16, D), jnp.bfloat16)
-        if gained:
-            for j in range(D // 128):
-                lanes = slice(j * 128, (j + 1) * 128)
-                wide = loaded[i, :, lanes].astype(jnp.float32)
-                wide = wide * gain_ref[j : j + 1, :].astype(jnp.float32)
-                rows[i * ROOM : i * ROOM + FF, lanes] = wide.astype(jnp.bfloat16)
-        else:
-            rows[i * ROOM : i * ROOM + FF, :] = loaded[i]
+    for load in loads:
+        load.wait()
+    if count == 2:
+        for j in range(D // 128):
+            lanes = slice(j * 128, (j + 1) * 128)
+            both = [loaded[i, :, lanes].astype(jnp.float32) for i in range(count)]
+            both = jnp.concatenate(both, axis=0) * gain_ref[j : j + 1, :].astype(jnp.float32)
+            rows[:, lanes] = both.astype(jnp.bfloat16)
+    else:
+        rows[ROOM - 16 :, :] = jnp.zeros((16, D), jnp.bfloat16)
+        rows[:FF, :] = loaded[0]
     stores = []
     for n in range(len(ks)):
         for m in range(D // width):
@@ -225,39 +218,59 @@
         store.wait()
 
 
-def regroup(ks, sources, gain, gained, after):
+def regroup(ks, sources, gain, after):
     count = len(sources)
-    return pl.pallas_call(
-        functools.partial(regroup_kernel, ks, count, gained),
-        out_shape=[shape(count * ROOM, 2 * OUT)] * len(ks),
+    height = 2 * FF if count == 2 else ROOM
+    return pl.pallas_call(
+        functools.partial(regroup_kernel, ks, count),
+        out_shape=[shape(height, 2 * OUT)] * len(ks),
         in_specs=[HBM] * count + [VMEM, ANY],
         out_specs=[HBM] * len(ks),
         scratch_shapes=[
-            pltpu.VMEM((count * ROOM, D), jnp.bfloat16),
+            pltpu.VMEM((height, D), jnp.bfloat16),
             pltpu.VMEM((count, FF, D), jnp.bfloat16),
-            pltpu.VMEM((len(ks), count * ROOM, 2 * OUT), jnp.bfloat16),
+            pltpu.VMEM((len(ks), height, 2 * OUT), jnp.bfloat16),
             pltpu.SemaphoreType.DMA((count,)),
             pltpu.SemaphoreType.DMA((len(ks),)),
         ],
         compiler_params=params(58),
         cost_estimate=pl.CostEstimate(
-            flops=2 * count * ROOM * D * 256 * len(ks), bytes_accessed=5 * 2**20, transcendentals=0
+            flops=2 * height * D * 256 * len(ks), bytes_accessed=5 * 2**20, transcendentals=0
         ),
         name="regroup",
     )(*sources, gain, after)
 
 
+def project_heads(heads_ref, w_ref):
+    def source(at):
+        ring, rest = at // (2 * NEW), at % (2 * NEW)
+        return rest // NEW * (N_RING * NEW) + ring * NEW + rest % NEW
+
+    split = one_hot(TOKENS, TOKENS, source)
+    heads = dot(split, heads_ref[...]).astype(jnp.bfloat16)
+    return dot(w_ref[:, :HALF], heads[: N_RING * NEW], NT) + dot(
+        w_ref[:, HALF:], heads[N_RING * NEW :], NT
+    )
+
+
 def project_own_kernel(heads_ref, w_ref, out_ref):
-    lanes = pl.ds(pl.multiple_of(lax.axis_index("c") * HALF, HALF), HALF)
-    out_ref[...] = dot(w_ref[:, lanes], heads_ref[...], NT)
+    out_ref[...] = project_heads(heads_ref, w_ref).astype(jnp.bfloat16)
 
 
 def project_more_kernel(first_ref, heads_ref, w_ref, out_ref):
-    lanes = pl.ds(pl.multiple_of((1 - lax.axis_index("c")) * HALF, HALF), HALF)
-    total = first_ref[...] + dot(w_ref[:, lanes], heads_ref[...], NT)
-    pieces = [total[t * PIECE : (t + 1) * PIECE] for t in range(N_TP)]
+    more = project_heads(heads_ref, w_ref).astype(jnp.bfloat16)
+    core, count = lax.axis_index("c"), N_RING * NEW
+    own_place = one_hot(count, TOKENS, lambda at: at - core * count)
+    more_place = one_hot(count, TOKENS, lambda at: at - (1 - core) * count)
+    total = dot(first_ref[...], own_place) + dot(more, more_place)
+
+    def source(at):
+        t, j = at // PIECE, at % PIECE
+        return (t % N_Y * 2 + t // N_Y) * PIECE + j
+
+    total = dot(one_hot(FEAT, FEAT, source), total.astype(jnp.bfloat16))
     for y in range(N_Y):
-        pair = jnp.concatenate([pieces[y], pieces[N_Y + y]], axis=0).astype(jnp.bfloat16)
+        pair = total[y * PAIR : (y + 1) * PAIR].astype(jnp.bfloat16)
         out_ref[y] = pair
         out_ref[N_Y + y] = pair
 
@@ -268,7 +281,7 @@
     )
     first = pl.pallas_call(
         project_own_kernel,
-        out_shape=shape(FEAT, TOKENS, dtype=jnp.float32),
+        out_shape=shape(FEAT, N_RING * NEW),
         in_specs=[VMEM] * 2,
         out_specs=VMEM,
         compiler_params=params(),
@@ -288,7 +301,7 @@
 
 def update_kernel(parts_ref, residual_ref, updated_ref, out_ref):
     attended = jnp.sum(parts_ref[...].astype(jnp.float32), axis=0)
-    updated = (residual_ref[...].astype(jnp.float32) + attended).astype(jnp.bfloat16)
+    updated = (dot(residual_ref[...], token_order()) + attended).astype(jnp.bfloat16)
     updated_ref[...] = updated
     for i in range(N_RING):
         out_ref[i] = updated
@@ -338,27 +351,29 @@
     more, squares = spaced(more_ref)
     squares = squares_ref[...] + squares
     high = squares.astype(jnp.bfloat16).astype(jnp.float32)
-    row = lax.broadcasted_iota(jnp.int32, (2 * ROOM, TOKENS), 0)
+    row = lax.broadcasted_iota(jnp.int32, (16, TOKENS), 0)
+    tail = jnp.where(row == 0, high, jnp.where(row == 1, squares - high, 0.0))
+    tail = tail.astype(jnp.bfloat16)
     y = lax.axis_index("y")
     for k in range(N_Y):
         copies[k].wait()
         part = part_ref[k] + dot(held[k], more)
-        part = jnp.where(row == FF, high, jnp.where(row == FF + 1, squares - high, part))
-        out_ref[y ^ k] = part.astype(jnp.bfloat16)
+        out_ref[y ^ k, : 2 * FF, :] = part.astype(jnp.bfloat16)
+        out_ref[y ^ k, 2 * FF :, :] = tail
 
 
 def mix(own, more, blocks):
     scratch = [
-        pltpu.VMEM((N_Y, 2 * ROOM, OUT), jnp.bfloat16),
+        pltpu.VMEM((N_Y, 2 * FF, OUT), jnp.bfloat16),
         pltpu.SemaphoreType.DMA((N_Y,)),
     ]
     cost = pl.CostEstimate(
-        flops=2 * N_Y * 2 * ROOM * OUT * TOKENS, bytes_accessed=4 * 2**20, transcendentals=0
+        flops=2 * N_Y * 2 * FF * OUT * TOKENS, bytes_accessed=4 * 2**20, transcendentals=0
     )
     part, squares = pl.pallas_call(
         mix_own_kernel,
         out_shape=(
-            shape(N_Y, 2 * ROOM, TOKENS, dtype=jnp.float32),
+            shape(N_Y, 2 * FF, TOKENS, dtype=jnp.float32),
             shape(1, TOKENS, dtype=jnp.float32),
         ),
         in_specs=[VMEM] + [ANY] * N_Y,
@@ -370,7 +385,7 @@
     )(own, *blocks)
     return pl.pallas_call(
         mix_more_kernel,
-        out_shape=shape(N_Y, 2 * ROOM, TOKENS),
+        out_shape=shape(N_Y, 2 * FF + 16, TOKENS),
         in_specs=[VMEM] * 3 + [ANY] * N_Y,
         out_specs=VMEM,
         scratch_shapes=scratch,
@@ -382,11 +397,11 @@
 
 def gate_kernel(parts_ref, out_ref):
     total = jnp.sum(parts_ref[...].astype(jnp.float32), axis=0)
-    mean = (total[FF : FF + 1] + total[FF + 1 : FF + 2]) * (1.0 / D)
+    mean = (total[2 * FF : 2 * FF + 1] + total[2 * FF + 1 : 2 * FF + 2]) * (1.0 / D)
     inverse_rms = lax.rsqrt(mean + EPS)
-    gate_out, up_out = total[:ROOM] * inverse_rms, total[ROOM:] * inverse_rms
-    row = lax.broadcasted_iota(jnp.int32, (ROOM, TOKENS), 0)
-    hidden = jnp.where(row < FF, gate_out / (1.0 + jnp.exp(-gate_out)) * up_out, 0.0)
+    gate_out, up_out = total[:FF] * inverse_rms, total[FF : 2 * FF] * inverse_rms
+    hidden = gate_out / (1.0 + jnp.exp(-gate_out)) * up_out
+    hidden = jnp.concatenate([hidden, jnp.zeros((ROOM - FF, TOKENS), jnp.float32)], axis=0)
     hidden = hidden.astype(jnp.bfloat16)
     for t in range(N_Y):
         out_ref[t] = hidden
@@ -440,6 +455,24 @@
     )(hidden, *blocks)
 
 
+def finish_kernel(updated_ref, parts_ref, out_ref):
+    wide = updated_ref[...].astype(jnp.float32)
+    own = jnp.where(lax.axis_index("xh") == 0, wide[:PIECE], wide[PIECE:])
+    total = own + jnp.sum(parts_ref[...].astype(jnp.float32), axis=0)[:PIECE]
+    out_ref[...] = dot(total.astype(jnp.bfloat16), token_order(), NT).astype(jnp.bfloat16)
+
+
+def finish(updated, parts):
+    return pl.pallas_call(
+        finish_kernel,
+        out_shape=shape(PIECE, TOKENS),
+        in_specs=[VMEM] * 2,
+        out_specs=VMEM,
+        compiler_params=params(),
+        name="finish",
+    )(updated, parts)
+
+
 def swap(x, axes):
     return lax.all_to_all(x, axes, 0, 0, tiled=True)
 
@@ -457,7 +490,7 @@
 ):
     xh = lax.axis_index("xh")
 
-    mine, theirs = attend(
+    heads = attend(
         cache_lengths.T, queries.reshape(ROWS, KDIM), jnp.transpose(new_latent, (1, 0, 2)), cache.T,
         w_uv,
     )
@@ -467,10 +500,10 @@
 
     gain = norm_gain.reshape(D // 128, 128)
     sources = (w_gate.T, w_up.T)
-    mix_1, mix_3 = regroup((1, 3), sources, gain, True, mine)
-    mix_2, mix_0 = regroup((2, 0), sources, gain, True, mix_1)
-
-    heads = swap(fan(mine, other_core(theirs)), RING).reshape(TOKENS, HALF)
+    mix_1, mix_3 = regroup((1, 3), sources, gain, heads)
+    mix_2, mix_0 = regroup((2, 0), sources, gain, mix_1)
+
+    heads = swap(heads, RING).reshape(TOKENS, HALF)
     heads, mix_1, mix_3, mix_0 = lax.optimization_barrier(
         (heads, exchange(mix_1, 1), exchange(mix_3, 3), mix_0)
     )
@@ -480,11 +513,11 @@
     residual = jnp.concatenate(
         [jnp.where(xh == 0, residual.T, partner), jnp.where(xh == 0, partner, residual.T)], axis=0
     )
-    down_blocks = regroup((1, 3, 2, 0), (w_down,), gain, False, partial)
-    updated, block = update(swap(partial, TP), residual)
-    block, mix_2, *down_blocks = lax.optimization_barrier(
-        (block, exchange(mix_2, 2), *down_blocks)
-    )
+    down_blocks = regroup((1, 3, 2, 0), (w_down,), gain, partial)
+    parts, mix_2, *down_blocks = lax.optimization_barrier(
+        (swap(partial, TP), exchange(mix_2, 2), *down_blocks)
+    )
+    updated, block = update(parts, residual)
     down_1, down_3, down_2, down_0 = down_blocks
     own, down_1, down_2, down_3 = lax.optimization_barrier(
         (swap(block, RING), exchange(down_1, 1), exchange(down_2, 2), exchange(down_3, 3))
@@ -495,9 +528,7 @@
     more = other_core(down(1, hidden, down_blocks))
     term = down(0, hidden, down_blocks) + more.astype(jnp.float32)
     term = swap(term.astype(jnp.bfloat16).reshape(2 * N_RING, PAD, TOKENS), RING + ("xh",))
-    term = jnp.sum(term.astype(jnp.float32), axis=0)[:PIECE]
-    updated = jnp.where(xh == 0, updated[:PIECE], updated[PIECE:])
-    return (updated.astype(jnp.float32) + term).astype(jnp.bfloat16).T
+    return finish(updated, term).T
 
 
 def solution(mesh):

time: 159 us -> 153 us (0.962)
  waiting for transfers between devices: 35.6 us -> 28.7 us
  Pallas kernels: 31.5 us -> 33.3 us
    ppermute x6, waiting for transfers between devices: 25.9 us -> 22.6 us  [exchange(): return lax.ppermute(block, 'y', [(i, i ^ k) for i in range(N_Y)])]
    all_to_all x3, waiting for transfers between devices: 6.46 us -> 4.17 us  [swap(): return lax.all_to_all(x, axes, 0, 0, tiled=True)]
    ppermute x4 -> x3, waiting for transfers between devices: 3.2 us -> 1.89 us  [other_core(): return lax.ppermute(x, 'c', [(0, 1), (1, 0)])]
  transfers between devices with their start and end apart: 14 -> 13, of which waited for: 9 -> 8; matrix products, arithmetic and copies ran while one was open for 0% -> 0% of each run, Pallas kernels for 13% -> 14%
where the time goes in v4:
time: 153 us; the launch traced here: 152 us
  blocking collectives  54.2 us (35%)
  Pallas kernels  33.3 us (22%)
  starting transfers between devices  33.3 us (22%)
  waiting for transfers between devices  28.7 us (19%)
  local copies, waits for them, and re-layouts  2.32 us (2%)
    all_to_all x3, blocking collectives, swap(): return lax.all_to_all(x, axes, 0, 0, tiled=True)  54.2 us
    ppermute x6, waiting for transfers between devices, exchange(): return lax.ppermute(block, 'y', [(i, i ^ k) for i in range(N_Y)])  22.6 us
    all_to_all x3, starting transfers between devices, swap(): return lax.all_to_all(x, axes, 0, 0, tiled=True)  20.7 us
    pallas_call x3, Pallas kernels, regroup(): pl.pallas_call(functools.partial(regroup_kernel, ks, count), out_shape=[s...  14.7 us
    ppermute x6, starting transfers between devices, exchange(): return lax.ppermute(block, 'y', [(i, i ^ k) for i in range(N_Y)])  9.77 us
    pallas_call x1, Pallas kernels, attend(): pl.pallas_call(attend_kernel, out_shape=shape(N_RING, 2 * NEW, HALF), in_...  7.81 us
    all_to_all x3, waiting for transfers between devices, swap(): return lax.all_to_all(x, axes, 0, 0, tiled=True)  4.17 us
    pallas_call x1, Pallas kernels, project(): pl.pallas_call(project_more_kernel, out_shape=shape(N_TP, PAIR, TOKENS),...  3.38 us
  transfers between devices with their start and end apart: 13, of which 8 were waited for; matrix products, arithmetic and copies ran while one was open for 0% of the time, Pallas kernels for 14%

profile of v4, /device:TPU:32, one launch (start us, length us, event | category | flops | bytes accessed | tf_op | source)
XLA Modules:
  0.0 152.3 jit_solution(10454108281184436747)
XLA Ops:
  0.0 7.8 %attend.1.refs_3_ = bf16[16,24,1024]{2,1,0:T(8,128)(2,1)} custom-call(s32[4,32]{1,0:T(4,128)} %bitcast.23, bf16[192,576]{1,0:T(8,128)(2,1)} %bitcast.20, bf16[3,4,576]{2,1,0:T(4,128)(2,1)} %bitcast.22, bf16[576,4096]{1,0:T(8,128)(2,1)} %bitcast.18, bf16[16,512,128]{2,1,0:T(8,128)(2,1)} %w_uv_hbm.1), custom_call_target="tpu_custom_call" | custom-call | flops 1711276032 | bytes 7340032 | tf_op jit(solution)/shard_map/attend/pallas_call | solution.py:135
  7.8 9.5 %all-to-all-start = ((bf16[16,24,1024]{2,1,0:T(8,128)(2,1)}), bf16[16,24,1024]{2,1,0:T(8,128)(2,1)S(1)}, u32[]{:S(2)}, u32[]{:S(2)}) async-start(bf16[16,24,1024]{2,1,0:T(8,128)(2,1)} %attend.1.refs_3_), calls=%async_computation | async-start | bytes 1572864 | tf_op jit(solution)/shard_map/all_to_all | solution.py:477
  17.3 4.6 %regroup.3 = (bf16[144,2048]{1,0:T(8,128)(2,1)}, bf16[144,2048]{1,0:T(8,128)(2,1)}) custom-call(bf16[72,7168]{1,0:T(8,128)(2,1)} %bitcast.24, bf16[72,7168]{1,0:T(8,128)(2,1)} %bitcast.26, bf16[56,128]{1,0:T(8,128)(2,1)} %bitcast.28, bf16[16,24,1024]{2,1,0:T(8,128)(2,1)} %attend.1.refs_3_), custom_call_target="tpu_custom_call" | custom-call | flops 1056964608 | bytes 5242880 | tf_op jit(solution)/shard_map/regroup/pallas_call | solution.py:224
  21.9 3.1 %collective-permute-start.1 = (bf16[144,2048]{1,0:T(8,128)(2,1)}, bf16[144,2048]{1,0:T(8,128)(2,1)S(1)}, u32[]{:S(2)}, u32[]{:S(2)}) collective-permute-start(bf16[144,2048]{1,0:T(8,128)(2,1)} %get-tuple-element.32), channel_id=1, source_target_pairs={{0,3},{1,2},{2,1},{3,0},{4,7},{5,6},{6,5},{7,4},{8,11},{9,10},{10,... | collective-permute-start | bytes 1769480 | tf_op jit(solution)/shard_map/ppermute | solution.py:499
  25.0 0.1 collective-permute-start
  25.2 4.7 %regroup.4 = (bf16[144,2048]{1,0:T(8,128)(2,1)}, bf16[144,2048]{1,0:T(8,128)(2,1)}) custom-call(bf16[72,7168]{1,0:T(8,128)(2,1)} %bitcast.25, bf16[72,7168]{1,0:T(8,128)(2,1)} %bitcast.27, bf16[56,128]{1,0:T(8,128)(2,1)} %bitcast.29, bf16[144,2048]{1,0:T(8,128)(2,1)} %get-tuple-element.31.refs_3_), custom_call_target="tpu_custom_call" | custom-call | flops 1056964608 | bytes 5242880 | tf_op jit(solution)/shard_map/regroup/pallas_call | solution.py:224
  29.8 8.2 %collective-permute-done.1.refs_3_ = bf16[144,2048]{1,0:T(8,128)(2,1)S(1)} collective-permute-done((bf16[144,2048]{1,0:T(8,128)(2,1)}, bf16[144,2048]{1,0:T(8,128)(2,1)S(1)}, u32[]{:S(2)}, u32[]{:S(2)}) %collective-permute-start.1) | collective-permute-done | bytes 589856 | tf_op jit(solution)/shard_map/ppermute | solution.py:499
  38.0 1.5 collective-permute-done.refs_1_
  39.5 0.0 all-to-all-done
  39.5 0.0 collective-permute-start.2
  39.5 1.8 %collective-permute-start.3 = (bf16[144,2048]{1,0:T(8,128)(2,1)}, bf16[144,2048]{1,0:T(8,128)(2,1)S(1)}, u32[]{:S(2)}, u32[]{:S(2)}) collective-permute-start(bf16[144,2048]{1,0:T(8,128)(2,1)} %get-tuple-element.35), channel_id=1, source_target_pairs={{0,2},{1,3},{2,0},{3,1},{4,6},{5,7},{6,4},{7,5},{8,10},{9,11},{10,... | collective-permute-start | bytes 1769480 | tf_op jit(solution)/shard_map/ppermute | solution.py:499
  41.3 0.0 copy-done.8
  41.3 2.7 %collective-permute-start.4 = (bf16[28,384]{1,0:T(8,128)(2,1)S(1)}, bf16[28,384]{1,0:T(8,128)(2,1)S(1)}, u32[]{:S(2)}, u32[]{:S(2)}) collective-permute-start(bf16[28,384]{1,0:T(8,128)(2,1)S(1)} %bitcast.21), channel_id=1, source_target_pairs={{0,4},{4,0},{1,5},{5,1},{2,6},{6,2},{3,7},{7,3},{8,12},{12,8},{9,1... | collective-permute-start | bytes 64520 | tf_op jit(solution)/shard_map/ppermute | solution.py:485
  44.0 0.0 copy-done
  44.0 1.2 project_own.1.first_ref
  45.2 0.0 collective-permute-done.2.heads_ref
  45.2 3.4 %project_more.1.refs_2_ = bf16[8,56,384]{2,1,0:T(8,128)(2,1)} custom-call(bf16[224,192]{1,0:T(8,128)(2,1)S(1)} %project_own.1.first_ref, bf16[384,1024]{1,0:T(8,128)(2,1)} %collective-permute-done.2.heads_ref, bf16[224,2048]{1,0:T(8,128)(2,1)S(1)} %bitcast.15), custom_call_target="tpu_custom_call" | custom-call | flops 176160768 | bytes 2097152 | tf_op jit(solution)/shard_map/project_more/pallas_call | solution.py:291
  48.6 3.6 %all-to-all-start.1 = ((bf16[8,56,384]{2,1,0:T(8,128)(2,1)}), bf16[8,56,384]{2,1,0:T(8,128)(2,1)S(1)}, u32[]{:S(2)}, u32[]{:S(2)}) async-start(bf16[8,56,384]{2,1,0:T(8,128)(2,1)} %project_more.1.refs_2_), calls=%async_computation.1 | async-start | bytes 688128 | tf_op jit(solution)/shard_map/all_to_all | solution.py:477
  52.2 0.0 collective-permute-done.4
  52.3 5.5 %regroup.5 = (bf16[80,2048]{1,0:T(8,128)(2,1)}, bf16[80,2048]{1,0:T(8,128)(2,1)}, bf16[80,2048]{1,0:T(8,128)(2,1)}, bf16[80,2048]{1,0:T(8,128)(2,1)}) custom-call(bf16[72,7168]{1,0:T(8,128)(2,1)} %refs_0_.1, bf16[56,128]{1,0:T(8,128)(2,1)} %bitcast.30, bf16[8,56,384]{2,1,0:T(8,128)(2,1)} %project_more.1.refs_2_), custom_call_target="tpu_custom_call" | custom-call | flops 1174405120 | bytes 5242880 | tf_op jit(solution)/shard_map/regroup/pallas_call | solution.py:224
  57.8 0.0 collective-permute-done.3.refs_2_
  57.8 4.2 %all-to-all-done.1.parts_ref = bf16[8,56,384]{2,1,0:T(8,128)(2,1)S(1)} async-done(((bf16[8,56,384]{2,1,0:T(8,128)(2,1)}), bf16[8,56,384]{2,1,0:T(8,128)(2,1)S(1)}, u32[]{:S(2)}, u32[]{:S(2)}) %all-to-all-start.1) | async-done | bytes 344096 | tf_op jit(solution)/shard_map/all_to_all | solution.py:477
  61.9 0.2 update.1
  62.2 0.8 copy-done.7
  63.0 7.6 %all-to-all-start.2 = ((bf16[16,56,384]{2,1,0:T(8,128)(2,1)}), bf16[16,56,384]{2,1,0:T(8,128)(2,1)S(1)}, u32[]{:S(2)}, u32[]{:S(2)}) async-start(bf16[16,56,384]{2,1,0:T(8,128)(2,1)} %copy-done.7), calls=%async_computation.2 | async-start | bytes 1376256 | tf_op jit(solution)/shard_map/all_to_all | solution.py:477
  70.6 0.1 collective-permute-start.5
  70.7 2.1 %collective-permute-start.6 = (bf16[80,2048]{1,0:T(8,128)(2,1)}, bf16[80,2048]{1,0:T(8,128)(2,1)S(1)}, u32[]{:S(2)}, u32[]{:S(2)}) collective-permute-start(bf16[80,2048]{1,0:T(8,128)(2,1)} %get-tuple-element.44), channel_id=1, source_target_pairs={{0,2},{1,3},{2,0},{3,1},{4,6},{5,7},{6,4},{7,5},{8,10},{9,11},{10,... | collective-permute-start | bytes 983048 | tf_op jit(solution)/shard_map/ppermute | solution.py:499
  72.8 2.5 %collective-permute-start.7 = (bf16[80,2048]{1,0:T(8,128)(2,1)}, bf16[80,2048]{1,0:T(8,128)(2,1)S(1)}, u32[]{:S(2)}, u32[]{:S(2)}) collective-permute-start(bf16[80,2048]{1,0:T(8,128)(2,1)} %get-tuple-element.45), channel_id=1, source_target_pairs={{0,3},{1,2},{2,1},{3,0},{4,7},{5,6},{6,5},{7,4},{8,11},{9,10},{10,... | collective-permute-start | bytes 983048 | tf_op jit(solution)/shard_map/ppermute | solution.py:499
  75.3 6.2 %collective-permute-done.5.refs_1_ = bf16[80,2048]{1,0:T(8,128)(2,1)S(1)} collective-permute-done((bf16[80,2048]{1,0:T(8,128)(2,1)}, bf16[80,2048]{1,0:T(8,128)(2,1)S(1)}, u32[]{:S(2)}, u32[]{:S(2)}) %collective-permute-start.5) | collective-permute-done | bytes 327712 | tf_op jit(solution)/shard_map/ppermute | solution.py:499
  81.5 5.0 %collective-permute-done.6.refs_2_ = bf16[80,2048]{1,0:T(8,128)(2,1)S(1)} collective-permute-done((bf16[80,2048]{1,0:T(8,128)(2,1)}, bf16[80,2048]{1,0:T(8,128)(2,1)S(1)}, u32[]{:S(2)}, u32[]{:S(2)}) %collective-permute-start.6) | collective-permute-done | bytes 327712 | tf_op jit(solution)/shard_map/ppermute | solution.py:499
  86.5 0.7 copy-done.3
  87.2 1.8 %collective-permute-done.7.refs_3_ = bf16[80,2048]{1,0:T(8,128)(2,1)S(1)} collective-permute-done((bf16[80,2048]{1,0:T(8,128)(2,1)}, bf16[80,2048]{1,0:T(8,128)(2,1)S(1)}, u32[]{:S(2)}, u32[]{:S(2)}) %collective-permute-start.7) | collective-permute-done | bytes 327712 | tf_op jit(solution)/shard_map/ppermute | solution.py:499
  89.1 0.7 copy-done.5
  89.8 0.0 all-to-all-done.2.own_ref
  89.8 0.0 collective-permute-start.8
  89.8 1.6 %mix_own.1 = (f32[4,144,384]{2,1,0:T(8,128)S(1)}, f32[1,384]{1,0:T(1,128)S(1)}) custom-call(bf16[16,56,384]{2,1,0:T(8,128)(2,1)S(1)} %all-to-all-done.2.own_ref, bf16[144,2048]{1,0:T(8,128)(2,1)S(1)} %copy-done.1, bf16[144,2048]{1,0:T(8,128)(2,1)S(1)} %collective-permute-done.refs_1_, bf16[144,2048]{1,0:T(8,128)(2,1)S(1)} %collective-permute-done.3.refs_2_, ...), custom_call_target="tpu_custom_call" | custom-call | flops 452984832 | bytes 4194304 | tf_op jit(solution)/shard_map/mix_own/pallas_call | solution.py:373
  91.5 0.5 collective-permute-done.8.more_ref
  92.0 1.6 %mix_more.1 = bf16[4,160,384]{2,1,0:T(8,128)(2,1)S(1)} custom-call(f32[4,144,384]{2,1,0:T(8,128)S(1)} %get-tuple-element.51.part_ref, f32[1,384]{1,0:T(1,128)S(1)} %get-tuple-element.52.squares_ref, bf16[16,56,384]{2,1,0:T(8,128)(2,1)S(1)} %collective-permute-done.8.more_ref, bf16[144,2048]{1,0:T(8,128)(2,1)S(1)} %copy-done.1, ...), custom_call_target="tpu_custom_call" | custom-call | flops 452984832 | bytes 4194304 | tf_op jit(solution)/shard_map/mix_more/pallas_call | solution.py:386
  93.6 12.2 %all_to_all.30.parts_ref = bf16[4,160,384]{2,1,0:T(8,128)(2,1)S(1)} all-to-all(bf16[4,160,384]{2,1,0:T(8,128)(2,1)S(1)} %mix_more.1), channel_id=1, replica_groups=mesh['xl'=2,'z'=8,'c'=2,'xh'=2,'y'=4] {'y'}, dimensions={0} | all-to-all | bytes 983040 | tf_op jit(solution)/shard_map/all_to_all | solution.py:477
  105.9 0.1 gate.1
  106.0 9.0 %all_to_all.31.hidden_ref = bf16[4,80,384]{2,1,0:T(8,128)(2,1)S(1)} all-to-all(bf16[4,80,384]{2,1,0:T(8,128)(2,1)S(1)} %gate.1), channel_id=1, replica_groups=mesh['xl'=2,'z'=8,'c'=2,'xh'=2,'y'=4] {'y'}, dimensions={0} | all-to-all | bytes 491520 | tf_op jit(solution)/shard_map/all_to_all | solution.py:477
  114.9 0.9 down.3
  115.8 0.1 collective-permute-start.9
  115.9 0.9 down.2
  116.8 1.4 collective-permute-done.9
  118.2 0.2 add_convert_fusion
  118.4 33.0 %all_to_all.32.parts_ref = bf16[32,32,384]{2,1,0:T(8,128)(2,1)S(1)} all-to-all(bf16[32,32,384]{2,1,0:T(8,128)(2,1)S(1)} %bitcast.19), channel_id=1, replica_groups=mesh['xl'=2,'z'=8,'c'=2,'xh'=2,'y'=4] {'xl','z','xh'}, dimensions={0} | all-to-all | bytes 1572864 | tf_op jit(solution)/shard_map/all_to_all | solution.py:477
  151.4 0.9 finish.1
  (15 shorter events, 0.1 us)
Async XLA Ops:
  7.8 31.6 %all-to-all-start = ((bf16[16,24,1024]{2,1,0:T(8,128)(2,1)}), bf16[16,24,1024]{2,1,0:T(8,128)(2,1)S(1)}, u32[]{:S(2)}, u32[]{:S(2)}) async-start(bf16[16,24,1024]{2,1,0:T(8,128)(2,1)} %attend.1.refs_3_), calls=%async_computation | async-start | bytes 1572864 | tf_op jit(solution)/shard_map/all_to_all | solution.py:477
  21.9 16.1 %collective-permute-start.1 = (bf16[144,2048]{1,0:T(8,128)(2,1)}, bf16[144,2048]{1,0:T(8,128)(2,1)S(1)}, u32[]{:S(2)}, u32[]{:S(2)}) collective-permute-start(bf16[144,2048]{1,0:T(8,128)(2,1)} %get-tuple-element.32), channel_id=1, source_target_pairs={{0,3},{1,2},{2,1},{3,0},{4,7},{5,6},{6,5},{7,4},{8,11},{9,10},{10,... | collective-permute-start | bytes 1769480 | tf_op jit(solution)/shard_map/ppermute | solution.py:499
  25.0 16.3 %copy-start.8 = (bf16[384,28]{0,1:T(8,128)(2,1)S(1)}, bf16[384,28]{0,1:T(8,128)(2,1)}, u32[]{:S(2)}) copy-start(bf16[384,28]{0,1:T(8,128)(2,1)} %param.17) | copy-start | bytes 64516
  25.0 19.0 %copy-start = (bf16[2048,224]{0,1:T(8,128)(2,1)S(1)}, bf16[2048,224]{0,1:T(8,128)(2,1)}, u32[]{:S(2)}) copy-start(bf16[2048,224]{0,1:T(8,128)(2,1)} %param.16) | copy-start | bytes 2752516
  25.0 14.4 %collective-permute-start = (bf16[144,2048]{1,0:T(8,128)(2,1)}, bf16[144,2048]{1,0:T(8,128)(2,1)S(1)}, u32[]{:S(2)}, u32[]{:S(2)}) collective-permute-start(bf16[144,2048]{1,0:T(8,128)(2,1)} %get-tuple-element.31.refs_3_), channel_id=1, source_target_pairs={{0,1},{1,0},{2,3},{3,2},{4,5},{5,4},{6,7},{7,6},{8,9},{9,8},{10,11... | collective-permute-start | bytes 1769480 | tf_op jit(solution)/shard_map/ppermute | solution.py:499
  39.5 5.8 %collective-permute-start.2 = (bf16[384,1024]{1,0:T(8,128)(2,1)S(1)}, bf16[384,1024]{1,0:T(8,128)(2,1)}, u32[]{:S(2)}, u32[]{:S(2)}) collective-permute-start(bf16[384,1024]{1,0:T(8,128)(2,1)S(1)} %bitcast.16), channel_id=1, source_target_pairs={{0,8},{8,0},{1,9},{9,1},{2,10},{10,2},{3,11},{11,3},{4,12},{12,4},... | collective-permute-start | bytes 2359304 | tf_op jit(solution)/shard_map/ppermute | solution.py:481
  39.5 18.3 %collective-permute-start.3 = (bf16[144,2048]{1,0:T(8,128)(2,1)}, bf16[144,2048]{1,0:T(8,128)(2,1)S(1)}, u32[]{:S(2)}, u32[]{:S(2)}) collective-permute-start(bf16[144,2048]{1,0:T(8,128)(2,1)} %get-tuple-element.35), channel_id=1, source_target_pairs={{0,2},{1,3},{2,0},{3,1},{4,6},{5,7},{6,4},{7,5},{8,10},{9,11},{10,... | collective-permute-start | bytes 1769480 | tf_op jit(solution)/shard_map/ppermute | solution.py:499
  41.3 10.9 %collective-permute-start.4 = (bf16[28,384]{1,0:T(8,128)(2,1)S(1)}, bf16[28,384]{1,0:T(8,128)(2,1)S(1)}, u32[]{:S(2)}, u32[]{:S(2)}) collective-permute-start(bf16[28,384]{1,0:T(8,128)(2,1)S(1)} %bitcast.21), channel_id=1, source_target_pairs={{0,4},{4,0},{1,5},{5,1},{2,6},{6,2},{3,7},{7,3},{8,12},{12,8},{9,1... | collective-permute-start | bytes 64520 | tf_op jit(solution)/shard_map/ppermute | solution.py:485
  48.6 13.3 %all-to-all-start.1 = ((bf16[8,56,384]{2,1,0:T(8,128)(2,1)}), bf16[8,56,384]{2,1,0:T(8,128)(2,1)S(1)}, u32[]{:S(2)}, u32[]{:S(2)}) async-start(bf16[8,56,384]{2,1,0:T(8,128)(2,1)} %project_more.1.refs_2_), calls=%async_computation.1 | async-start | bytes 688128 | tf_op jit(solution)/shard_map/all_to_all | solution.py:477
  57.8 32.1 %copy-start.1 = (bf16[144,2048]{1,0:T(8,128)(2,1)S(1)}, bf16[144,2048]{1,0:T(8,128)(2,1)}, u32[]{:S(2)}) copy-start(bf16[144,2048]{1,0:T(8,128)(2,1)} %get-tuple-element.47.refs_0_) | copy-start | bytes 1769476
  62.2 0.8 copy-start.7
  63.0 26.8 %all-to-all-start.2 = ((bf16[16,56,384]{2,1,0:T(8,128)(2,1)}), bf16[16,56,384]{2,1,0:T(8,128)(2,1)S(1)}, u32[]{:S(2)}, u32[]{:S(2)}) async-start(bf16[16,56,384]{2,1,0:T(8,128)(2,1)} %copy-done.7), calls=%async_computation.2 | async-start | bytes 1376256 | tf_op jit(solution)/shard_map/all_to_all | solution.py:477
  70.6 10.9 %collective-permute-start.5 = (bf16[80,2048]{1,0:T(8,128)(2,1)}, bf16[80,2048]{1,0:T(8,128)(2,1)S(1)}, u32[]{:S(2)}, u32[]{:S(2)}) collective-permute-start(bf16[80,2048]{1,0:T(8,128)(2,1)} %get-tuple-element.43), channel_id=1, source_target_pairs={{0,1},{1,0},{2,3},{3,2},{4,5},{5,4},{6,7},{7,6},{8,9},{9,8},{10,11... | collective-permute-start | bytes 983048 | tf_op jit(solution)/shard_map/ppermute | solution.py:499
  70.7 15.8 %collective-permute-start.6 = (bf16[80,2048]{1,0:T(8,128)(2,1)}, bf16[80,2048]{1,0:T(8,128)(2,1)S(1)}, u32[]{:S(2)}, u32[]{:S(2)}) collective-permute-start(bf16[80,2048]{1,0:T(8,128)(2,1)} %get-tuple-element.44), channel_id=1, source_target_pairs={{0,2},{1,3},{2,0},{3,1},{4,6},{5,7},{6,4},{7,5},{8,10},{9,11},{10,... | collective-permute-start | bytes 983048 | tf_op jit(solution)/shard_map/ppermute | solution.py:499
  72.8 16.2 %collective-permute-start.7 = (bf16[80,2048]{1,0:T(8,128)(2,1)}, bf16[80,2048]{1,0:T(8,128)(2,1)S(1)}, u32[]{:S(2)}, u32[]{:S(2)}) collective-permute-start(bf16[80,2048]{1,0:T(8,128)(2,1)} %get-tuple-element.45), channel_id=1, source_target_pairs={{0,3},{1,2},{2,1},{3,0},{4,7},{5,6},{6,5},{7,4},{8,11},{9,10},{10,... | collective-permute-start | bytes 983048 | tf_op jit(solution)/shard_map/ppermute | solution.py:499
  86.5 0.7 copy-start.3
  89.1 0.7 copy-start.5
  89.8 2.1 %collective-permute-start.8 = (bf16[16,56,384]{2,1,0:T(8,128)(2,1)S(1)}, bf16[16,56,384]{2,1,0:T(8,128)(2,1)S(1)}, u32[]{:S(2)}, u32[]{:S(2)}) collective-permute-start(bf16[16,56,384]{2,1,0:T(8,128)(2,1)S(1)} %all-to-all-done.2.own_ref), channel_id=1, source_target_pairs={{0,8},{8,0},{1,9},{9,1},{2,10},{10,2},{3,11},{11,3},{4,12},{12,4},... | collective-permute-start | bytes 2064392 | tf_op jit(solution)/shard_map/ppermute | solution.py:481
  93.6 21.3 %copy-start.2 = (bf16[80,2048]{1,0:T(8,128)(2,1)S(1)}, bf16[80,2048]{1,0:T(8,128)(2,1)}, u32[]{:S(2)}) copy-start(bf16[80,2048]{1,0:T(8,128)(2,1)} %get-tuple-element.53.refs_0_) | copy-start | bytes 983044
  93.6 21.3 %copy-start.4 = (bf16[80,2048]{1,0:T(8,128)(2,1)S(1)}, bf16[80,2048]{1,0:T(8,128)(2,1)}, u32[]{:S(2)}) copy-start(bf16[80,2048]{1,0:T(8,128)(2,1)} %copy-done.3) | copy-start | bytes 983044
  93.6 21.3 %copy-start.6 = (bf16[80,2048]{1,0:T(8,128)(2,1)S(1)}, bf16[80,2048]{1,0:T(8,128)(2,1)}, u32[]{:S(2)}) copy-start(bf16[80,2048]{1,0:T(8,128)(2,1)} %copy-done.5) | copy-start | bytes 983044
  115.8 2.4 %collective-permute-start.9 = (bf16[1024,384]{1,0:T(8,128)(2,1)S(1)}, bf16[1024,384]{1,0:T(8,128)(2,1)S(1)}, u32[]{:S(2)}, u32[]{:S(2)}) collective-permute-start(bf16[1024,384]{1,0:T(8,128)(2,1)S(1)} %down.3), channel_id=1, source_target_pairs={{0,8},{8,0},{1,9},{9,1},{2,10},{10,2},{3,11},{11,3},{4,12},{12,4},... | collective-permute-start | bytes 2359304 | tf_op jit(solution)/shard_map/ppermute | solution.py:481

commit v5 on v4

--- a/solution.py
+++ b/solution.py
@@ -184,26 +184,17 @@
 
 def regroup_kernel(ks, count, *refs):
     sources, gain_ref, refs = refs[:count], refs[count], refs[count + 2 :]
-    outs, (rows, loaded, moved_ref, in_sems, out_sems) = refs[:-5], refs[-5:]
+    outs, (rows, moved_ref, out_sems) = refs[:-3], refs[-3:]
     width = 4 * FEAT
-    loads = [
-        pltpu.make_async_copy(source, loaded.at[i], in_sems.at[i])
-        for i, source in enumerate(sources)
-    ]
-    for load in loads:
-        load.start()
     pick = pick_columns(ks, width)
-    for load in loads:
-        load.wait()
-    if count == 2:
-        for j in range(D // 128):
-            lanes = slice(j * 128, (j + 1) * 128)
-            both = [loaded[i, :, lanes].astype(jnp.float32) for i in range(count)]
-            both = jnp.concatenate(both, axis=0) * gain_ref[j : j + 1, :].astype(jnp.float32)
-            rows[:, lanes] = both.astype(jnp.bfloat16)
-    else:
-        rows[ROOM - 16 :, :] = jnp.zeros((16, D), jnp.bfloat16)
-        rows[:FF, :] = loaded[0]
+    for j in range(D // 128):
+        lanes = slice(j * 128, (j + 1) * 128)
+        wide = [ref[:, lanes].astype(jnp.float32) for ref in sources]
+        if count == 2:
+            wide = jnp.concatenate(wide, axis=0) * gain_ref[j : j + 1, :].astype(jnp.float32)
+        else:
+            wide = jnp.concatenate(wide + [jnp.zeros((ROOM - FF, 128), jnp.float32)], axis=0)
+        rows[:, lanes] = wide.astype(jnp.bfloat16)
     stores = []
     for n in range(len(ks)):
         for m in range(D // width):
@@ -224,13 +215,11 @@
     return pl.pallas_call(
         functools.partial(regroup_kernel, ks, count),
         out_shape=[shape(height, 2 * OUT)] * len(ks),
-        in_specs=[HBM] * count + [VMEM, ANY],
+        in_specs=[VMEM] * (count + 1) + [ANY],
         out_specs=[HBM] * len(ks),
         scratch_shapes=[
             pltpu.VMEM((height, D), jnp.bfloat16),
-            pltpu.VMEM((count, FF, D), jnp.bfloat16),
             pltpu.VMEM((len(ks), height, 2 * OUT), jnp.bfloat16),
-            pltpu.SemaphoreType.DMA((count,)),
             pltpu.SemaphoreType.DMA((len(ks),)),
         ],
         compiler_params=params(58),

time: 153 us -> 152 us (level)
  Pallas kernels: 33.3 us -> 31.3 us
    pallas_call x3, Pallas kernels: 14.7 us -> 12.6 us  [regroup(): pl.pallas_call(functools.partial(regroup_kernel, ks, count), out_shape=[s...]
  transfers between devices with their start and end apart: 13 -> 13, of which waited for: 8 -> 8; matrix products, arithmetic and copies ran while one was open for 0% -> 0% of each run, Pallas kernels for 14% -> 13%
where the time goes in v5:
time: 152 us
  blocking collectives  54.2 us (36%)
  starting transfers between devices  33.5 us (22%)
  Pallas kernels  31.3 us (21%)
  waiting for transfers between devices  29.9 us (20%)
  local copies, waits for them, and re-layouts  2.32 us (2%)
    all_to_all x3, blocking collectives, swap(): return lax.all_to_all(x, axes, 0, 0, tiled=True)  54.2 us
    ppermute x6, waiting for transfers between devices, exchange(): return lax.ppermute(block, 'y', [(i, i ^ k) for i in range(N_Y)])  23.3 us
    all_to_all x3, starting transfers between devices, swap(): return lax.all_to_all(x, axes, 0, 0, tiled=True)  20.2 us
    pallas_call x3, Pallas kernels, regroup(): pl.pallas_call(functools.partial(regroup_kernel, ks, count), out_shape=[s...  12.6 us
    ppermute x6, starting transfers between devices, exchange(): return lax.ppermute(block, 'y', [(i, i ^ k) for i in range(N_Y)])  10.5 us
    pallas_call x1, Pallas kernels, attend(): pl.pallas_call(attend_kernel, out_shape=shape(N_RING, 2 * NEW, HALF), in_...  7.81 us
    all_to_all x3, waiting for transfers between devices, swap(): return lax.all_to_all(x, axes, 0, 0, tiled=True)  4.68 us
    pallas_call x1, Pallas kernels, project(): pl.pallas_call(project_more_kernel, out_shape=shape(N_TP, PAIR, TOKENS),...  3.38 us
  transfers between devices with their start and end apart: 13, of which 8 were waited for; matrix products, arithmetic and copies ran while one was open for 0% of the time, Pallas kernels for 13%

profile of v5, /device:TPU:32, one launch (start us, length us, event | category | flops | bytes accessed | tf_op | source)
XLA Modules:
  0.0 151.6 jit_solution(9690207206500290212)
XLA Ops:
  0.0 7.8 %attend.1.refs_3_ = bf16[16,24,1024]{2,1,0:T(8,128)(2,1)} custom-call(s32[4,32]{1,0:T(4,128)} %bitcast.23, bf16[192,576]{1,0:T(8,128)(2,1)} %bitcast.20, bf16[3,4,576]{2,1,0:T(4,128)(2,1)} %bitcast.22, bf16[576,4096]{1,0:T(8,128)(2,1)} %bitcast.18, bf16[16,512,128]{2,1,0:T(8,128)(2,1)} %w_uv_hbm.1), custom_call_target="tpu_custom_call" | custom-call | flops 1711276032 | bytes 7340032 | tf_op jit(solution)/shard_map/attend/pallas_call | solution.py:135
  7.8 9.5 %all-to-all-start = ((bf16[16,24,1024]{2,1,0:T(8,128)(2,1)}), bf16[16,24,1024]{2,1,0:T(8,128)(2,1)S(1)}, u32[]{:S(2)}, u32[]{:S(2)}) async-start(bf16[16,24,1024]{2,1,0:T(8,128)(2,1)} %attend.1.refs_3_), calls=%async_computation | async-start | bytes 1572864 | tf_op jit(solution)/shard_map/all_to_all | solution.py:466
  17.3 3.9 %regroup.3 = (bf16[144,2048]{1,0:T(8,128)(2,1)}, bf16[144,2048]{1,0:T(8,128)(2,1)}) custom-call(bf16[72,7168]{1,0:T(8,128)(2,1)} %bitcast.24, bf16[72,7168]{1,0:T(8,128)(2,1)} %bitcast.26, bf16[56,128]{1,0:T(8,128)(2,1)} %bitcast.28, bf16[16,24,1024]{2,1,0:T(8,128)(2,1)} %attend.1.refs_3_), custom_call_target="tpu_custom_call" | custom-call | flops 1056964608 | bytes 5242880 | tf_op jit(solution)/shard_map/regroup/pallas_call | solution.py:215
  21.2 3.1 %collective-permute-start.1 = (bf16[144,2048]{1,0:T(8,128)(2,1)}, bf16[144,2048]{1,0:T(8,128)(2,1)S(1)}, u32[]{:S(2)}, u32[]{:S(2)}) collective-permute-start(bf16[144,2048]{1,0:T(8,128)(2,1)} %get-tuple-element.32), channel_id=1, source_target_pairs={{0,3},{1,2},{2,1},{3,0},{4,7},{5,6},{6,5},{7,4},{8,11},{9,10},{10,... | collective-permute-start | bytes 1769480 | tf_op jit(solution)/shard_map/ppermute | solution.py:488
  24.3 0.1 collective-permute-start
  24.5 4.0 %regroup.4 = (bf16[144,2048]{1,0:T(8,128)(2,1)}, bf16[144,2048]{1,0:T(8,128)(2,1)}) custom-call(bf16[72,7168]{1,0:T(8,128)(2,1)} %bitcast.25, bf16[72,7168]{1,0:T(8,128)(2,1)} %bitcast.27, bf16[56,128]{1,0:T(8,128)(2,1)} %bitcast.29, bf16[144,2048]{1,0:T(8,128)(2,1)} %get-tuple-element.31.refs_3_), custom_call_target="tpu_custom_call" | custom-call | flops 1056964608 | bytes 5242880 | tf_op jit(solution)/shard_map/regroup/pallas_call | solution.py:215
  28.5 8.8 %collective-permute-done.1.refs_3_ = bf16[144,2048]{1,0:T(8,128)(2,1)S(1)} collective-permute-done((bf16[144,2048]{1,0:T(8,128)(2,1)}, bf16[144,2048]{1,0:T(8,128)(2,1)S(1)}, u32[]{:S(2)}, u32[]{:S(2)}) %collective-permute-start.1) | collective-permute-done | bytes 589856 | tf_op jit(solution)/shard_map/ppermute | solution.py:488
  37.3 1.5 collective-permute-done.refs_1_
  38.8 0.0 all-to-all-done
  38.8 0.0 collective-permute-start.2
  38.8 2.5 %collective-permute-start.3 = (bf16[144,2048]{1,0:T(8,128)(2,1)}, bf16[144,2048]{1,0:T(8,128)(2,1)S(1)}, u32[]{:S(2)}, u32[]{:S(2)}) collective-permute-start(bf16[144,2048]{1,0:T(8,128)(2,1)} %get-tuple-element.35), channel_id=1, source_target_pairs={{0,2},{1,3},{2,0},{3,1},{4,6},{5,7},{6,4},{7,5},{8,10},{9,11},{10,... | collective-permute-start | bytes 1769480 | tf_op jit(solution)/shard_map/ppermute | solution.py:488
  41.3 0.0 copy-done.8
  41.3 2.7 %collective-permute-start.4 = (bf16[28,384]{1,0:T(8,128)(2,1)S(1)}, bf16[28,384]{1,0:T(8,128)(2,1)S(1)}, u32[]{:S(2)}, u32[]{:S(2)}) collective-permute-start(bf16[28,384]{1,0:T(8,128)(2,1)S(1)} %bitcast.21), channel_id=1, source_target_pairs={{0,4},{4,0},{1,5},{5,1},{2,6},{6,2},{3,7},{7,3},{8,12},{12,8},{9,1... | collective-permute-start | bytes 64520 | tf_op jit(solution)/shard_map/ppermute | solution.py:474
  44.0 0.0 copy-done
  44.0 1.2 project_own.1.first_ref
  45.2 0.0 collective-permute-done.2.heads_ref
  45.2 3.4 %project_more.1.refs_2_ = bf16[8,56,384]{2,1,0:T(8,128)(2,1)} custom-call(bf16[224,192]{1,0:T(8,128)(2,1)S(1)} %project_own.1.first_ref, bf16[384,1024]{1,0:T(8,128)(2,1)} %collective-permute-done.2.heads_ref, bf16[224,2048]{1,0:T(8,128)(2,1)S(1)} %bitcast.15), custom_call_target="tpu_custom_call" | custom-call | flops 176160768 | bytes 2097152 | tf_op jit(solution)/shard_map/project_more/pallas_call | solution.py:280
  48.6 3.6 %all-to-all-start.1 = ((bf16[8,56,384]{2,1,0:T(8,128)(2,1)}), bf16[8,56,384]{2,1,0:T(8,128)(2,1)S(1)}, u32[]{:S(2)}, u32[]{:S(2)}) async-start(bf16[8,56,384]{2,1,0:T(8,128)(2,1)} %project_more.1.refs_2_), calls=%async_computation.1 | async-start | bytes 688128 | tf_op jit(solution)/shard_map/all_to_all | solution.py:466
  52.2 0.0 collective-permute-done.4
  52.3 4.8 %regroup.5 = (bf16[80,2048]{1,0:T(8,128)(2,1)}, bf16[80,2048]{1,0:T(8,128)(2,1)}, bf16[80,2048]{1,0:T(8,128)(2,1)}, bf16[80,2048]{1,0:T(8,128)(2,1)}) custom-call(bf16[72,7168]{1,0:T(8,128)(2,1)} %refs_0_.1, bf16[56,128]{1,0:T(8,128)(2,1)} %bitcast.30, bf16[8,56,384]{2,1,0:T(8,128)(2,1)} %project_more.1.refs_2_), custom_call_target="tpu_custom_call" | custom-call | flops 1174405120 | bytes 5242880 | tf_op jit(solution)/shard_map/regroup/pallas_call | solution.py:215
  57.1 0.0 collective-permute-done.3.refs_2_
  57.1 4.7 %all-to-all-done.1.parts_ref = bf16[8,56,384]{2,1,0:T(8,128)(2,1)S(1)} async-done(((bf16[8,56,384]{2,1,0:T(8,128)(2,1)}), bf16[8,56,384]{2,1,0:T(8,128)(2,1)S(1)}, u32[]{:S(2)}, u32[]{:S(2)}) %all-to-all-start.1) | async-done | bytes 344096 | tf_op jit(solution)/shard_map/all_to_all | solution.py:466
  61.8 0.2 update.1
  62.0 0.8 copy-done.7
  62.9 7.1 %all-to-all-start.2 = ((bf16[16,56,384]{2,1,0:T(8,128)(2,1)}), bf16[16,56,384]{2,1,0:T(8,128)(2,1)S(1)}, u32[]{:S(2)}, u32[]{:S(2)}) async-start(bf16[16,56,384]{2,1,0:T(8,128)(2,1)} %copy-done.7), calls=%async_computation.2 | async-start | bytes 1376256 | tf_op jit(solution)/shard_map/all_to_all | solution.py:466
  69.9 0.1 collective-permute-start.5
  70.1 2.1 %collective-permute-start.6 = (bf16[80,2048]{1,0:T(8,128)(2,1)}, bf16[80,2048]{1,0:T(8,128)(2,1)S(1)}, u32[]{:S(2)}, u32[]{:S(2)}) collective-permute-start(bf16[80,2048]{1,0:T(8,128)(2,1)} %get-tuple-element.44), channel_id=1, source_target_pairs={{0,2},{1,3},{2,0},{3,1},{4,6},{5,7},{6,4},{7,5},{8,10},{9,11},{10,... | collective-permute-start | bytes 983048 | tf_op jit(solution)/shard_map/ppermute | solution.py:488
  72.2 2.5 %collective-permute-start.7 = (bf16[80,2048]{1,0:T(8,128)(2,1)}, bf16[80,2048]{1,0:T(8,128)(2,1)S(1)}, u32[]{:S(2)}, u32[]{:S(2)}) collective-permute-start(bf16[80,2048]{1,0:T(8,128)(2,1)} %get-tuple-element.45), channel_id=1, source_target_pairs={{0,3},{1,2},{2,1},{3,0},{4,7},{5,6},{6,5},{7,4},{8,11},{9,10},{10,... | collective-permute-start | bytes 983048 | tf_op jit(solution)/shard_map/ppermute | solution.py:488
  74.6 6.2 %collective-permute-done.5.refs_1_ = bf16[80,2048]{1,0:T(8,128)(2,1)S(1)} collective-permute-done((bf16[80,2048]{1,0:T(8,128)(2,1)}, bf16[80,2048]{1,0:T(8,128)(2,1)S(1)}, u32[]{:S(2)}, u32[]{:S(2)}) %collective-permute-start.5) | collective-permute-done | bytes 327712 | tf_op jit(solution)/shard_map/ppermute | solution.py:488
  80.8 5.0 %collective-permute-done.6.refs_2_ = bf16[80,2048]{1,0:T(8,128)(2,1)S(1)} collective-permute-done((bf16[80,2048]{1,0:T(8,128)(2,1)}, bf16[80,2048]{1,0:T(8,128)(2,1)S(1)}, u32[]{:S(2)}, u32[]{:S(2)}) %collective-permute-start.6) | collective-permute-done | bytes 327712 | tf_op jit(solution)/shard_map/ppermute | solution.py:488
  85.8 0.7 copy-done.3
  86.5 1.8 %collective-permute-done.7.refs_3_ = bf16[80,2048]{1,0:T(8,128)(2,1)S(1)} collective-permute-done((bf16[80,2048]{1,0:T(8,128)(2,1)}, bf16[80,2048]{1,0:T(8,128)(2,1)S(1)}, u32[]{:S(2)}, u32[]{:S(2)}) %collective-permute-start.7) | collective-permute-done | bytes 327712 | tf_op jit(solution)/shard_map/ppermute | solution.py:488
  88.4 0.7 copy-done.5
  89.1 0.0 all-to-all-done.2.own_ref
  89.1 0.0 collective-permute-start.8
  89.1 1.6 %mix_own.1 = (f32[4,144,384]{2,1,0:T(8,128)S(1)}, f32[1,384]{1,0:T(1,128)S(1)}) custom-call(bf16[16,56,384]{2,1,0:T(8,128)(2,1)S(1)} %all-to-all-done.2.own_ref, bf16[144,2048]{1,0:T(8,128)(2,1)S(1)} %copy-done.1, bf16[144,2048]{1,0:T(8,128)(2,1)S(1)} %collective-permute-done.refs_1_, bf16[144,2048]{1,0:T(8,128)(2,1)S(1)} %collective-permute-done.3.refs_2_, ...), custom_call_target="tpu_custom_call" | custom-call | flops 452984832 | bytes 4194304 | tf_op jit(solution)/shard_map/mix_own/pallas_call | solution.py:362
  90.8 0.5 collective-permute-done.8.more_ref
  91.3 1.6 %mix_more.1 = bf16[4,160,384]{2,1,0:T(8,128)(2,1)S(1)} custom-call(f32[4,144,384]{2,1,0:T(8,128)S(1)} %get-tuple-element.51.part_ref, f32[1,384]{1,0:T(1,128)S(1)} %get-tuple-element.52.squares_ref, bf16[16,56,384]{2,1,0:T(8,128)(2,1)S(1)} %collective-permute-done.8.more_ref, bf16[144,2048]{1,0:T(8,128)(2,1)S(1)} %copy-done.1, ...), custom_call_target="tpu_custom_call" | custom-call | flops 452984832 | bytes 4194304 | tf_op jit(solution)/shard_map/mix_more/pallas_call | solution.py:375
  93.0 12.2 %all_to_all.30.parts_ref = bf16[4,160,384]{2,1,0:T(8,128)(2,1)S(1)} all-to-all(bf16[4,160,384]{2,1,0:T(8,128)(2,1)S(1)} %mix_more.1), channel_id=1, replica_groups=mesh['xl'=2,'z'=8,'c'=2,'xh'=2,'y'=4] {'y'}, dimensions={0} | all-to-all | bytes 983040 | tf_op jit(solution)/shard_map/all_to_all | solution.py:466
  105.2 0.1 gate.1
  105.3 9.0 %all_to_all.31.hidden_ref = bf16[4,80,384]{2,1,0:T(8,128)(2,1)S(1)} all-to-all(bf16[4,80,384]{2,1,0:T(8,128)(2,1)S(1)} %gate.1), channel_id=1, replica_groups=mesh['xl'=2,'z'=8,'c'=2,'xh'=2,'y'=4] {'y'}, dimensions={0} | all-to-all | bytes 491520 | tf_op jit(solution)/shard_map/all_to_all | solution.py:466
  114.3 0.9 down.3
  115.2 0.1 collective-permute-start.9
  115.3 0.9 down.2
  116.1 1.4 collective-permute-done.9
  117.5 0.2 add_convert_fusion
  117.7 33.0 %all_to_all.32.parts_ref = bf16[32,32,384]{2,1,0:T(8,128)(2,1)S(1)} all-to-all(bf16[32,32,384]{2,1,0:T(8,128)(2,1)S(1)} %bitcast.19), channel_id=1, replica_groups=mesh['xl'=2,'z'=8,'c'=2,'xh'=2,'y'=4] {'xl','z','xh'}, dimensions={0} | all-to-all | bytes 1572864 | tf_op jit(solution)/shard_map/all_to_all | solution.py:466
  150.7 0.9 finish.1
  (15 shorter events, 0.1 us)
Async XLA Ops:
  7.8 31.0 %all-to-all-start = ((bf16[16,24,1024]{2,1,0:T(8,128)(2,1)}), bf16[16,24,1024]{2,1,0:T(8,128)(2,1)S(1)}, u32[]{:S(2)}, u32[]{:S(2)}) async-start(bf16[16,24,1024]{2,1,0:T(8,128)(2,1)} %attend.1.refs_3_), calls=%async_computation | async-start | bytes 1572864 | tf_op jit(solution)/shard_map/all_to_all | solution.py:466
  21.2 16.1 %collective-permute-start.1 = (bf16[144,2048]{1,0:T(8,128)(2,1)}, bf16[144,2048]{1,0:T(8,128)(2,1)S(1)}, u32[]{:S(2)}, u32[]{:S(2)}) collective-permute-start(bf16[144,2048]{1,0:T(8,128)(2,1)} %get-tuple-element.32), channel_id=1, source_target_pairs={{0,3},{1,2},{2,1},{3,0},{4,7},{5,6},{6,5},{7,4},{8,11},{9,10},{10,... | collective-permute-start | bytes 1769480 | tf_op jit(solution)/shard_map/ppermute | solution.py:488
  24.3 17.0 %copy-start.8 = (bf16[384,28]{0,1:T(8,128)(2,1)S(1)}, bf16[384,28]{0,1:T(8,128)(2,1)}, u32[]{:S(2)}) copy-start(bf16[384,28]{0,1:T(8,128)(2,1)} %param.17) | copy-start | bytes 64516
  24.3 19.7 %copy-start = (bf16[2048,224]{0,1:T(8,128)(2,1)S(1)}, bf16[2048,224]{0,1:T(8,128)(2,1)}, u32[]{:S(2)}) copy-start(bf16[2048,224]{0,1:T(8,128)(2,1)} %param.16) | copy-start | bytes 2752516
  24.3 14.4 %collective-permute-start = (bf16[144,2048]{1,0:T(8,128)(2,1)}, bf16[144,2048]{1,0:T(8,128)(2,1)S(1)}, u32[]{:S(2)}, u32[]{:S(2)}) collective-permute-start(bf16[144,2048]{1,0:T(8,128)(2,1)} %get-tuple-element.31.refs_3_), channel_id=1, source_target_pairs={{0,1},{1,0},{2,3},{3,2},{4,5},{5,4},{6,7},{7,6},{8,9},{9,8},{10,11... | collective-permute-start | bytes 1769480 | tf_op jit(solution)/shard_map/ppermute | solution.py:488
  38.8 6.4 %collective-permute-start.2 = (bf16[384,1024]{1,0:T(8,128)(2,1)S(1)}, bf16[384,1024]{1,0:T(8,128)(2,1)}, u32[]{:S(2)}, u32[]{:S(2)}) collective-permute-start(bf16[384,1024]{1,0:T(8,128)(2,1)S(1)} %bitcast.16), channel_id=1, source_target_pairs={{0,8},{8,0},{1,9},{9,1},{2,10},{10,2},{3,11},{11,3},{4,12},{12,4},... | collective-permute-start | bytes 2359304 | tf_op jit(solution)/shard_map/ppermute | solution.py:470
  38.8 18.3 %collective-permute-start.3 = (bf16[144,2048]{1,0:T(8,128)(2,1)}, bf16[144,2048]{1,0:T(8,128)(2,1)S(1)}, u32[]{:S(2)}, u32[]{:S(2)}) collective-permute-start(bf16[144,2048]{1,0:T(8,128)(2,1)} %get-tuple-element.35), channel_id=1, source_target_pairs={{0,2},{1,3},{2,0},{3,1},{4,6},{5,7},{6,4},{7,5},{8,10},{9,11},{10,... | collective-permute-start | bytes 1769480 | tf_op jit(solution)/shard_map/ppermute | solution.py:488
  41.3 10.9 %collective-permute-start.4 = (bf16[28,384]{1,0:T(8,128)(2,1)S(1)}, bf16[28,384]{1,0:T(8,128)(2,1)S(1)}, u32[]{:S(2)}, u32[]{:S(2)}) collective-permute-start(bf16[28,384]{1,0:T(8,128)(2,1)S(1)} %bitcast.21), channel_id=1, source_target_pairs={{0,4},{4,0},{1,5},{5,1},{2,6},{6,2},{3,7},{7,3},{8,12},{12,8},{9,1... | collective-permute-start | bytes 64520 | tf_op jit(solution)/shard_map/ppermute | solution.py:474
  48.6 13.2 %all-to-all-start.1 = ((bf16[8,56,384]{2,1,0:T(8,128)(2,1)}), bf16[8,56,384]{2,1,0:T(8,128)(2,1)S(1)}, u32[]{:S(2)}, u32[]{:S(2)}) async-start(bf16[8,56,384]{2,1,0:T(8,128)(2,1)} %project_more.1.refs_2_), calls=%async_computation.1 | async-start | bytes 688128 | tf_op jit(solution)/shard_map/all_to_all | solution.py:466
  57.1 32.1 %copy-start.1 = (bf16[144,2048]{1,0:T(8,128)(2,1)S(1)}, bf16[144,2048]{1,0:T(8,128)(2,1)}, u32[]{:S(2)}) copy-start(bf16[144,2048]{1,0:T(8,128)(2,1)} %get-tuple-element.47.refs_0_) | copy-start | bytes 1769476
  62.0 0.8 copy-start.7
  62.9 26.3 %all-to-all-start.2 = ((bf16[16,56,384]{2,1,0:T(8,128)(2,1)}), bf16[16,56,384]{2,1,0:T(8,128)(2,1)S(1)}, u32[]{:S(2)}, u32[]{:S(2)}) async-start(bf16[16,56,384]{2,1,0:T(8,128)(2,1)} %copy-done.7), calls=%async_computation.2 | async-start | bytes 1376256 | tf_op jit(solution)/shard_map/all_to_all | solution.py:466
  69.9 10.9 %collective-permute-start.5 = (bf16[80,2048]{1,0:T(8,128)(2,1)}, bf16[80,2048]{1,0:T(8,128)(2,1)S(1)}, u32[]{:S(2)}, u32[]{:S(2)}) collective-permute-start(bf16[80,2048]{1,0:T(8,128)(2,1)} %get-tuple-element.43), channel_id=1, source_target_pairs={{0,1},{1,0},{2,3},{3,2},{4,5},{5,4},{6,7},{7,6},{8,9},{9,8},{10,11... | collective-permute-start | bytes 983048 | tf_op jit(solution)/shard_map/ppermute | solution.py:488
  70.1 15.8 %collective-permute-start.6 = (bf16[80,2048]{1,0:T(8,128)(2,1)}, bf16[80,2048]{1,0:T(8,128)(2,1)S(1)}, u32[]{:S(2)}, u32[]{:S(2)}) collective-permute-start(bf16[80,2048]{1,0:T(8,128)(2,1)} %get-tuple-element.44), channel_id=1, source_target_pairs={{0,2},{1,3},{2,0},{3,1},{4,6},{5,7},{6,4},{7,5},{8,10},{9,11},{10,... | collective-permute-start | bytes 983048 | tf_op jit(solution)/shard_map/ppermute | solution.py:488
  72.2 16.2 %collective-permute-start.7 = (bf16[80,2048]{1,0:T(8,128)(2,1)}, bf16[80,2048]{1,0:T(8,128)(2,1)S(1)}, u32[]{:S(2)}, u32[]{:S(2)}) collective-permute-start(bf16[80,2048]{1,0:T(8,128)(2,1)} %get-tuple-element.45), channel_id=1, source_target_pairs={{0,3},{1,2},{2,1},{3,0},{4,7},{5,6},{6,5},{7,4},{8,11},{9,10},{10,... | collective-permute-start | bytes 983048 | tf_op jit(solution)/shard_map/ppermute | solution.py:488
  85.8 0.7 copy-start.3
  88.4 0.7 copy-start.5
  89.1 2.1 %collective-permute-start.8 = (bf16[16,56,384]{2,1,0:T(8,128)(2,1)S(1)}, bf16[16,56,384]{2,1,0:T(8,128)(2,1)S(1)}, u32[]{:S(2)}, u32[]{:S(2)}) collective-permute-start(bf16[16,56,384]{2,1,0:T(8,128)(2,1)S(1)} %all-to-all-done.2.own_ref), channel_id=1, source_target_pairs={{0,8},{8,0},{1,9},{9,1},{2,10},{10,2},{3,11},{11,3},{4,12},{12,4},... | collective-permute-start | bytes 2064392 | tf_op jit(solution)/shard_map/ppermute | solution.py:470
  92.9 21.3 %copy-start.2 = (bf16[80,2048]{1,0:T(8,128)(2,1)S(1)}, bf16[80,2048]{1,0:T(8,128)(2,1)}, u32[]{:S(2)}) copy-start(bf16[80,2048]{1,0:T(8,128)(2,1)} %get-tuple-element.53.refs_0_) | copy-start | bytes 983044
  92.9 21.3 %copy-start.4 = (bf16[80,2048]{1,0:T(8,128)(2,1)S(1)}, bf16[80,2048]{1,0:T(8,128)(2,1)}, u32[]{:S(2)}) copy-start(bf16[80,2048]{1,0:T(8,128)(2,1)} %copy-done.3) | copy-start | bytes 983044
  92.9 21.3 %copy-start.6 = (bf16[80,2048]{1,0:T(8,128)(2,1)S(1)}, bf16[80,2048]{1,0:T(8,128)(2,1)}, u32[]{:S(2)}) copy-start(bf16[80,2048]{1,0:T(8,128)(2,1)} %copy-done.5) | copy-start | bytes 983044
  115.2 2.4 %collective-permute-start.9 = (bf16[1024,384]{1,0:T(8,128)(2,1)S(1)}, bf16[1024,384]{1,0:T(8,128)(2,1)S(1)}, u32[]{:S(2)}, u32[]{:S(2)}) collective-permute-start(bf16[1024,384]{1,0:T(8,128)(2,1)S(1)} %down.3), channel_id=1, source_target_pairs={{0,8},{8,0},{1,9},{9,1},{2,10},{10,2},{3,11},{11,3},{4,12},{12,4},... | collective-permute-start | bytes 2359304 | tf_op jit(solution)/shard_map/ppermute | solution.py:470

commit v6 on v5

--- a/solution.py
+++ b/solution.py
@@ -316,27 +316,14 @@
 
 
 def mix_own_kernel(own_ref, *refs):
-    blocks, (out_ref, squares_ref, held, sems) = refs[:N_Y], refs[N_Y:]
-    copies = [
-        pltpu.make_async_copy(blocks[k].at[:, pl.ds(0, OUT)], held.at[k], sems.at[k])
-        for k in range(N_Y)
-    ]
-    for copy in copies:
-        copy.start()
+    blocks, (out_ref, squares_ref) = refs[:N_Y], refs[N_Y:]
     own, squares_ref[...] = spaced(own_ref)
     for k in range(N_Y):
-        copies[k].wait()
-        out_ref[k] = dot(held[k], own)
+        out_ref[k] = dot(blocks[k][:, :OUT], own)
 
 
 def mix_more_kernel(part_ref, squares_ref, more_ref, *refs):
-    blocks, (out_ref, held, sems) = refs[:N_Y], refs[N_Y:]
-    copies = [
-        pltpu.make_async_copy(blocks[k].at[:, pl.ds(OUT, OUT)], held.at[k], sems.at[k])
-        for k in range(N_Y)
-    ]
-    for copy in copies:
-        copy.start()
+    blocks, out_ref = refs[:N_Y], refs[N_Y]
     more, squares = spaced(more_ref)
     squares = squares_ref[...] + squares
     high = squares.astype(jnp.bfloat16).astype(jnp.float32)
@@ -345,17 +332,12 @@
     tail = tail.astype(jnp.bfloat16)
     y = lax.axis_index("y")
     for k in range(N_Y):
-        copies[k].wait()
-        part = part_ref[k] + dot(held[k], more)
+        part = part_ref[k] + dot(blocks[k][:, OUT:], more)
         out_ref[y ^ k, : 2 * FF, :] = part.astype(jnp.bfloat16)
         out_ref[y ^ k, 2 * FF :, :] = tail
 
 
 def mix(own, more, blocks):
-    scratch = [
-        pltpu.VMEM((N_Y, 2 * FF, OUT), jnp.bfloat16),
-        pltpu.SemaphoreType.DMA((N_Y,)),
-    ]
     cost = pl.CostEstimate(
         flops=2 * N_Y * 2 * FF * OUT * TOKENS, bytes_accessed=4 * 2**20, transcendentals=0
     )
@@ -365,20 +347,18 @@
             shape(N_Y, 2 * FF, TOKENS, dtype=jnp.float32),
             shape(1, TOKENS, dtype=jnp.float32),
         ),
-        in_specs=[VMEM] + [ANY] * N_Y,
+        in_specs=[VMEM] * (1 + N_Y),
         out_specs=(VMEM, VMEM),
-        scratch_shapes=scratch,
-        compiler_params=params(),
+        compiler_params=params(16),
         cost_estimate=cost,
         name="mix_own",
     )(own, *blocks)
     return pl.pallas_call(
         mix_more_kernel,
         out_shape=shape(N_Y, 2 * FF + 16, TOKENS),
-        in_specs=[VMEM] * 3 + [ANY] * N_Y,
-        out_specs=VMEM,
-        scratch_shapes=scratch,
-        compiler_params=params(),
+        in_specs=[VMEM] * (3 + N_Y),
+        out_specs=VMEM,
+        compiler_params=params(16),
         cost_estimate=cost,
         name="mix_more",
     )(part, squares, more, *blocks)

time: 152 us -> 151 us (level)
  Pallas kernels: 31.3 us -> 29.6 us
where the time goes in v6:
time: 151 us
  blocking collectives  54.2 us (36%)
  starting transfers between devices  33.5 us (22%)
  waiting for transfers between devices  30.7 us (20%)
  Pallas kernels  29.6 us (20%)
  local copies, waits for them, and re-layouts  2.32 us (2%)
    all_to_all x3, blocking collectives, swap(): return lax.all_to_all(x, axes, 0, 0, tiled=True)  54.2 us
    ppermute x6, waiting for transfers between devices, exchange(): return lax.ppermute(block, 'y', [(i, i ^ k) for i in range(N_Y)])  23.3 us
    all_to_all x3, starting transfers between devices, swap(): return lax.all_to_all(x, axes, 0, 0, tiled=True)  20.2 us
    pallas_call x3, Pallas kernels, regroup(): pl.pallas_call(functools.partial(regroup_kernel, ks, count), out_shape=[s...  12.6 us
    ppermute x6, starting transfers between devices, exchange(): return lax.ppermute(block, 'y', [(i, i ^ k) for i in range(N_Y)])  10.5 us
    pallas_call x1, Pallas kernels, attend(): pl.pallas_call(attend_kernel, out_shape=shape(N_RING, 2 * NEW, HALF), in_...  7.81 us
    all_to_all x3, waiting for transfers between devices, swap(): return lax.all_to_all(x, axes, 0, 0, tiled=True)  4.68 us
    pallas_call x1, Pallas kernels, project(): pl.pallas_call(project_more_kernel, out_shape=shape(N_TP, PAIR, TOKENS),...  3.38 us
  transfers between devices with their start and end apart: 13, of which 8 were waited for; matrix products, arithmetic and copies ran while one was open for 0% of the time, Pallas kernels for 13%

profile of v6, /device:TPU:32, one launch (start us, length us, event | category | flops | bytes accessed | tf_op | source)
XLA Modules:
  0.0 150.8 jit_solution(13153545478712707813)
XLA Ops:
  0.0 7.8 %attend.1.refs_3_ = bf16[16,24,1024]{2,1,0:T(8,128)(2,1)} custom-call(s32[4,32]{1,0:T(4,128)} %bitcast.23, bf16[192,576]{1,0:T(8,128)(2,1)} %bitcast.20, bf16[3,4,576]{2,1,0:T(4,128)(2,1)} %bitcast.22, bf16[576,4096]{1,0:T(8,128)(2,1)} %bitcast.18, bf16[16,512,128]{2,1,0:T(8,128)(2,1)} %w_uv_hbm.1), custom_call_target="tpu_custom_call" | custom-call | flops 1711276032 | bytes 7340032 | tf_op jit(solution)/shard_map/attend/pallas_call | solution.py:135
  7.8 9.5 %all-to-all-start = ((bf16[16,24,1024]{2,1,0:T(8,128)(2,1)}), bf16[16,24,1024]{2,1,0:T(8,128)(2,1)S(1)}, u32[]{:S(2)}, u32[]{:S(2)}) async-start(bf16[16,24,1024]{2,1,0:T(8,128)(2,1)} %attend.1.refs_3_), calls=%async_computation | async-start | bytes 1572864 | tf_op jit(solution)/shard_map/all_to_all | solution.py:446
  17.3 3.9 %regroup.3 = (bf16[144,2048]{1,0:T(8,128)(2,1)}, bf16[144,2048]{1,0:T(8,128)(2,1)}) custom-call(bf16[72,7168]{1,0:T(8,128)(2,1)} %bitcast.24, bf16[72,7168]{1,0:T(8,128)(2,1)} %bitcast.26, bf16[56,128]{1,0:T(8,128)(2,1)} %bitcast.28, bf16[16,24,1024]{2,1,0:T(8,128)(2,1)} %attend.1.refs_3_), custom_call_target="tpu_custom_call" | custom-call | flops 1056964608 | bytes 5242880 | tf_op jit(solution)/shard_map/regroup/pallas_call | solution.py:215
  21.2 3.1 %collective-permute-start.1 = (bf16[144,2048]{1,0:T(8,128)(2,1)}, bf16[144,2048]{1,0:T(8,128)(2,1)S(1)}, u32[]{:S(2)}, u32[]{:S(2)}) collective-permute-start(bf16[144,2048]{1,0:T(8,128)(2,1)} %get-tuple-element.32), channel_id=1, source_target_pairs={{0,3},{1,2},{2,1},{3,0},{4,7},{5,6},{6,5},{7,4},{8,11},{9,10},{10,... | collective-permute-start | bytes 1769480 | tf_op jit(solution)/shard_map/ppermute | solution.py:468
  24.3 0.1 collective-permute-start
  24.5 4.0 %regroup.4 = (bf16[144,2048]{1,0:T(8,128)(2,1)}, bf16[144,2048]{1,0:T(8,128)(2,1)}) custom-call(bf16[72,7168]{1,0:T(8,128)(2,1)} %bitcast.25, bf16[72,7168]{1,0:T(8,128)(2,1)} %bitcast.27, bf16[56,128]{1,0:T(8,128)(2,1)} %bitcast.29, bf16[144,2048]{1,0:T(8,128)(2,1)} %get-tuple-element.31.refs_3_), custom_call_target="tpu_custom_call" | custom-call | flops 1056964608 | bytes 5242880 | tf_op jit(solution)/shard_map/regroup/pallas_call | solution.py:215
  28.5 8.8 %collective-permute-done.1.refs_3_ = bf16[144,2048]{1,0:T(8,128)(2,1)S(1)} collective-permute-done((bf16[144,2048]{1,0:T(8,128)(2,1)}, bf16[144,2048]{1,0:T(8,128)(2,1)S(1)}, u32[]{:S(2)}, u32[]{:S(2)}) %collective-permute-start.1) | collective-permute-done | bytes 589856 | tf_op jit(solution)/shard_map/ppermute | solution.py:468
  37.3 1.5 collective-permute-done.refs_1_
  38.8 0.0 all-to-all-done
  38.8 0.0 collective-permute-start.2
  38.8 2.5 %collective-permute-start.3 = (bf16[144,2048]{1,0:T(8,128)(2,1)}, bf16[144,2048]{1,0:T(8,128)(2,1)S(1)}, u32[]{:S(2)}, u32[]{:S(2)}) collective-permute-start(bf16[144,2048]{1,0:T(8,128)(2,1)} %get-tuple-element.35), channel_id=1, source_target_pairs={{0,2},{1,3},{2,0},{3,1},{4,6},{5,7},{6,4},{7,5},{8,10},{9,11},{10,... | collective-permute-start | bytes 1769480 | tf_op jit(solution)/shard_map/ppermute | solution.py:468
  41.3 0.0 copy-done.8
  41.3 2.7 %collective-permute-start.4 = (bf16[28,384]{1,0:T(8,128)(2,1)S(1)}, bf16[28,384]{1,0:T(8,128)(2,1)S(1)}, u32[]{:S(2)}, u32[]{:S(2)}) collective-permute-start(bf16[28,384]{1,0:T(8,128)(2,1)S(1)} %bitcast.21), channel_id=1, source_target_pairs={{0,4},{4,0},{1,5},{5,1},{2,6},{6,2},{3,7},{7,3},{8,12},{12,8},{9,1... | collective-permute-start | bytes 64520 | tf_op jit(solution)/shard_map/ppermute | solution.py:454
  44.0 0.0 copy-done
  44.0 1.2 project_own.1.first_ref
  45.2 0.0 collective-permute-done.2.heads_ref
  45.2 3.4 %project_more.1.refs_2_ = bf16[8,56,384]{2,1,0:T(8,128)(2,1)} custom-call(bf16[224,192]{1,0:T(8,128)(2,1)S(1)} %project_own.1.first_ref, bf16[384,1024]{1,0:T(8,128)(2,1)} %collective-permute-done.2.heads_ref, bf16[224,2048]{1,0:T(8,128)(2,1)S(1)} %bitcast.15), custom_call_target="tpu_custom_call" | custom-call | flops 176160768 | bytes 2097152 | tf_op jit(solution)/shard_map/project_more/pallas_call | solution.py:280
  48.6 3.6 %all-to-all-start.1 = ((bf16[8,56,384]{2,1,0:T(8,128)(2,1)}), bf16[8,56,384]{2,1,0:T(8,128)(2,1)S(1)}, u32[]{:S(2)}, u32[]{:S(2)}) async-start(bf16[8,56,384]{2,1,0:T(8,128)(2,1)} %project_more.1.refs_2_), calls=%async_computation.1 | async-start | bytes 688128 | tf_op jit(solution)/shard_map/all_to_all | solution.py:446
  52.2 0.0 collective-permute-done.4
  52.3 4.8 %regroup.5 = (bf16[80,2048]{1,0:T(8,128)(2,1)}, bf16[80,2048]{1,0:T(8,128)(2,1)}, bf16[80,2048]{1,0:T(8,128)(2,1)}, bf16[80,2048]{1,0:T(8,128)(2,1)}) custom-call(bf16[72,7168]{1,0:T(8,128)(2,1)} %refs_0_.1, bf16[56,128]{1,0:T(8,128)(2,1)} %bitcast.30, bf16[8,56,384]{2,1,0:T(8,128)(2,1)} %project_more.1.refs_2_), custom_call_target="tpu_custom_call" | custom-call | flops 1174405120 | bytes 5242880 | tf_op jit(solution)/shard_map/regroup/pallas_call | solution.py:215
  57.1 0.0 collective-permute-done.3.refs_2_
  57.1 4.7 %all-to-all-done.1.parts_ref = bf16[8,56,384]{2,1,0:T(8,128)(2,1)S(1)} async-done(((bf16[8,56,384]{2,1,0:T(8,128)(2,1)}), bf16[8,56,384]{2,1,0:T(8,128)(2,1)S(1)}, u32[]{:S(2)}, u32[]{:S(2)}) %all-to-all-start.1) | async-done | bytes 344096 | tf_op jit(solution)/shard_map/all_to_all | solution.py:446
  61.8 0.2 update.1
  62.0 0.8 copy-done.7
  62.9 7.1 %all-to-all-start.2 = ((bf16[16,56,384]{2,1,0:T(8,128)(2,1)}), bf16[16,56,384]{2,1,0:T(8,128)(2,1)S(1)}, u32[]{:S(2)}, u32[]{:S(2)}) async-start(bf16[16,56,384]{2,1,0:T(8,128)(2,1)} %copy-done.7), calls=%async_computation.2 | async-start | bytes 1376256 | tf_op jit(solution)/shard_map/all_to_all | solution.py:446
  69.9 0.1 collective-permute-start.5
  70.1 2.1 %collective-permute-start.6 = (bf16[80,2048]{1,0:T(8,128)(2,1)}, bf16[80,2048]{1,0:T(8,128)(2,1)S(1)}, u32[]{:S(2)}, u32[]{:S(2)}) collective-permute-start(bf16[80,2048]{1,0:T(8,128)(2,1)} %get-tuple-element.44), channel_id=1, source_target_pairs={{0,2},{1,3},{2,0},{3,1},{4,6},{5,7},{6,4},{7,5},{8,10},{9,11},{10,... | collective-permute-start | bytes 983048 | tf_op jit(solution)/shard_map/ppermute | solution.py:468
  72.2 2.5 %collective-permute-start.7 = (bf16[80,2048]{1,0:T(8,128)(2,1)}, bf16[80,2048]{1,0:T(8,128)(2,1)S(1)}, u32[]{:S(2)}, u32[]{:S(2)}) collective-permute-start(bf16[80,2048]{1,0:T(8,128)(2,1)} %get-tuple-element.45), channel_id=1, source_target_pairs={{0,3},{1,2},{2,1},{3,0},{4,7},{5,6},{6,5},{7,4},{8,11},{9,10},{10,... | collective-permute-start | bytes 983048 | tf_op jit(solution)/shard_map/ppermute | solution.py:468
  74.6 6.2 %collective-permute-done.5.refs_1_ = bf16[80,2048]{1,0:T(8,128)(2,1)S(1)} collective-permute-done((bf16[80,2048]{1,0:T(8,128)(2,1)}, bf16[80,2048]{1,0:T(8,128)(2,1)S(1)}, u32[]{:S(2)}, u32[]{:S(2)}) %collective-permute-start.5) | collective-permute-done | bytes 327712 | tf_op jit(solution)/shard_map/ppermute | solution.py:468
  80.8 5.0 %collective-permute-done.6.refs_2_ = bf16[80,2048]{1,0:T(8,128)(2,1)S(1)} collective-permute-done((bf16[80,2048]{1,0:T(8,128)(2,1)}, bf16[80,2048]{1,0:T(8,128)(2,1)S(1)}, u32[]{:S(2)}, u32[]{:S(2)}) %collective-permute-start.6) | collective-permute-done | bytes 327712 | tf_op jit(solution)/shard_map/ppermute | solution.py:468
  85.8 0.7 copy-done.3
  86.5 1.8 %collective-permute-done.7.refs_3_ = bf16[80,2048]{1,0:T(8,128)(2,1)S(1)} collective-permute-done((bf16[80,2048]{1,0:T(8,128)(2,1)}, bf16[80,2048]{1,0:T(8,128)(2,1)S(1)}, u32[]{:S(2)}, u32[]{:S(2)}) %collective-permute-start.7) | collective-permute-done | bytes 327712 | tf_op jit(solution)/shard_map/ppermute | solution.py:468
  88.4 0.7 copy-done.5
  89.1 0.0 all-to-all-done.2.own_ref
  89.1 0.0 collective-permute-start.8
  89.1 0.8 mix_own.1
  89.9 1.3 collective-permute-done.8.more_ref
  91.3 0.8 mix_more.1
  92.1 12.2 %all_to_all.30.parts_ref = bf16[4,160,384]{2,1,0:T(8,128)(2,1)S(1)} all-to-all(bf16[4,160,384]{2,1,0:T(8,128)(2,1)S(1)} %mix_more.1), channel_id=1, replica_groups=mesh['xl'=2,'z'=8,'c'=2,'xh'=2,'y'=4] {'y'}, dimensions={0} | all-to-all | bytes 983040 | tf_op jit(solution)/shard_map/all_to_all | solution.py:446
  104.3 0.1 gate.1
  104.4 9.0 %all_to_all.31.hidden_ref = bf16[4,80,384]{2,1,0:T(8,128)(2,1)S(1)} all-to-all(bf16[4,80,384]{2,1,0:T(8,128)(2,1)S(1)} %gate.1), channel_id=1, replica_groups=mesh['xl'=2,'z'=8,'c'=2,'xh'=2,'y'=4] {'y'}, dimensions={0} | all-to-all | bytes 491520 | tf_op jit(solution)/shard_map/all_to_all | solution.py:446
  113.4 0.9 down.3
  114.3 0.1 collective-permute-start.9
  114.4 0.9 down.2
  115.3 1.4 collective-permute-done.9
  116.7 0.2 add_convert_fusion
  116.8 33.0 %all_to_all.32.parts_ref = bf16[32,32,384]{2,1,0:T(8,128)(2,1)S(1)} all-to-all(bf16[32,32,384]{2,1,0:T(8,128)(2,1)S(1)} %bitcast.19), channel_id=1, replica_groups=mesh['xl'=2,'z'=8,'c'=2,'xh'=2,'y'=4] {'xl','z','xh'}, dimensions={0} | all-to-all | bytes 1572864 | tf_op jit(solution)/shard_map/all_to_all | solution.py:446
  149.9 0.9 finish.1
  (15 shorter events, 0.1 us)
Async XLA Ops:
  7.8 31.0 %all-to-all-start = ((bf16[16,24,1024]{2,1,0:T(8,128)(2,1)}), bf16[16,24,1024]{2,1,0:T(8,128)(2,1)S(1)}, u32[]{:S(2)}, u32[]{:S(2)}) async-start(bf16[16,24,1024]{2,1,0:T(8,128)(2,1)} %attend.1.refs_3_), calls=%async_computation | async-start | bytes 1572864 | tf_op jit(solution)/shard_map/all_to_all | solution.py:446
  21.2 16.1 %collective-permute-start.1 = (bf16[144,2048]{1,0:T(8,128)(2,1)}, bf16[144,2048]{1,0:T(8,128)(2,1)S(1)}, u32[]{:S(2)}, u32[]{:S(2)}) collective-permute-start(bf16[144,2048]{1,0:T(8,128)(2,1)} %get-tuple-element.32), channel_id=1, source_target_pairs={{0,3},{1,2},{2,1},{3,0},{4,7},{5,6},{6,5},{7,4},{8,11},{9,10},{10,... | collective-permute-start | bytes 1769480 | tf_op jit(solution)/shard_map/ppermute | solution.py:468
  24.3 17.0 %copy-start.8 = (bf16[384,28]{0,1:T(8,128)(2,1)S(1)}, bf16[384,28]{0,1:T(8,128)(2,1)}, u32[]{:S(2)}) copy-start(bf16[384,28]{0,1:T(8,128)(2,1)} %param.17) | copy-start | bytes 64516
  24.3 19.7 %copy-start = (bf16[2048,224]{0,1:T(8,128)(2,1)S(1)}, bf16[2048,224]{0,1:T(8,128)(2,1)}, u32[]{:S(2)}) copy-start(bf16[2048,224]{0,1:T(8,128)(2,1)} %param.16) | copy-start | bytes 2752516
  24.3 14.4 %collective-permute-start = (bf16[144,2048]{1,0:T(8,128)(2,1)}, bf16[144,2048]{1,0:T(8,128)(2,1)S(1)}, u32[]{:S(2)}, u32[]{:S(2)}) collective-permute-start(bf16[144,2048]{1,0:T(8,128)(2,1)} %get-tuple-element.31.refs_3_), channel_id=1, source_target_pairs={{0,1},{1,0},{2,3},{3,2},{4,5},{5,4},{6,7},{7,6},{8,9},{9,8},{10,11... | collective-permute-start | bytes 1769480 | tf_op jit(solution)/shard_map/ppermute | solution.py:468
  38.8 6.4 %collective-permute-start.2 = (bf16[384,1024]{1,0:T(8,128)(2,1)S(1)}, bf16[384,1024]{1,0:T(8,128)(2,1)}, u32[]{:S(2)}, u32[]{:S(2)}) collective-permute-start(bf16[384,1024]{1,0:T(8,128)(2,1)S(1)} %bitcast.16), channel_id=1, source_target_pairs={{0,8},{8,0},{1,9},{9,1},{2,10},{10,2},{3,11},{11,3},{4,12},{12,4},... | collective-permute-start | bytes 2359304 | tf_op jit(solution)/shard_map/ppermute | solution.py:450
  38.8 18.3 %collective-permute-start.3 = (bf16[144,2048]{1,0:T(8,128)(2,1)}, bf16[144,2048]{1,0:T(8,128)(2,1)S(1)}, u32[]{:S(2)}, u32[]{:S(2)}) collective-permute-start(bf16[144,2048]{1,0:T(8,128)(2,1)} %get-tuple-element.35), channel_id=1, source_target_pairs={{0,2},{1,3},{2,0},{3,1},{4,6},{5,7},{6,4},{7,5},{8,10},{9,11},{10,... | collective-permute-start | bytes 1769480 | tf_op jit(solution)/shard_map/ppermute | solution.py:468
  41.3 10.9 %collective-permute-start.4 = (bf16[28,384]{1,0:T(8,128)(2,1)S(1)}, bf16[28,384]{1,0:T(8,128)(2,1)S(1)}, u32[]{:S(2)}, u32[]{:S(2)}) collective-permute-start(bf16[28,384]{1,0:T(8,128)(2,1)S(1)} %bitcast.21), channel_id=1, source_target_pairs={{0,4},{4,0},{1,5},{5,1},{2,6},{6,2},{3,7},{7,3},{8,12},{12,8},{9,1... | collective-permute-start | bytes 64520 | tf_op jit(solution)/shard_map/ppermute | solution.py:454
  48.6 13.2 %all-to-all-start.1 = ((bf16[8,56,384]{2,1,0:T(8,128)(2,1)}), bf16[8,56,384]{2,1,0:T(8,128)(2,1)S(1)}, u32[]{:S(2)}, u32[]{:S(2)}) async-start(bf16[8,56,384]{2,1,0:T(8,128)(2,1)} %project_more.1.refs_2_), calls=%async_computation.1 | async-start | bytes 688128 | tf_op jit(solution)/shard_map/all_to_all | solution.py:446
  57.1 32.1 %copy-start.1 = (bf16[144,2048]{1,0:T(8,128)(2,1)S(1)}, bf16[144,2048]{1,0:T(8,128)(2,1)}, u32[]{:S(2)}) copy-start(bf16[144,2048]{1,0:T(8,128)(2,1)} %get-tuple-element.47.refs_0_) | copy-start | bytes 1769476
  62.0 0.8 copy-start.7
  62.9 26.3 %all-to-all-start.2 = ((bf16[16,56,384]{2,1,0:T(8,128)(2,1)}), bf16[16,56,384]{2,1,0:T(8,128)(2,1)S(1)}, u32[]{:S(2)}, u32[]{:S(2)}) async-start(bf16[16,56,384]{2,1,0:T(8,128)(2,1)} %copy-done.7), calls=%async_computation.2 | async-start | bytes 1376256 | tf_op jit(solution)/shard_map/all_to_all | solution.py:446
  69.9 10.9 %collective-permute-start.5 = (bf16[80,2048]{1,0:T(8,128)(2,1)}, bf16[80,2048]{1,0:T(8,128)(2,1)S(1)}, u32[]{:S(2)}, u32[]{:S(2)}) collective-permute-start(bf16[80,2048]{1,0:T(8,128)(2,1)} %get-tuple-element.43), channel_id=1, source_target_pairs={{0,1},{1,0},{2,3},{3,2},{4,5},{5,4},{6,7},{7,6},{8,9},{9,8},{10,11... | collective-permute-start | bytes 983048 | tf_op jit(solution)/shard_map/ppermute | solution.py:468
  70.1 15.8 %collective-permute-start.6 = (bf16[80,2048]{1,0:T(8,128)(2,1)}, bf16[80,2048]{1,0:T(8,128)(2,1)S(1)}, u32[]{:S(2)}, u32[]{:S(2)}) collective-permute-start(bf16[80,2048]{1,0:T(8,128)(2,1)} %get-tuple-element.44), channel_id=1, source_target_pairs={{0,2},{1,3},{2,0},{3,1},{4,6},{5,7},{6,4},{7,5},{8,10},{9,11},{10,... | collective-permute-start | bytes 983048 | tf_op jit(solution)/shard_map/ppermute | solution.py:468
  72.2 16.2 %collective-permute-start.7 = (bf16[80,2048]{1,0:T(8,128)(2,1)}, bf16[80,2048]{1,0:T(8,128)(2,1)S(1)}, u32[]{:S(2)}, u32[]{:S(2)}) collective-permute-start(bf16[80,2048]{1,0:T(8,128)(2,1)} %get-tuple-element.45), channel_id=1, source_target_pairs={{0,3},{1,2},{2,1},{3,0},{4,7},{5,6},{6,5},{7,4},{8,11},{9,10},{10,... | collective-permute-start | bytes 983048 | tf_op jit(solution)/shard_map/ppermute | solution.py:468
  85.8 0.7 copy-start.3
  88.4 0.7 copy-start.5
  89.1 2.1 %collective-permute-start.8 = (bf16[16,56,384]{2,1,0:T(8,128)(2,1)S(1)}, bf16[16,56,384]{2,1,0:T(8,128)(2,1)S(1)}, u32[]{:S(2)}, u32[]{:S(2)}) collective-permute-start(bf16[16,56,384]{2,1,0:T(8,128)(2,1)S(1)} %all-to-all-done.2.own_ref), channel_id=1, source_target_pairs={{0,8},{8,0},{1,9},{9,1},{2,10},{10,2},{3,11},{11,3},{4,12},{12,4},... | collective-permute-start | bytes 2064392 | tf_op jit(solution)/shard_map/ppermute | solution.py:450
  92.1 21.3 %copy-start.2 = (bf16[80,2048]{1,0:T(8,128)(2,1)S(1)}, bf16[80,2048]{1,0:T(8,128)(2,1)}, u32[]{:S(2)}) copy-start(bf16[80,2048]{1,0:T(8,128)(2,1)} %get-tuple-element.53.refs_0_) | copy-start | bytes 983044
  92.1 21.3 %copy-start.4 = (bf16[80,2048]{1,0:T(8,128)(2,1)S(1)}, bf16[80,2048]{1,0:T(8,128)(2,1)}, u32[]{:S(2)}) copy-start(bf16[80,2048]{1,0:T(8,128)(2,1)} %copy-done.3) | copy-start | bytes 983044
  92.1 21.3 %copy-start.6 = (bf16[80,2048]{1,0:T(8,128)(2,1)S(1)}, bf16[80,2048]{1,0:T(8,128)(2,1)}, u32[]{:S(2)}) copy-start(bf16[80,2048]{1,0:T(8,128)(2,1)} %copy-done.5) | copy-start | bytes 983044
  114.3 2.4 %collective-permute-start.9 = (bf16[1024,384]{1,0:T(8,128)(2,1)S(1)}, bf16[1024,384]{1,0:T(8,128)(2,1)S(1)}, u32[]{:S(2)}, u32[]{:S(2)}) collective-permute-start(bf16[1024,384]{1,0:T(8,128)(2,1)S(1)} %down.3), channel_id=1, source_target_pairs={{0,8},{8,0},{1,9},{9,1},{2,10},{10,2},{3,11},{11,3},{4,12},{12,4},... | collective-permute-start | bytes 2359304 | tf_op jit(solution)/shard_map/ppermute | solution.py:450
